TPU v7x, 128 devices: a whole 4x4x4 slice. The times are simulated.
128 devices in a mesh: ctx: 16 (over y, x), exp: 8 (over z, core).
Axes of the slice: x: 4, y: 4, z: 4, core: 2. Of those that a mesh axis runs over, the one named last changes fastest.
Arguments:
- tokens: bfloat16 [8, 2048, 768], P('exp', 'ctx'), may hold values from -6 to 6
- segment_ids: int32 [8, 2048], P('exp', 'ctx'), may hold values from 0 to 1, never falling along the last dimension, each value on 1 to 1792 neighbouring positions
- buckets: int32 [2048], replicated, may hold values from 0 to 31, as said below
- routes: int32 [8, 2048, 2], P('exp', 'ctx'), may hold values from 0 to 7, all different within a row; in each aligned block of 128 rows (0 to 127, 128 to 255, ..., all dimensions but the last counted through in order) at most 40 rows name the same one
- attention_gain: float32 [768], replicated, may hold values from 0.5 to 1.5
- query_weight: bfloat16 [768, 768], replicated, may hold values from -0.21875 to 0.21875
- key_weight: bfloat16 [768, 768], replicated, may hold values from -0.21875 to 0.21875
- value_weight: bfloat16 [768, 768], replicated, may hold values from -0.21875 to 0.21875
- output_weight: bfloat16 [768, 768], replicated, may hold values from -1.75 to 1.75
- bias_table: float32 [32, 12], replicated, may hold values from -4 to 4
- expert_gain: float32 [768], replicated, may hold values from 0.5 to 1.5
- router_weight: bfloat16 [768, 8], replicated, may hold values from -0.21875 to 0.21875
- expert_up: bfloat16 [768, 8, 3072], P('ctx', 'exp'), may hold values from -0.21875 to 0.21875
- expert_down: bfloat16 [768, 8, 3072], P('ctx', 'exp'), may hold values from -0.109375 to 0.109375
- out_grad: bfloat16 [8, 2048, 768], P('exp', 'ctx'), may hold values from -6 to 6
Outputs:
- layer_out: bfloat16 [8, 2048, 768], P('exp', 'ctx')
- tokens_grad: float32 [8, 2048, 768], P('exp', 'ctx')
- attention_gain_grad: float32 [768], replicated
- query_weight_grad: float32 [768, 768], replicated
- key_weight_grad: float32 [768, 768], replicated
- value_weight_grad: float32 [768, 768], replicated
- output_weight_grad: float32 [768, 768], replicated
- bias_table_grad: float32 [32, 12], replicated
- expert_gain_grad: float32 [768], replicated
- router_weight_grad: float32 [768, 8], replicated
- expert_up_grad: float32 [768, 8, 3072], P('ctx', 'exp')
- expert_down_grad: float32 [768, 8, 3072], P('ctx', 'exp')
Inputs may be any that keep to these rules, and one draw needn't show every extreme that they name: buckets[r] is the bucket of relative distance r: 0 at r = 0, never falling as r grows, 31 at r = 2047. `routes`: a token's two experts differ; among the 256 choices of the tokens of one device (aligned blocks of 128 tokens) no expert is named more than 40 times, and in some such blocks one expert is named exactly 40 times. `segment_ids`: within a sequence the numbers never fall; each of the 2 documents holds 1 to 1792 tokens.
All inputs are finite; a program needn't handle non-finite values.
Results may differ from a plain program's by a relative error of at most 0.025.
Values may be sent and summed in bfloat16 or wider, within the bound.
No kernel may reach another device: no remote copies, remote signals or barrier semaphores. Data moves between devices by JAX's collectives and lax.ppermute only.
A program may use at most 128 MiB of HBM per device.

v0:
```python
import math

import jax
import jax.numpy as jnp
from jax import lax
from jax.sharding import PartitionSpec as P

HEADS = 12
HEAD_DIM = 64
EXP_DEV = 1


EPS = 1e-06
NEG = -1e30


def in_one_piece(arrays, axis, dim, along):
    columns = [a.reshape(*a.shape[:along], -1) for a in arrays]
    both = jnp.concatenate(columns, axis=along)
    result, at, outs = (lax.all_gather(both, axis, axis=dim, tiled=True), 0, [])
    for a, column in zip(arrays, columns):
        section = result[..., at : at + column.shape[along]]
        outs.append(section.reshape(*section.shape[:along], *a.shape[along:]))
        at += column.shape[along]
    return tuple(outs)


def sent_together(arrays, axis, dim, along):
    widths = [a.shape[along] for a in arrays]
    both = jnp.concatenate(arrays, axis=along)
    result = lax.all_gather(both, axis, axis=dim, tiled=True)
    return tuple(jnp.split(result, [sum(widths[:k]) for k in range(1, len(widths))], axis=along))


def sent_together_2(arrays, axis, dim, along):
    both = jnp.concatenate(arrays, axis=along)
    result, at, outs = (lax.psum_scatter(both, axis, scatter_dimension=dim, tiled=True), 0, [])
    for a in arrays:
        outs.append(lax.slice_in_dim(result, at, at + a.shape[along], axis=along))
        at += a.shape[along]
    return tuple(outs)


def norm_rows(value):
    inverse = lax.rsqrt(jnp.mean(value * value, axis=-1, keepdims=True) + EPS)
    return (value * inverse, inverse)


def norm_back(incoming, normed, inverse, gain):
    scaled = incoming * gain
    gain_grad = jnp.sum(incoming * normed, axis=0)
    average = jnp.mean(scaled * normed, axis=-1, keepdims=True)
    return (inverse * (scaled - normed * average), gain_grad)


def bounded(folder, carry, pieces, offset):
    total = pieces[0].shape[0]
    width_step = math.gcd(total, 1024)

    def one_turn(index, state):
        inner = index * width_step
        parts = tuple((lax.dynamic_slice_in_dim(member, inner, width_step, 0) for member in pieces))
        return folder(state, parts, offset + inner)

    return lax.fori_loop(0, total // width_step, one_turn, carry)


def on_device(
    tokens,
    segment_ids,
    buckets,
    routes,
    attention_gain,
    query_weight,
    key_weight,
    value_weight,
    output_weight,
    bias_table,
    expert_gain,
    router_weight,
    expert_up,
    expert_down,
    out_grad,
):
    f32 = jnp.float32
    bf16 = jnp.bfloat16
    rows = tokens.shape[1]
    width = tokens.shape[2]
    length = buckets.shape[0]
    groups = lax.axis_size("exp")
    experts = router_weight.shape[1]
    capacity = 5 * rows // (2 * experts)
    scale = HEAD_DIM ** (-0.5)
    num_buckets = bias_table.shape[0]
    positions = lax.axis_index("ctx") * rows + jnp.arange(rows, dtype=jnp.int32)
    own_segment = segment_ids[0]
    own_label = own_segment.astype(bf16)
    edges = jnp.sum(
        (buckets[None, :] < jnp.arange(num_buckets + 1, dtype=jnp.int32)[:, None]).astype(
            jnp.int32
        ),
        axis=1,
    )
    lower_edge = edges[:-1]
    upper_edge = edges[1:]

    def pair_scores(query_heads_in, query_pos, query_label, key_heads_in, key_pos, key_label):
        distance = query_pos[:, None] - key_pos[None, :]
        allowed = (distance >= 0) & (query_label[:, None] == key_label[None, :])
        clipped = jnp.clip(distance, 0, length - 1)
        bucket_hot = (clipped[:, :, None] >= lower_edge[None, None, :]) & (
            clipped[:, :, None] < upper_edge[None, None, :]
        )
        bias = jnp.einsum(
            "bh,qkb->hqk", bias_table, bucket_hot.astype(f32), preferred_element_type=f32
        )
        scores = (
            jnp.einsum("qhd,khd->hqk", query_heads_in, key_heads_in, preferred_element_type=f32)
            * scale
            + bias
        )
        return (scores, allowed, bucket_hot)

    inputs = tokens[0].astype(f32)
    normed_one, inverse_one = norm_rows(inputs)
    hidden_one = (normed_one * attention_gain).astype(bf16)
    queries = jnp.dot(hidden_one, query_weight, preferred_element_type=f32).astype(bf16)
    keys_local = jnp.dot(hidden_one, key_weight, preferred_element_type=f32).astype(bf16)
    values_local = jnp.dot(hidden_one, value_weight, preferred_element_type=f32).astype(bf16)
    query_heads = queries.reshape(rows, HEADS, HEAD_DIM)
    own_key_heads = keys_local.reshape(rows, HEADS, HEAD_DIM)
    own_value_heads = values_local.reshape(rows, HEADS, HEAD_DIM)

    def forward_step(carry, pieces, offset):
        running_max, running_sum, accum = carry
        key_piece, value_piece, label_piece = pieces
        count = key_piece.shape[0]
        key_pos = offset + jnp.arange(count, dtype=jnp.int32)
        scores, allowed, bucket_hot = pair_scores(
            query_heads,
            positions,
            own_label,
            key_piece.reshape(count, HEADS, HEAD_DIM),
            key_pos,
            label_piece,
        )
        scores = jnp.where(allowed[None], scores, NEG)
        new_max = jnp.maximum(running_max, jnp.max(scores, axis=-1))
        weights = jnp.where(allowed[None], jnp.exp(scores - new_max[..., None]), 0.0)
        factor = jnp.exp(running_max - new_max)
        running_sum = running_sum * factor + jnp.sum(weights, axis=-1)
        added = jnp.einsum(
            "hqk,khd->qhd",
            weights.astype(bf16),
            value_piece.reshape(-1, HEADS, HEAD_DIM),
            preferred_element_type=f32,
        )
        accum = accum * factor.T[:, :, None] + added
        return (new_max, running_sum, accum)

    start_state = (
        jnp.full((HEADS, rows), NEG, f32),
        jnp.zeros((HEADS, rows), f32),
        jnp.zeros((rows, HEADS, HEAD_DIM), f32),
    )
    gathered = in_one_piece((keys_local, values_local, own_label), "ctx", 0, 1)
    final_state = bounded(forward_step, start_state, gathered, 0)
    row_max, row_sum, accum = final_state
    log_sum = row_max + jnp.log(row_sum)
    attention = accum / row_sum.T[:, :, None]
    attention_low = attention.reshape(rows, width).astype(bf16)
    residual = inputs + jnp.dot(attention_low, output_weight, preferred_element_type=f32)
    normed_two, inverse_two = norm_rows(residual)
    hidden_two = (normed_two * expert_gain).astype(bf16)
    logits = jnp.dot(hidden_two, router_weight, preferred_element_type=f32)
    routed = routes[0]
    route_hot = (routed[:, :, None] == jnp.arange(experts, dtype=jnp.int32)[None, None, :]).astype(
        f32
    )
    picked_logits = jnp.sum(route_hot * logits[:, None, :], axis=-1)
    gates = jax.nn.softmax(picked_logits, axis=-1)
    flat_routes = routed.reshape(2 * rows)
    flat_hot = (flat_routes[:, None] == jnp.arange(experts, dtype=jnp.int32)[None, :]).astype(
        jnp.int32
    )
    earlier = jnp.cumsum(flat_hot, axis=0) - flat_hot
    slots = jnp.sum(flat_hot * earlier, axis=1)
    place = (flat_routes % EXP_DEV * groups + flat_routes // EXP_DEV) * capacity + slots
    owners = jnp.arange(2 * rows, dtype=jnp.int32) // 2
    buffer_rows = EXP_DEV * groups * capacity
    send_rows = jnp.zeros((buffer_rows, width), bf16).at[place].set(hidden_two[owners])
    received = lax.all_to_all(
        send_rows.reshape(EXP_DEV, groups, capacity, width),
        "exp",
        split_axis=1,
        concat_axis=1,
        tiled=True,
    )
    expert_rows = received.reshape(EXP_DEV, groups * capacity, width)
    up_full, down_full = sent_together((expert_up, expert_down), "ctx", 0, 1)
    pre_act = jnp.einsum("erd,def->erf", expert_rows, up_full, preferred_element_type=f32)
    hidden_act = jax.nn.gelu(pre_act).astype(bf16)
    expert_result = jnp.einsum(
        "erf,def->erd", hidden_act, down_full, preferred_element_type=f32
    ).astype(bf16)
    returned = lax.all_to_all(
        expert_result.reshape(EXP_DEV, groups, capacity, width),
        "exp",
        split_axis=1,
        concat_axis=1,
        tiled=True,
    )
    pair_out = returned.reshape(buffer_rows, width)[place].astype(f32).reshape(rows, 2, width)
    mixed = jnp.sum(gates[:, :, None] * pair_out, axis=1)
    layer_out = (residual + mixed).astype(bf16)
    upstream = out_grad[0].astype(f32)
    pair_grad = (gates[:, :, None] * upstream[:, None, :]).reshape(2 * rows, width).astype(bf16)
    gate_grad = jnp.sum(pair_out * upstream[:, None, :], axis=-1)
    pick_grad = gates * (gate_grad - jnp.sum(gates * gate_grad, axis=-1, keepdims=True))
    logit_grad = jnp.sum(pick_grad[:, :, None] * route_hot, axis=1)
    grad_rows = jnp.zeros((buffer_rows, width), bf16).at[place].set(pair_grad)
    expert_grad_in = lax.all_to_all(
        grad_rows.reshape(EXP_DEV, groups, capacity, width),
        "exp",
        split_axis=1,
        concat_axis=1,
        tiled=True,
    )
    expert_grad_in = expert_grad_in.reshape(EXP_DEV, groups * capacity, width)
    act_grad = jnp.einsum("erd,def->erf", expert_grad_in, down_full, preferred_element_type=f32)
    unused, gelu_back = jax.vjp(jax.nn.gelu, pre_act)
    pre_grad = gelu_back(act_grad)[0].astype(bf16)
    down_grad = jnp.einsum("erd,erf->def", expert_grad_in, hidden_act, preferred_element_type=f32)
    up_grad = jnp.einsum("erd,erf->def", expert_rows, pre_grad, preferred_element_type=f32)
    row_grad = jnp.einsum("erf,def->erd", pre_grad, up_full, preferred_element_type=f32).astype(
        bf16
    )
    back_rows = lax.all_to_all(
        row_grad.reshape(EXP_DEV, groups, capacity, width),
        "exp",
        split_axis=1,
        concat_axis=1,
        tiled=True,
    )
    hidden_two_grad = jnp.sum(
        back_rows.reshape(buffer_rows, width)[place].astype(f32).reshape(rows, 2, width), axis=1
    )
    router_float = router_weight.astype(f32)
    hidden_two_grad = hidden_two_grad + jnp.dot(
        logit_grad, router_float.T, preferred_element_type=f32
    )
    router_grad = jnp.dot(hidden_two.astype(f32).T, logit_grad, preferred_element_type=f32)
    up_summed, down_summed = tuple(
        (
            part.astype(jnp.float32)
            for part in sent_together_2(
                (up_grad.astype(jnp.bfloat16), down_grad.astype(jnp.bfloat16)), "ctx", 0, 1
            )
        )
    )
    residual_extra, expert_gain_grad = norm_back(
        hidden_two_grad, normed_two, inverse_two, expert_gain
    )
    residual_grad = upstream + residual_extra
    branch_grad = residual_grad.astype(bf16)
    output_weight_grad = jnp.einsum(
        "rd,re->de", attention_low, branch_grad, preferred_element_type=f32
    )
    attention_grad = jnp.einsum(
        "re,de->rd", branch_grad, output_weight, preferred_element_type=f32
    ).astype(bf16)
    grad_heads = attention_grad.reshape(rows, HEADS, HEAD_DIM)
    delta = jnp.sum(grad_heads.astype(f32) * attention, axis=-1).T

    def key_side(key_piece, value_piece, label_piece, offset):
        count = key_piece.shape[0]
        key_heads = key_piece.reshape(count, HEADS, HEAD_DIM)
        value_heads = value_piece.reshape(count, HEADS, HEAD_DIM)
        key_pos = offset + jnp.arange(count, dtype=jnp.int32)
        scores, allowed, bucket_hot = pair_scores(
            query_heads, positions, own_label, key_heads, key_pos, label_piece
        )
        probs = jnp.where(allowed[None], jnp.exp(scores - log_sum[..., None]), 0.0)
        prob_grad = jnp.einsum("qhd,khd->hqk", grad_heads, value_heads, preferred_element_type=f32)
        score_grad = (probs * (prob_grad - delta[..., None])).astype(bf16)
        query_term = jnp.einsum("hqk,khd->qhd", score_grad, key_heads, preferred_element_type=f32)
        bias_term = jnp.einsum(
            "hqk,qkb->hb", score_grad, bucket_hot.astype(bf16), preferred_element_type=f32
        )
        return (count, probs, score_grad, query_term, bias_term)

    def query_only_step(carry, pieces, offset):
        query_acc, bias_acc = carry
        count, probs, score_grad, query_term, bias_term = key_side(
            pieces[0], pieces[1], pieces[2], offset
        )
        return (query_acc + query_term, bias_acc + bias_term)

    query_zero = jnp.zeros((rows, HEADS, HEAD_DIM), f32)
    bias_zero = jnp.zeros((HEADS, num_buckets), f32)
    back_start = (query_zero, bias_zero)
    back_state = bounded(query_only_step, back_start, gathered, 0)
    query_acc, bias_acc = back_state
    all_log_sum, all_delta = sent_together((log_sum.T, delta.T), "ctx", 0, 1)

    def owner_step(carry, pieces, offset):
        key_acc, value_acc = carry
        query_piece, grad_piece, label_piece = pieces
        count = query_piece.shape[0]
        piece_heads = query_piece.reshape(count, HEADS, HEAD_DIM)
        piece_grads = grad_piece.reshape(count, HEADS, HEAD_DIM)
        query_pos = offset + jnp.arange(count, dtype=jnp.int32)
        scores, allowed, bucket_hot = pair_scores(
            piece_heads, query_pos, label_piece, own_key_heads, positions, own_label
        )
        piece_log_sum = lax.dynamic_slice_in_dim(all_log_sum, offset, count, 0).T
        piece_delta = lax.dynamic_slice_in_dim(all_delta, offset, count, 0).T
        probs = jnp.where(allowed[None], jnp.exp(scores - piece_log_sum[..., None]), 0.0)
        prob_grad = jnp.einsum(
            "qhd,khd->hqk", piece_grads, own_value_heads, preferred_element_type=f32
        )
        score_grad = (probs * (prob_grad - piece_delta[..., None])).astype(bf16)
        key_acc = (
            key_acc
            + jnp.einsum("hqk,qhd->khd", score_grad, piece_heads, preferred_element_type=f32)
            * scale
        )
        value_acc = value_acc + jnp.einsum(
            "hqk,qhd->khd", probs.astype(bf16), piece_grads, preferred_element_type=f32
        )
        return (key_acc, value_acc)

    owner_state = bounded(
        owner_step,
        (query_zero, query_zero),
        in_one_piece((queries, attention_grad, own_label), "ctx", 0, 1),
        jnp.int32(0),
    )
    key_grad = owner_state[0].reshape(rows, width).astype(bf16)
    value_grad = owner_state[1].reshape(rows, width).astype(bf16)
    query_grad = (query_acc * scale).reshape(rows, width).astype(bf16)
    query_weight_grad = jnp.einsum("rd,re->de", hidden_one, query_grad, preferred_element_type=f32)
    key_weight_grad = jnp.einsum("rd,re->de", hidden_one, key_grad, preferred_element_type=f32)
    value_weight_grad = jnp.einsum("rd,re->de", hidden_one, value_grad, preferred_element_type=f32)
    hidden_one_grad = jnp.einsum("re,de->rd", query_grad, query_weight, preferred_element_type=f32)
    hidden_one_grad = hidden_one_grad + jnp.einsum(
        "re,de->rd", key_grad, key_weight, preferred_element_type=f32
    )
    hidden_one_grad = hidden_one_grad + jnp.einsum(
        "re,de->rd", value_grad, value_weight, preferred_element_type=f32
    )
    tokens_extra, attention_gain_grad = norm_back(
        hidden_one_grad, normed_one, inverse_one, attention_gain
    )
    tokens_grad = residual_grad + tokens_extra
    table_grad = bias_acc.T
    summed = lax.psum(
        (
            query_weight_grad,
            key_weight_grad,
            value_weight_grad,
            output_weight_grad,
            table_grad,
            attention_gain_grad,
            expert_gain_grad,
            router_grad,
        ),
        ("ctx", "exp"),
    )
    return (
        layer_out[None],
        tokens_grad[None],
        summed[5],
        summed[0],
        summed[1],
        summed[2],
        summed[3],
        summed[4],
        summed[6],
        summed[7],
        up_summed,
        down_summed,
    )


def solution(mesh):
    placed = (
        P("exp", "ctx", None),
        P("exp", "ctx"),
        P(),
        P("exp", "ctx", None),
        P(),
        P(),
        P(),
        P(),
        P(),
        P(),
        P(),
        P(),
        P("ctx", "exp", None),
        P("ctx", "exp", None),
        P("exp", "ctx", None),
    )
    return jax.shard_map(
        on_device,
        mesh=mesh,
        in_specs=placed,
        out_specs=(
            P("exp", "ctx", None),
            P("exp", "ctx", None),
            P(),
            P(),
            P(),
            P(),
            P(),
            P(),
            P(),
            P(),
            P("ctx", "exp", None),
            P("ctx", "exp", None),
        ),
        check_vma=False,
    )
```

profile of v0, /device:TPU:1, one launch (start us, length us, event | category | flops | bytes accessed | tf_op | source)
XLA Modules:
  0.0 648.5 jit_solution(14847083519224980038)
XLA Ops:
  24.2 56.0 %all-gather.4.cloned.1.call-done = bf16[2048,1537]{1,0:T(8,128)(2,1)} async-done(((bf16[128,1537]{1,0:T(8,128)(2,1)}), bf16[2048,1537]{1,0:T(8,128)(2,1)}) %all-gather.4.cloned.1.call-update) | async-done | bytes 6295568 | tf_op jit(solution)/shard_map/all_gather | solution.py:20
  80.2 5.9 fusion.140
  96.8 62.1 %while.50 = (s32[]{:T(128)}, f32[12,128]{1,0:T(8,128)S(1)}, f32[12,128]{1,0:T(8,128)S(1)}, f32[128,12,64]{0,2,1:T(8,128)}, bf16[128]{0:T(256)(128)(2,1)S(1)}, /*...) while((s32[]{:T(128)}, f32[12,128]{1,0:T(8,128)S(1)}, ...), condition=%wide.region_5.6_spmd.clone, body=%wide.region_2.5_spmd.clone.sunk | while | flops 532981888 | bytes 107533336 | solution.py:65
  97.3 6.7 %fusion.238 = f32[128,1024,12]{1,2,0:T(8,128)} fusion(s32[128,1024]{1,0:T(8,128)S(1)} %copy.182, s32[32]{0:T(128)} %get-tuple-element.1572, s32[32]{0:T(128)} %get-tuple-element.1571, bf16[32,12]{0,1:T(8,128)(2,1)} %get-tuple-element.1573), kind=kOutput, calls=%fused_computation.8.clone.1 | convolution fusion | flops 113246208 | bytes 6816768 | tf_op jit(solution)/shard_map/while/body/eval_jaxpr/bh,qkb->hqk/dot_general | solution.py:114
  103.9 8.3 %copy.183 = f32[128,1024,12]{0,1,2:T(8,128)} copy(f32[128,1024,12]{1,2,0:T(8,128)} %fusion.238) | data formatting | bytes 12582912 | tf_op jit(solution)/shard_map/while/body/eval_jaxpr/bh,qkb->hqk/dot_general | solution.py:114
  127.7 6.7 %fusion.238 = f32[128,1024,12]{1,2,0:T(8,128)} fusion(s32[128,1024]{1,0:T(8,128)S(1)} %copy.182, s32[32]{0:T(128)} %get-tuple-element.1572, s32[32]{0:T(128)} %get-tuple-element.1571, bf16[32,12]{0,1:T(8,128)(2,1)} %get-tuple-element.1573), kind=kOutput, calls=%fused_computation.8.clone.1 | convolution fusion | flops 113246208 | bytes 6816768 | tf_op jit(solution)/shard_map/while/body/eval_jaxpr/bh,qkb->hqk/dot_general | solution.py:114
  134.3 8.3 %copy.183 = f32[128,1024,12]{0,1,2:T(8,128)} copy(f32[128,1024,12]{1,2,0:T(8,128)} %fusion.238) | data formatting | bytes 12582912 | tf_op jit(solution)/shard_map/while/body/eval_jaxpr/bh,qkb->hqk/dot_general | solution.py:114
  184.7 6.2 fusion.84
  193.8 7.2 %fusion.93 = bf16[320,3072]{1,0:T(8,128)(2,1)S(1)} fusion(f32[320,3072]{1,0:T(8,128)} %fusion.84, bf16[320,768]{1,0:T(8,128)(2,1)S(1)} %bitcast.324, bf16[768,2,3072]{2,0,1:T(8,128)(2,1)} %all-gather.6.cloned.1.call-done), kind=kOutput, calls=%fused_computation.120 | convolution fusion | flops 1529610240 | bytes 11108352 | tf_op jit(solution)/shard_map/erd,def->erf/dot_general | solution.py:230
  208.4 6.8 %fusion.94 = bf16[320,768]{1,0:T(8,128)(2,1)} fusion(bf16[768,2,3072]{2,0,1:T(8,128)(2,1)} %all-gather.6.cloned.1.call-done, f32[320,3072]{1,0:T(8,128)} %fusion.84), kind=kOutput, calls=%fused_computation.122 | convolution fusion | flops 1519042560 | bytes 9142272 | tf_op jit(solution)/shard_map/erf,def->erd/dot_general | solution.py:203
  248.5 6.6 %fusion.81 = bf16[768,1,3072]{0,2,1:T(8,128)(2,1)} fusion(bf16[320,3072]{1,0:T(8,128)(2,1)} %copy-done.59, bf16[320,768]{1,0:T(8,128)(2,1)} %bitcast.13), kind=kOutput, calls=%fused_computation.108 | convolution fusion | flops 1512308736 | bytes 7176192 | tf_op jit(solution)/shard_map/erd,erf->def/dot_general | solution.py:234
  259.7 8.4 %pad_maximum_fusion = bf16[768,2,3072]{0,2,1:T(8,128)(2,1)} fusion(bf16[768,1,3072]{0,2,1:T(8,128)(2,1)} %fusion.82, bf16[768,1,3072]{0,2,1:T(8,128)(2,1)} %fusion.81), kind=kLoop, calls=%fused_computation.101 | loop fusion | flops 4718592 | bytes 18874368 | tf_op jit(solution)/shard_map/concatenate | solution.py:36
  268.2 24.2 %copy.162 = bf16[768,2,3072]{2,1,0:T(2,128)(2,1)} copy(bf16[768,2,3072]{0,2,1:T(8,128)(2,1)} %pad_maximum_fusion) | data formatting | bytes 18874368 | tf_op jit(solution)/shard_map/concatenate | solution.py:36
  293.5 45.5 %while.51 = (s32[]{:T(128)}, f32[128,12,64]{0,2,1:T(8,128)}, f32[12,32]{1,0:T(8,128)S(1)}, bf16[2048,768]{0,1:T(8,128)(2,1)}, bf16[128]{0:T(256)(128)(2,1)S(1)},...) while((s32[]{:T(128)}, f32[128,12,64]{0,2,1:T(8,128)}, ...), condition=%wide.region_23.24_spmd.clone, body=%wide.region_22.23_spmd.clone.sunk | while | flops 842729344 | bytes 65442124 | solution.py:65
  339.0 21.9 %all_gather.15 = f32[2048,24]{0,1:T(8,128)S(1)} all-gather(f32[128,24]{0,1:T(8,128)S(1)} %pad_maximum_fusion.4), channel_id=1, replica_groups=mesh['ctx'=16,'exp'=8] {'ctx'}, dimensions={0}, use_global_device_ids=true | all-gather | bytes 208896 | tf_op jit(solution)/shard_map/all_gather | solution.py:31
  369.5 6.4 fusion.139
  375.9 64.0 %while.52 = (s32[]{:T(128)}, f32[128,12,64]{0,2,1:T(8,128)}, f32[128,12,64]{0,2,1:T(8,128)}, bf16[2048,768]{1,0:T(8,128)(2,1)}, bf16[2048]{0:T(1024)(128)(2,1)S(...) while((s32[]{:T(128)}, f32[128,12,64]{0,2,1:T(8,128)}, ...), condition=%wide.region_25.26_spmd.clone, body=%wide.region_24.25_spmd.clone.sunk | while | flops 932676736 | bytes 55104592 | solution.py:65
  386.6 6.9 %fusion.270 = f32[12,1024,128]{2,1,0:T(8,128)} fusion(f32[1024,128,12]{1,2,0:T(8,128)S(1)} %fusion.268, f32[12,1024]{1,0:T(8,128)S(1)} %get-tuple-element.1526, pred[1024,128]{1,0:T(8,128)(4,1)S(1)} %fusion.269, bf16[1024,12,64]{0,2,1:T(8,128)(2,1)S(1)} %bitcast.296, bf16[128,12,64]{0,2,1:T(8,128)(2,1)S(1)} %get-tuple-element.1681), kind=kOutput, calls=%fused_computation.79.clone.1 | convolution fusion | flops 207618048 | bytes 14532608 | tf_op jit(solution)/shard_map/while/body/eval_jaxpr/qhd,khd->hqk/dot_general | solution.py:118
  396.0 7.2 %fusion.271 = f32[128,12,64]{0,2,1:T(8,128)} fusion(bf16[1024,12,64]{0,2,1:T(8,128)(2,1)S(1)} %bitcast.297, f32[12,1024,128]{2,1,0:T(8,128)} %fusion.270, f32[12,1024]{1,0:T(8,128)S(1)} %get-tuple-element.1527, bf16[1024,12,64]{0,2,1:T(8,128)(2,1)} %bitcast.300, bf16[128,12,64]{0,2,1:T(8,128)(2,1)S(1)} %get-tuple-element.1687, ...), kind=kOutput, calls=%fused_computation.90.clone.1 | convolution fusion | flops 407666688 | bytes 10469377 | tf_op jit(solution)/shard_map/while/body/eval_jaxpr/hqk,qhd->khd/dot_general | solution.py:325
  418.6 6.9 %fusion.270 = f32[12,1024,128]{2,1,0:T(8,128)} fusion(f32[1024,128,12]{1,2,0:T(8,128)S(1)} %fusion.268, f32[12,1024]{1,0:T(8,128)S(1)} %get-tuple-element.1526, pred[1024,128]{1,0:T(8,128)(4,1)S(1)} %fusion.269, bf16[1024,12,64]{0,2,1:T(8,128)(2,1)S(1)} %bitcast.296, bf16[128,12,64]{0,2,1:T(8,128)(2,1)S(1)} %get-tuple-element.1681), kind=kOutput, calls=%fused_computation.79.clone.1 | convolution fusion | flops 207618048 | bytes 14532608 | tf_op jit(solution)/shard_map/while/body/eval_jaxpr/qhd,khd->hqk/dot_general | solution.py:118
  428.0 7.0 %fusion.271 = f32[128,12,64]{0,2,1:T(8,128)} fusion(bf16[1024,12,64]{0,2,1:T(8,128)(2,1)S(1)} %bitcast.297, f32[12,1024,128]{2,1,0:T(8,128)} %fusion.270, f32[12,1024]{1,0:T(8,128)S(1)} %get-tuple-element.1527, bf16[1024,12,64]{0,2,1:T(8,128)(2,1)} %bitcast.300, bf16[128,12,64]{0,2,1:T(8,128)(2,1)S(1)} %get-tuple-element.1687, ...), kind=kOutput, calls=%fused_computation.90.clone.1 | convolution fusion | flops 407666688 | bytes 10469377 | tf_op jit(solution)/shard_map/while/body/eval_jaxpr/hqk,qhd->khd/dot_general | solution.py:325
  449.5 13.2 %all-reduce.6.cloned.1.call-done = bf16[768,2,3072]{2,1,0:T(2,128)(2,1)} async-done(((bf16[768,2,3072]{2,1,0:T(2,128)(2,1)}), bf16[768,2,3072]{2,1,0:T(2,128)(2,1)}) %all-reduce.6.cloned.1.call-update) | async-done | bytes 9437200
  468.5 66.2 %all-reduce.1 = (f32[768]{0:T(1024)}, f32[32,12]{0,1:T(8,128)}, f32[768]{0:T(1024)}, f32[768,8]{0,1:T(8,128)}) all-reduce(f32[768]{0:T(1024)S(1)} %get-tuple-element.1115, f32[32,12]{0,1:T(8,128)S(1)} %bitcast.332, f32[768]{0:T(1024)S(1)} %copy-done.47, f32[768,8]{0,1:T(8,128)S(1)} %fusion.147), channel_id=1, replica_groups=mesh['ctx'=16,'exp'=8] {'ctx','exp'}, use_global_device_ids=true, to_apply=%region_28.29 | all-reduce | flops 8064 | bytes 64512 | tf_op jit(solution)/shard_map/psum | solution.py:357
  535.7 98.2 %all-reduce.8.cloned.1.call-done = (f32[768,768]{1,0:T(8,128)}, f32[768,768]{1,0:T(8,128)}, f32[768,768]{1,0:T(8,128)}, f32[768,768]{1,0:T(8,128)}) async-done(((f32[768,768]{1,0:T(8,128)}, f32[768,768]{1,0:T(8,128)}, f32[768,768]{1,0:T(8,128)}, f32[768,768]{1,0:T(8,128)}), (f32[768,768]{1,0:T(8,128)}, f32[768,768]{1,0:T(8,128)}, f32[768,768]{1,0:T(8,128)}, ...) | async-done | bytes 9437200 | tf_op jit(solution)/shard_map/psum | solution.py:357
  (325 shorter events, 246.6 us)
Async XLA Ops:
  7.2 72.9 %all-gather.4.cloned.1.call-start = ((), (), s32[]{:S(2)}) async-start(), calls=%async_computation.4 | async-start | bytes 7241728 | tf_op jit(solution)/shard_map/all_gather | solution.py:20
  13.3 171.4 %all-gather.6.cloned.1.call-start = ((), (), s32[]{:S(2)}) async-start(), calls=%async_computation.5 | async-start | bytes 10027008 | tf_op jit(solution)/shard_map/all_gather | solution.py:31
  16.1 70.0 %copy-start.30 = (bf16[128,768]{1,0:T(8,128)(2,1)}, bf16[128,768]{1,0:T(8,128)(2,1)S(1)}, u32[]{:S(2)}) copy-start(bf16[128,768]{1,0:T(8,128)(2,1)S(1)} %convolution_convert_fusion.3) | copy-start | bytes 589828
  96.8 65.1 %copy-start.42 = (f32[768]{0:T(1024)S(1)}, f32[768]{0:T(1024)}, u32[]{:S(2)}) copy-start(f32[768]{0:T(1024)} %param.31) | copy-start | bytes 9220
  96.8 65.2 %copy-start.55 = (s32[256,1]{0,1:T(1,128)S(1)}, s32[256,1]{0,1:T(1,128)}, u32[]{:S(2)}) copy-start(s32[256,1]{0,1:T(1,128)} %compare_select_fusion.1) | copy-start | bytes 3076
  158.9 12.3 %copy-start.41 = (bf16[768,8]{0,1:T(8,128)(2,1)S(1)}, bf16[768,8]{0,1:T(8,128)(2,1)}, u32[]{:S(2)}) copy-start(bf16[768,8]{0,1:T(8,128)(2,1)} %param.32) | copy-start | bytes 36868
  158.9 13.8 %copy-start.16 = (f32[256,768]{1,0:T(8,128)S(1)}, f32[256,768]{1,0:T(8,128)}, u32[]{:S(2)}) copy-start(f32[256,768]{1,0:T(8,128)} %mul.380) | copy-start | bytes 2359300
  160.1 30.8 %copy-start.20 = (bf16[128,12,64]{0,2,1:T(8,128)(2,1)}, bf16[128,12,64]{0,2,1:T(8,128)(2,1)S(1)}, u32[]{:S(2)}) copy-start(bf16[128,12,64]{0,2,1:T(8,128)(2,1)S(1)} %fusion.120) | copy-start | bytes 589828
  162.0 28.9 %copy-start.24 = (bf16[128,768]{1,0:T(8,128)(2,1)}, bf16[128,768]{1,0:T(8,128)(2,1)S(1)}, u32[]{:S(2)}) copy-start(bf16[128,768]{1,0:T(8,128)(2,1)S(1)} %multiply_convert_fusion.12) | copy-start | bytes 589828
  166.1 14.4 %all-to-all-start = ((bf16[1,8,40,768]{3,2,0,1:T(8,128)(2,1)}), bf16[1,8,40,768]{3,2,0,1:T(8,128)(2,1)}, u32[]{:S(2)}, u32[]{:S(2)}) async-start(bf16[1,8,40,768]{3,2,0,1:T(8,128)(2,1)} %bitcast.312), calls=%async_computation | async-start | bytes 983040 | tf_op jit(solution)/shard_map/all_to_all | solution.py:192
  180.4 13.4 %all-to-all-start.2 = ((bf16[1,8,40,768]{3,2,0,1:T(8,128)(2,1)}), bf16[1,8,40,768]{3,2,0,1:T(8,128)(2,1)S(1)}, u32[]{:S(2)}, u32[]{:S(2)}) async-start(bf16[1,8,40,768]{3,2,0,1:T(8,128)(2,1)} %bitcast.313), calls=%async_computation.2 | async-start | bytes 983040 | tf_op jit(solution)/shard_map/all_to_all | solution.py:222
  203.6 13.9 %all-to-all-start.3 = ((bf16[1,8,40,768]{3,2,0,1:T(8,128)(2,1)}), bf16[1,8,40,768]{3,2,0,1:T(8,128)(2,1)S(1)}, u32[]{:S(2)}, u32[]{:S(2)}) async-start(bf16[1,8,40,768]{3,2,0,1:T(8,128)(2,1)} %bitcast.25), calls=%async_computation.3 | async-start | bytes 983040 | tf_op jit(solution)/shard_map/all_to_all | solution.py:238
  217.5 13.4 %all-to-all-start.1 = ((bf16[1,8,40,768]{3,2,0,1:T(8,128)(2,1)}), bf16[1,8,40,768]{3,2,0,1:T(8,128)(2,1)S(1)}, u32[]{:S(2)}, u32[]{:S(2)}) async-start(bf16[1,8,40,768]{3,2,0,1:T(8,128)(2,1)} %bitcast.326), calls=%async_computation.1 | async-start | bytes 983040 | tf_op jit(solution)/shard_map/all_to_all | solution.py:206
  221.7 146.5 %all-gather.8.cloned.1.call-start = ((), (), s32[]{:S(2)}) async-start(), calls=%async_computation.6 | async-start | bytes 7241728 | tf_op jit(solution)/shard_map/all_gather | solution.py:20
  221.7 12.5 %copy-start.15 = (f32[128,768]{1,0:T(8,128)S(1)}, f32[128,768]{1,0:T(8,128)}, u32[]{:S(2)}) copy-start(f32[128,768]{1,0:T(8,128)} %copy-done.14) | copy-start | bytes 1179652
  246.7 216.0 %all-reduce.6.cloned.1.call-start = ((), (), s32[]{:S(2)}) async-start(), calls=%async_computation.7 | async-start | bytes 18874368
  292.4 341.5 %all-reduce.8.cloned.1.call-start = ((), (), s32[]{:S(2)}) async-start(), calls=%async_computation.8 | async-start | bytes 18874368 | tf_op jit(solution)/shard_map/psum | solution.py:357
  293.5 69.1 %copy-start.5 = (bf16[1,128,768]{2,1,0:T(8,128)(2,1)S(1)}, bf16[1,128,768]{2,1,0:T(8,128)(2,1)}, u32[]{:S(2)}) copy-start(bf16[1,128,768]{2,1,0:T(8,128)(2,1)} %param.21) | copy-start | bytes 589828
  293.5 69.1 %copy-start.40 = (f32[768]{0:T(1024)S(1)}, f32[768]{0:T(1024)}, u32[]{:S(2)}) copy-start(f32[768]{0:T(1024)} %param.25) | copy-start | bytes 9220
  293.5 69.1 %copy-start.44 = (f32[128]{0:T(128)S(1)}, f32[128]{0:T(128)}, u32[]{:S(2)}) copy-start(f32[128]{0:T(128)} %copy-done.43) | copy-start | bytes 1540
  339.0 36.9 %copy-start.50 = (f32[12,32]{1,0:T(8,128)}, f32[12,32]{1,0:T(8,128)S(1)}, u32[]{:S(2)}) copy-start(f32[12,32]{1,0:T(8,128)S(1)} %get-tuple-element.724) | copy-start | bytes 4612
  448.2 20.3 %copy-start.47 = (f32[768]{0:T(1024)S(1)}, f32[768]{0:T(1024)}, u32[]{:S(2)}) copy-start(f32[768]{0:T(1024)} %get-tuple-element.1111) | copy-start | bytes 9220
  448.2 20.3 %copy-start.51 = (f32[12,32]{1,0:T(8,128)S(1)}, f32[12,32]{1,0:T(8,128)}, u32[]{:S(2)}) copy-start(f32[12,32]{1,0:T(8,128)} %copy-done.50) | copy-start | bytes 4612
  448.2 86.5 %copy-start.11 = (f32[128,768]{1,0:T(8,128)S(1)}, f32[128,768]{1,0:T(8,128)}, u32[]{:S(2)}) copy-start(f32[128,768]{1,0:T(8,128)} %copy-done.10) | copy-start | bytes 1179652
  (53 other events, 274.2 us)
Sparse Core Ops, SparseCore 0:
  13.4 66.6 all-gather.3
  82.9 75.2 all-gather.5
  246.8 61.4 all-gather.7
  311.9 150.7 all-reduce.5
  469.5 164.3 all-reduce.7
where the time goes:
time: 660 us; the launch traced here: 649 us
  waiting for transfers between devices  183 us (28%)
  matrix products  169 us (26%)
  local copies, waits for them, and re-layouts  125 us (19%)
  blocking collectives  88.1 us (13%)
  other arithmetic  48.1 us (7%)
  starting transfers between devices  18.6 us (3%)
  between operations  15.7 us (2%)
    psum x1, waiting for transfers between devices, on_device(): lax.psum((query_weight_grad, key_weight_grad, value_weight_grad, output_w...  98.2 us
    psum x1, blocking collectives, on_device(): lax.psum((query_weight_grad, key_weight_grad, value_weight_grad, output_w...  66.2 us
    all_gather x2, waiting for transfers between devices, in_one_piece(): result, at, outs = (lax.all_gather(both, axis, axis=dim, tiled=True), 0, [])  56 us
    dot_general x6, matrix products, pair_scores(): jnp.einsum('bh,qkb->hqk', bias_table, bucket_hot.astype(f32), preferred_e...  31.1 us
    dynamic_slice x16, local copies, waits for them, and re-layouts, one_turn(): lax.dynamic_slice_in_dim(member, inner, width_step, 0)  25.5 us
    dot_general x6, matrix products, pair_scores(): jnp.einsum('qhd,khd->hqk', query_heads_in, key_heads_in, preferred_elemen...  24.9 us
    concatenate x1, local copies, waits for them, and re-layouts, sent_together_2(): both = jnp.concatenate(arrays, axis=along)  24.2 us
    unnamed x112, local copies, waits for them, and re-layouts  22.5 us
  transfers between devices with their start and end apart: 9, of which 7 were waited for; matrix products, arithmetic and copies ran while one was open for 46% of the time, Pallas kernels for 0%

commit v1 on v0

v1 whole, which is shorter than its diff:
```python
import jax
import jax.numpy as jnp
from jax import lax
from jax.experimental import pallas as pl
from jax.experimental.pallas import tpu as pltpu
from jax.sharding import PartitionSpec as P

HEADS = 12
HEAD_DIM = 64
EPS = 1e-06
NEG = -1e30
BIG = 2.0**99
SCALE = HEAD_DIM ** (-0.5)
AUG = 16
ROWS = 256
f32 = jnp.float32
bf16 = jnp.bfloat16
MB = 1024 * 1024


def nn(a, b):
    return lax.dot_general(a, b, (((1,), (0,)), ((), ())), preferred_element_type=f32)


def nt(a, b):
    return lax.dot_general(a, b, (((1,), (1,)), ((), ())), preferred_element_type=f32)


def tn(a, b):
    return lax.dot_general(a, b, (((0,), (0,)), ((), ())), preferred_element_type=f32)


def call(kernel, out_shape, vmem=48, flops=0, moved=0, **kw):
    return pl.pallas_call(
        kernel,
        out_shape=out_shape,
        compiler_params=pltpu.CompilerParams(vmem_limit_bytes=vmem * MB),
        cost_estimate=pl.CostEstimate(flops=flops, bytes_accessed=moved, transcendentals=0),
        **kw,
    )


def sds(shape, dtype):
    return jax.ShapeDtypeStruct(shape, dtype)


def inv_rms(value):
    return lax.rsqrt(jnp.mean(value * value, axis=-1, keepdims=True) + EPS)


def project_kernel(tok_ref, gain_ref, seg_ref, wq_ref, wk_ref, wv_ref, out_ref, hid_ref):
    x = tok_ref[...].astype(f32)
    hidden = (x * inv_rms(x) * gain_ref[...]).astype(bf16)
    hid_ref[...] = hidden
    tokens = x.shape[0]
    heads = out_ref.shape[0]

    def put(weight_ref, at, factor):
        t = (nn(hidden, weight_ref[...]).astype(bf16).astype(f32) * factor).T.astype(bf16)
        out_ref[0:HEADS, at : at + HEAD_DIM, :] = t.reshape(HEADS, HEAD_DIM, tokens)
        out_ref[HEADS:, at : at + HEAD_DIM, :] = jnp.zeros((heads - HEADS, HEAD_DIM, tokens), bf16)

    put(wq_ref, 0, SCALE)
    put(wk_ref, HEAD_DIM + AUG, 1.0)
    put(wv_ref, 2 * (HEAD_DIM + AUG), 1.0)
    s = jnp.broadcast_to(seg_ref[...].astype(f32), (AUG, tokens))
    row = lax.broadcasted_iota(jnp.int32, (AUG, tokens), 0)
    q_rows = jnp.where(row == 0, s * BIG, jnp.where(row == 1, (1.0 - s) * BIG, 0.0)).astype(bf16)
    k_rows = jnp.where(
        row == 0, s - 1.0, jnp.where(row == 1, -s, jnp.where(row < 5, 1.0, 0.0))
    ).astype(bf16)
    full = (heads, AUG, tokens)
    out_ref[:, HEAD_DIM : HEAD_DIM + AUG, :] = jnp.broadcast_to(q_rows[None], full)
    out_ref[:, 2 * HEAD_DIM + AUG : 2 * (HEAD_DIM + AUG), :] = jnp.broadcast_to(k_rows[None], full)


QA = HEAD_DIM + AUG
TQ = 256


def bias_tiles(bucket_ref, tab_ref, tile_ref):
    length = bucket_ref.shape[1]
    buckets = bucket_ref[...]
    nb = tab_ref.shape[0]
    hot = jnp.broadcast_to(buckets, (nb, length)) == lax.broadcasted_iota(
        jnp.int32, (nb, length), 0
    )
    b = jnp.sum(jnp.where(hot, tab_ref[...], 0.0), axis=0, keepdims=True)
    w = jnp.concatenate([jnp.full((1, TQ), NEG, f32), b], axis=1)
    x = jnp.broadcast_to(w, (8, length + TQ))
    row = lax.broadcasted_iota(jnp.int32, x.shape, 0)
    for bit in (1, 2, 4):
        x = jnp.where((row & bit) > 0, pltpu.roll(x, bit, axis=1), x)
    for bit in (8, 16, 32, 64):
        x = jnp.concatenate([x, pltpu.roll(x, bit, axis=1)], axis=0)
    for d in range(length // TQ):
        at = (d + 1) * TQ
        tile_ref[d, 0:128, :] = x[:, at : at + TQ]
        tile_ref[d, 128:256, :] = x[:, at - 128 : at - 128 + TQ]


def transposed(block):
    return block.astype(f32).T.astype(bf16)


def pair(ref, index, at, size):
    return jnp.concatenate(
        [ref[2 * index, at : at + size, :], ref[2 * index + 1, at : at + size, :]], axis=1
    )


def boundary(recv_ref):
    ones = recv_ref[:, QA + HEAD_DIM : QA + HEAD_DIM + AUG, :].astype(f32)
    row = lax.broadcasted_iota(jnp.int32, ones.shape, 1)
    total = jnp.sum(jnp.where(row == 1, ones, 0.0))
    return recv_ref.shape[0] * recv_ref.shape[2] + total.astype(jnp.int32)


def first_tile(qb, edge):
    return jnp.where(qb * TQ >= edge, edge // TQ, 0)


def attend_kernel(recv_ref, bucket_ref, tab_ref, ot_ref, otf_ref, lse_ref, kn_ref, tile_ref):
    blocks = recv_ref.shape[0]
    bias_tiles(bucket_ref, tab_ref, tile_ref)
    for c in range(blocks):
        kn_ref[c // 2, (c % 2) * 128 : (c % 2) * 128 + 128, :] = transposed(
            recv_ref[c, QA : 2 * QA, :]
        )
    edge = boundary(recv_ref)

    def one_query_tile(qb, carry):
        qt = pair(recv_ref, qb, 0, QA)

        def one_key_tile(i, state):
            top, total, acc = state
            kb = qb - i
            s = nn(kn_ref[kb], qt) + tile_ref[i]
            new_top = jnp.maximum(top, jnp.max(s, axis=0, keepdims=True))
            p = jnp.exp(s - new_top)
            factor = jnp.exp(top - new_top)
            total = total * factor + jnp.sum(p, axis=0, keepdims=True)
            acc = acc * factor + nn(pair(recv_ref, kb, 2 * QA, HEAD_DIM), p.astype(bf16))
            return new_top, total, acc

        start = (jnp.full((1, TQ), NEG, f32), jnp.zeros((1, TQ), f32), jnp.zeros((HEAD_DIM, TQ), f32))
        top, total, acc = lax.fori_loop(0, qb - first_tile(qb, edge) + 1, one_key_tile, start)
        o = acc / total
        otf_ref[qb] = o
        lse_ref[qb] = top + jnp.log(total)
        low = o.astype(bf16)
        ot_ref[2 * qb] = low[:, :128]
        ot_ref[2 * qb + 1] = low[:, 128:]
        return carry

    lax.fori_loop(0, blocks // 2, one_query_tile, 0)


def attend_back_kernel(
    recv_ref, gt_ref, otf_ref, lse_ref, bucket_ref, tab_ref,
    out_ref, flat_ref, bias_ref,
    kn_ref, vn_ref, tile_ref, dtile_ref, dk_ref, dv_ref,
):
    blocks = recv_ref.shape[0]
    tiles = blocks // 2
    bias_tiles(bucket_ref, tab_ref, tile_ref)
    for c in range(blocks):
        at = (c % 2) * 128
        kn_ref[c // 2, at : at + 128, :] = transposed(recv_ref[c, QA : 2 * QA, :])
        vn_ref[c // 2, at : at + 128, :] = transposed(recv_ref[c, 2 * QA : 2 * QA + HEAD_DIM, :])
    edge = boundary(recv_ref)
    dtile_ref[...] = jnp.zeros_like(dtile_ref)
    dk_ref[...] = jnp.zeros_like(dk_ref)
    dv_ref[...] = jnp.zeros_like(dv_ref)

    def one_query_tile(qb, carry):
        qt = pair(recv_ref, qb, 0, QA)
        gt = pair(gt_ref, qb, 0, HEAD_DIM)
        lse = lse_ref[qb]
        delta = jnp.sum(gt.astype(f32) * otf_ref[qb], axis=0, keepdims=True)

        def one_key_tile(i, acc):
            kb = qb - i
            p = jnp.exp(nn(kn_ref[kb], qt) + tile_ref[i] - lse)
            dp = nn(vn_ref[kb], gt)
            ds = (p * (dp - delta)).astype(bf16)
            dtile_ref[i] += ds.astype(f32)
            dv_ref[kb] += nt(gt, p.astype(bf16))
            dk_ref[kb] += nt(qt[:HEAD_DIM], ds)
            return acc + nn(pair(recv_ref, kb, QA, HEAD_DIM), ds)

        acc = lax.fori_loop(
            0, qb - first_tile(qb, edge) + 1, one_key_tile, jnp.zeros((HEAD_DIM, TQ), f32)
        )
        low = (acc * SCALE).astype(bf16)
        out_ref[2 * qb, 0:HEAD_DIM, :] = low[:, :128]
        out_ref[2 * qb + 1, 0:HEAD_DIM, :] = low[:, 128:]
        return carry

    lax.fori_loop(0, tiles, one_query_tile, 0)
    for kb in range(tiles):
        for ref, at in ((dk_ref, HEAD_DIM), (dv_ref, 2 * HEAD_DIM)):
            low = ref[kb].astype(bf16)
            out_ref[2 * kb, at : at + HEAD_DIM, :] = low[:, :128]
            out_ref[2 * kb + 1, at : at + HEAD_DIM, :] = low[:, 128:]
    for c in range(blocks):
        flat_ref[:, c * 128 : (c + 1) * 128] = out_ref[c]
    upper = jnp.concatenate([dtile_ref[d, 0:128, :] for d in range(tiles)], axis=1)
    lower = jnp.concatenate([dtile_ref[d, 128:256, :] for d in range(tiles)], axis=1)
    pad = jnp.zeros((128, 128), f32)
    x = jnp.concatenate([pad, pad, upper], axis=1) + jnp.concatenate([pad, lower, pad], axis=1)
    wide = x.shape[1]
    for half in (64, 32, 16, 8, 4, 2, 1):
        x = x[0:half] + pltpu.roll(x[half : 2 * half], wide - half, axis=1)
    g = x[:, TQ:]
    nb, length = tab_ref.shape[0], bucket_ref.shape[1]
    hot = jnp.broadcast_to(bucket_ref[...], (nb, length)) == lax.broadcasted_iota(
        jnp.int32, (nb, length), 0
    )
    sums = jnp.sum(jnp.where(hot, jnp.broadcast_to(g, (nb, length)), 0.0), axis=1, keepdims=True)
    column = jnp.concatenate([jnp.broadcast_to(sums, (nb, 128)), jnp.zeros((128 - nb, 128), f32)], axis=0)
    bias_ref[...] = column.T[0:8, :]


def route_kernel(
    ot_ref, tok_ref, wo_ref, gain_ref, router_ref, rt_ref, rcol_ref, grad_ref,
    send_ref, res_ref, gate_ref, hid_ref,
):
    tokens, width = tok_ref.shape
    experts = router_ref.shape[1]
    slots_all = send_ref.shape[0]
    capacity = slots_all // experts
    att = ot_ref[0:HEADS].reshape(width, tokens)
    residual = tok_ref[...].astype(f32) + tn(att, wo_ref[...])
    res_ref[...] = residual
    hidden = (residual * inv_rms(residual) * gain_ref[...]).astype(bf16)
    hid_ref[...] = hidden
    logits = nn(hidden, router_ref[...])
    expert_lane = lax.broadcasted_iota(jnp.int32, (tokens, experts), 1)
    picked = [
        jnp.sum(jnp.where(expert_lane == rcol_ref[:, c : c + 1], logits, 0.0), axis=1, keepdims=True)
        for c in (0, 1)
    ]
    top = jnp.maximum(picked[0], picked[1])
    e0, e1 = jnp.exp(picked[0] - top), jnp.exp(picked[1] - top)
    gates = [e0 / (e0 + e1), e1 / (e0 + e1)]
    gate_ref[...] = jnp.concatenate(
        [jnp.broadcast_to(g, (tokens, 128)) for g in gates], axis=1
    )
    expert_row = lax.broadcasted_iota(jnp.int32, (experts, tokens), 0)
    before = (
        lax.broadcasted_iota(jnp.int32, (tokens, tokens), 0)
        < lax.broadcasted_iota(jnp.int32, (tokens, tokens), 1)
    ).astype(bf16)
    slot_row = lax.broadcasted_iota(jnp.int32, (slots_all, tokens), 0)
    hots = [(expert_row == rt_ref[c : c + 1, :]).astype(f32) for c in (0, 1)]
    counts = jnp.sum(hots[0], axis=1, keepdims=True)
    taken = [nn(hots[0].astype(bf16), before), nn(hots[1].astype(bf16), before) + counts]
    to_slot = []
    for c in (0, 1):
        slot = jnp.sum(hots[c] * taken[c], axis=0, keepdims=True).astype(jnp.int32)
        place = rt_ref[c : c + 1, :] * capacity + slot
        to_slot.append((slot_row == place).astype(bf16))
    send_ref[:, 0:width] = nn(to_slot[0] + to_slot[1], hidden).astype(bf16)
    upstream = grad_ref[...].astype(f32)
    weighted = jnp.concatenate([(g * upstream).astype(bf16) for g in gates], axis=0)
    send_ref[:, width:] = nn(jnp.concatenate(to_slot, axis=1), weighted).astype(bf16)


def combine_kernel(
    ret_ref, res_ref, grad_ref, gate_ref, hid_ref, rcol_ref, gain_ref, router_t_ref, wo_ref, ot_ref,
    layer_ref, rgrad_ref, gt_ref, wo_grad_ref, small_ref,
):
    tokens, width = res_ref.shape
    experts = router_t_ref.shape[0]
    slots_all = ret_ref.shape[0]
    capacity = slots_all // experts
    lane = lax.broadcasted_iota(jnp.int32, (tokens, 128), 1)
    earlier = (
        lax.broadcasted_iota(jnp.int32, (tokens, tokens), 1)
        < lax.broadcasted_iota(jnp.int32, (tokens, tokens), 0)
    ).astype(bf16)
    hots = [(lane == rcol_ref[:, c : c + 1]).astype(f32) for c in (0, 1)]
    counts = jnp.sum(hots[0], axis=0, keepdims=True)
    taken = [nn(earlier, hots[0].astype(bf16)), nn(earlier, hots[1].astype(bf16)) + counts]
    slot_lane = lax.broadcasted_iota(jnp.int32, (tokens, slots_all), 1)
    from_slot = []
    for c in (0, 1):
        slot = jnp.sum(hots[c] * taken[c], axis=1, keepdims=True).astype(jnp.int32)
        place = rcol_ref[:, c : c + 1] * capacity + slot
        from_slot.append((slot_lane == place).astype(bf16))
    outs = [nn(m, ret_ref[:, 0:width]) for m in from_slot]
    row_sum = nn(from_slot[0] + from_slot[1], ret_ref[:, width:])
    gates = [gate_ref[:, 0:1], gate_ref[:, 128:129]]
    residual = res_ref[...]
    layer_ref[...] = (residual + (gates[0] * outs[0] + gates[1] * outs[1])).astype(bf16)
    upstream = grad_ref[...].astype(f32)
    gate_grads = [jnp.sum(upstream * o, axis=1, keepdims=True) for o in outs]
    mixed = gates[0] * gate_grads[0] + gates[1] * gate_grads[1]
    logit_grad = (
        gates[0] * (gate_grads[0] - mixed) * hots[0] + gates[1] * (gate_grads[1] - mixed) * hots[1]
    )
    h2g = row_sum
    for e in range(experts):
        h2g = h2g + logit_grad[:, e : e + 1] * router_t_ref[e : e + 1, :]
    inverse = inv_rms(residual)
    normed = residual * inverse
    logit_t = logit_grad.T
    high = logit_t.astype(bf16)
    rest = (logit_t - high.astype(f32)).astype(bf16)
    router_grad = nn(high, hid_ref[...]) + nn(rest, hid_ref[...])
    small_ref[0:8, :] = jnp.broadcast_to(jnp.sum(h2g * normed, axis=0, keepdims=True), (8, width))
    small_ref[8:16, :] = router_grad[0:experts]
    scaled = h2g * gain_ref[...]
    average = jnp.mean(scaled * normed, axis=-1, keepdims=True)
    residual_grad = upstream + inverse * (scaled - normed * average)
    rgrad_ref[...] = residual_grad
    branch = residual_grad.astype(bf16)
    gt = nt(wo_ref[...], branch).astype(bf16)
    gt_ref[0:HEADS] = gt.reshape(HEADS, HEAD_DIM, tokens)
    gt_ref[HEADS:] = jnp.zeros((gt_ref.shape[0] - HEADS, HEAD_DIM, tokens), bf16)
    att = ot_ref[0:HEADS].reshape(width, tokens)
    wo_grad_ref[...] = nn(att, branch).astype(bf16)


def expert_kernel(rows_ref, up_ref, down_ref, ret_ref, pre_ref, act_ref, out_acc, row_acc):
    step = pl.program_id(0)
    width = up_ref.shape[0]
    rows = rows_ref[:, 0:width]
    grads = rows_ref[:, width:]
    up, down = up_ref[...], down_ref[...]
    x = nn(rows, up)
    c = 0.7978845608028654
    t = jnp.tanh(c * (x + 0.044715 * (x * x * x)))
    hidden = (0.5 * x * (1.0 + t)).astype(bf16)
    slope = 0.5 * (1.0 + t) + 0.5 * x * (1.0 - t * t) * (c * (1.0 + 3 * 0.044715 * (x * x)))
    pre = (nn(grads, down) * slope).astype(bf16)
    act_ref[...] = hidden
    pre_ref[...] = pre
    out_part, row_part = nt(hidden, down), nt(pre, up)

    @pl.when(step == 0)
    def _():
        out_acc[...] = out_part
        row_acc[...] = row_part

    @pl.when(step > 0)
    def _():
        out_acc[...] += out_part
        row_acc[...] += row_part

    @pl.when(step == pl.num_programs(0) - 1)
    def _():
        ret_ref[:, 0:width] = out_acc[...].astype(bf16)
        ret_ref[:, width:] = row_acc[...].astype(bf16)


def expert_grad_kernel(rows_ref, pre_ref, act_ref, out_ref, left_ref):
    step = pl.program_id(0)
    steps = pl.num_programs(0)
    width = out_ref.shape[0]

    @pl.when(step == 0)
    def _():
        left_ref[...] = rows_ref[:, 0:width].astype(f32).T.astype(bf16)

    @pl.when(step == steps // 2)
    def _():
        left_ref[...] = rows_ref[:, width:].astype(f32).T.astype(bf16)

    @pl.when(step < steps // 2)
    def _():
        out_ref[...] = nn(left_ref[...], pre_ref[...]).astype(bf16)

    @pl.when(step >= steps // 2)
    def _():
        out_ref[...] = nn(left_ref[...], act_ref[...]).astype(bf16)


def pack_kernel(flat_ref, hid_ref, wt_ref, gain_ref, wo_ref, small_ref, bias_ref, out_ref):
    width = hid_ref.shape[1]
    grad = nn(flat_ref[...], hid_ref[...])
    part = jnp.sum(grad * wt_ref[...].astype(f32), axis=0, keepdims=True) / gain_ref[...]
    out_ref[0:192, :] = grad.astype(bf16)
    wo = wo_ref[0].astype(f32)
    for c in range(1, wo_ref.shape[0]):
        wo = wo + wo_ref[c].astype(f32)
    out_ref[192:240, :] = wo.astype(bf16)
    bias = jnp.concatenate([bias_ref[...], jnp.zeros((8, width - 128), f32)], axis=1)
    row = lax.broadcasted_iota(jnp.int32, (8, width), 0)
    first = jnp.where(
        row == 0, jnp.broadcast_to(part, (8, width)), jnp.where(row == 1, small_ref[0:8, :], bias)
    )
    out_ref[240:256, :] = jnp.concatenate([first, small_ref[8:16, :]], axis=0).astype(bf16)


def tokens_kernel(recv_ref, tok_ref, gain_ref, rgrad_ref, wq_ref, wk_ref, wv_ref, out_ref):
    tokens, width = tok_ref.shape
    acc = None
    for weight_ref, at in ((wq_ref, 0), (wk_ref, HEAD_DIM), (wv_ref, 2 * HEAD_DIM)):
        grad = recv_ref[0:HEADS, at : at + HEAD_DIM, :].reshape(width, tokens)
        part = nn(weight_ref[...], grad)
        acc = part if acc is None else acc + part
    hidden_grad = acc.T
    x = tok_ref[...].astype(f32)
    inverse = inv_rms(x)
    normed = x * inverse
    scaled = hidden_grad * gain_ref[...]
    average = jnp.mean(scaled * normed, axis=-1, keepdims=True)
    out_ref[...] = rgrad_ref[...] + inverse * (scaled - normed * average)


def unpack_kernel(all_ref, q_ref, k_ref, v_ref):
    for ref, at in ((q_ref, 0), (k_ref, HEAD_DIM), (v_ref, 2 * HEAD_DIM)):
        both = jnp.concatenate(
            [all_ref[0, at : at + HEAD_DIM, :], all_ref[1, at : at + HEAD_DIM, :]], axis=0
        )
        ref[...] = both.astype(f32).T


def on_device(
    tokens, segment_ids, buckets, routes, attention_gain, query_weight, key_weight, value_weight,
    output_weight, bias_table, expert_gain, router_weight, expert_up, expert_down, out_grad,
):
    n_ctx, n_exp = lax.axis_size("ctx"), lax.axis_size("exp")
    rows, width = tokens.shape[1:]
    length = buckets.shape[0]
    experts = router_weight.shape[1]
    capacity = 5 * rows // (2 * experts)
    slots = experts * capacity
    hidden_units = expert_up.shape[2]
    head = lax.axis_index("ctx")
    gain_one = attention_gain.reshape(1, width)
    gain_two = expert_gain.reshape(1, width)
    bucket_row = buckets.reshape(1, length)
    table = jnp.pad(bias_table, ((0, 0), (0, n_ctx - HEADS)))
    tab = lax.dynamic_slice_in_dim(table, head, 1, axis=1)

    up_down = jnp.concatenate([expert_up[:, 0], expert_down[:, 0]], axis=1)
    weights = lax.all_gather(up_down, "ctx", axis=0, tiled=True)

    x = tokens[0]
    qkv, hidden = call(
        project_kernel,
        (sds((n_ctx, 2 * QA + HEAD_DIM, rows), bf16), sds((rows, width), bf16)),
        flops=6 * rows * width * width,
        moved=4 * MB,
    )(x, gain_one, segment_ids, query_weight, key_weight, value_weight)
    qkv = lax.all_to_all(qkv, "ctx", split_axis=0, concat_axis=0, tiled=True)
    hidden_all = lax.all_gather(hidden, "ctx", axis=0, tiled=True)

    tiles = length // TQ
    ot, otf, lse = call(
        attend_kernel,
        (
            sds((n_ctx, HEAD_DIM, rows), bf16),
            sds((tiles, HEAD_DIM, TQ), f32),
            sds((tiles, 1, TQ), f32),
        ),
        scratch_shapes=[pltpu.VMEM((tiles, TQ, QA), bf16), pltpu.VMEM((tiles, TQ, TQ), f32)],
        flops=8 * 10**9,
        moved=10 * MB,
    )(qkv, bucket_row, tab)
    ot = lax.all_to_all(ot, "ctx", split_axis=0, concat_axis=0, tiled=True)

    routed = routes[0]
    grads_in = out_grad[0]
    send, residual, gates, hidden_two = call(
        route_kernel,
        (
            sds((slots, 2 * width), bf16),
            sds((rows, width), f32),
            sds((rows, 256), f32),
            sds((rows, width), bf16),
        ),
        flops=10**9,
        moved=4 * MB,
    )(ot, x, output_weight, gain_two, router_weight, routed.T, routed, grads_in)
    received = lax.all_to_all(send, "exp", split_axis=0, concat_axis=0, tiled=True)

    chunk = 512
    steps = hidden_units // chunk
    whole = lambda shape: pl.BlockSpec(shape, lambda i: (0, 0))
    result, pre, act = call(
        expert_kernel,
        (
            sds((slots, 2 * width), bf16),
            sds((slots, hidden_units), bf16),
            sds((slots, hidden_units), bf16),
        ),
        grid=(steps,),
        in_specs=[
            whole((slots, 2 * width)),
            pl.BlockSpec((width, chunk), lambda i: (0, i)),
            pl.BlockSpec((width, chunk), lambda i: (0, steps + i)),
        ],
        out_specs=[
            whole((slots, 2 * width)),
            pl.BlockSpec((slots, chunk), lambda i: (0, i)),
            pl.BlockSpec((slots, chunk), lambda i: (0, i)),
        ],
        scratch_shapes=[pltpu.VMEM((slots, width), f32), pltpu.VMEM((slots, width), f32)],
        flops=8 * slots * width * hidden_units,
        moved=16 * MB,
    )(received, weights, weights)
    returned = lax.all_to_all(result, "exp", split_axis=0, concat_axis=0, tiled=True)
    weight_grads = call(
        expert_grad_kernel,
        sds((width, 2 * hidden_units), bf16),
        grid=(2 * steps,),
        in_specs=[
            whole((slots, 2 * width)),
            pl.BlockSpec((slots, chunk), lambda i: (0, jnp.minimum(i, steps - 1))),
            pl.BlockSpec((slots, chunk), lambda i: (0, jnp.maximum(i - steps, 0))),
        ],
        out_specs=pl.BlockSpec((width, chunk), lambda i: (0, i)),
        scratch_shapes=[pltpu.VMEM((width, slots), bf16)],
        flops=4 * slots * width * hidden_units,
        moved=16 * MB,
    )(received, pre, act)
    returned, weight_grads = lax.optimization_barrier((returned, weight_grads))
    summed = lax.psum_scatter(weight_grads, "ctx", scatter_dimension=0, tiled=True)

    layer_out, residual_grad, gt, wo_grad, small = call(
        combine_kernel,
        (
            sds((rows, width), bf16),
            sds((rows, width), f32),
            sds((n_ctx, HEAD_DIM, rows), bf16),
            sds((width, width), bf16),
            sds((16, width), f32),
        ),
        flops=10**9,
        moved=6 * MB,
    )(
        returned, residual, grads_in, gates, hidden_two, routed, gain_two,
        router_weight.astype(f32).T, output_weight, ot,
    )
    gt = lax.all_to_all(gt, "ctx", split_axis=0, concat_axis=0, tiled=True)
    wo_parts = lax.all_to_all(
        wo_grad.reshape(n_ctx, width // n_ctx, width), "ctx", split_axis=0, concat_axis=0, tiled=True
    )

    dqkv, flat, bias_grad = call(
        attend_back_kernel,
        (
            sds((n_ctx, 3 * HEAD_DIM, rows), bf16),
            sds((3 * HEAD_DIM, length), bf16),
            sds((8, 128), f32),
        ),
        scratch_shapes=[
            pltpu.VMEM((tiles, TQ, QA), bf16),
            pltpu.VMEM((tiles, TQ, HEAD_DIM), bf16),
            pltpu.VMEM((tiles, TQ, TQ), f32),
            pltpu.VMEM((tiles, TQ, TQ), f32),
            pltpu.VMEM((tiles, HEAD_DIM, TQ), f32),
            pltpu.VMEM((tiles, HEAD_DIM, TQ), f32),
        ],
        flops=20 * 10**9,
        moved=20 * MB,
    )(qkv, gt, otf, lse, bucket_row, tab)

    at = jnp.minimum(head, HEADS - 1) * HEAD_DIM
    own_weights = jnp.concatenate(
        [
            lax.dynamic_slice_in_dim(w, at, HEAD_DIM, axis=1).T
            for w in (query_weight, key_weight, value_weight)
        ],
        axis=0,
    )
    packed = call(
        pack_kernel,
        sds((ROWS, width), bf16),
        flops=6 * length * width * HEAD_DIM,
        moved=6 * MB,
    )(flat, hidden_all, own_weights, gain_one, wo_parts, small, bias_grad)
    parts = lax.all_to_all(
        packed.reshape(n_exp, ROWS // n_exp, width), "exp", split_axis=0, concat_axis=0, tiled=True
    )
    share = jnp.sum(parts.astype(f32), axis=0).astype(bf16)
    everything = lax.all_gather(share, ("ctx", "exp"), axis=0, tiled=True)
    everything = everything.reshape(n_ctx, ROWS, width)

    back = lax.all_to_all(dqkv, "ctx", split_axis=0, concat_axis=0, tiled=True)
    tokens_grad = call(
        tokens_kernel,
        sds((rows, width), f32),
        flops=6 * rows * width * width,
        moved=6 * MB,
    )(back, x, gain_one, residual_grad, query_weight, key_weight, value_weight)

    full = sds((width, width), f32)
    column = pl.BlockSpec((width, 128), lambda i: (0, i))
    query_grad, key_grad, value_grad = call(
        unpack_kernel,
        (full, full, full),
        grid=(HEADS // 2,),
        in_specs=[pl.BlockSpec((2, ROWS, width), lambda i: (i, 0, 0))],
        out_specs=[column, column, column],
        moved=16 * MB,
    )(everything)
    output_grad = everything[:, 192:240].reshape(width, width).astype(f32)
    tails = jnp.sum(everything[:, 240:256].astype(f32), axis=0)
    table_grad = everything[:HEADS, 242, : bias_table.shape[0]].astype(f32).T
    return (
        layer_out[None],
        tokens_grad[None],
        tails[0],
        query_grad,
        key_grad,
        value_grad,
        output_grad,
        table_grad,
        tails[1],
        tails[8:].T,
        summed[:, :hidden_units].astype(f32)[:, None],
        summed[:, hidden_units:].astype(f32)[:, None],
    )


def solution(mesh):
    placed = (
        P("exp", "ctx", None),
        P("exp", "ctx"),
        P(),
        P("exp", "ctx", None),
        P(),
        P(),
        P(),
        P(),
        P(),
        P(),
        P(),
        P(),
        P("ctx", "exp", None),
        P("ctx", "exp", None),
        P("exp", "ctx", None),
    )
    return jax.shard_map(
        on_device,
        mesh=mesh,
        in_specs=placed,
        out_specs=(
            P("exp", "ctx", None),
            P("exp", "ctx", None),
            P(),
            P(),
            P(),
            P(),
            P(),
            P(),
            P(),
            P(),
            P("ctx", "exp", None),
            P("ctx", "exp", None),
        ),
        check_vma=False,
    )
```

time: 660 us -> 377 us (0.57); the launches traced: 649 us -> 374 us
  matrix products: 169 us -> 0 us
  local copies, waits for them, and re-layouts: 125 us -> 44.7 us
  Pallas kernels: 0 us -> 66.5 us
  other arithmetic: 48.1 us -> 10.1 us
  blocking collectives: 88.1 us -> 55.7 us
  waiting for transfers between devices: 183 us -> 154 us
  starting transfers between devices: 18.6 us -> 28.5 us
    dot_general x45 -> x0, matrix products: 169 us -> none  [the longest x6 31.1 us: pair_scores(): jnp.einsum('bh,qkb->hqk', bias_table, bucket_hot.astype(f32), preferred_e...]
    psum x1 -> x0, waiting for transfers between devices: 98.2 us -> none  [on_device(): lax.psum((query_weight_grad, key_weight_grad, value_weight_grad, output_w...]
    reduce_scatter x0 -> x1, waiting for transfers between devices: none -> 73.9 us  [on_device(): lax.psum_scatter(weight_grads, 'ctx', scatter_dimension=0, tiled=True)]
    pallas_call x0 -> x10, Pallas kernels: none -> 66.5 us  [the longest x1 15.3 us: on_device(): call(attend_back_kernel, (sds((n_ctx, 3 * HEAD_DIM, rows), bf16), sds((3...]
    psum x1 -> x0, blocking collectives: 66.2 us -> none  [on_device(): lax.psum((query_weight_grad, key_weight_grad, value_weight_grad, output_w...]
    all_to_all x0 -> x3, blocking collectives: none -> 55.7 us  [the longest x1 23.7 us: on_device(): lax.all_to_all(send, 'exp', split_axis=0, concat_axis=0, tiled=True)]
    concatenate x1 -> x0, local copies, waits for them, and re-layouts: 24.2 us -> none  [sent_together_2(): both = jnp.concatenate(arrays, axis=along)]
    dynamic_slice x16 -> x3, local copies, waits for them, and re-layouts: 25.5 us -> 1.8 us  [the longest x2 1.73 us: on_device(): lax.dynamic_slice_in_dim(w, at, HEAD_DIM, axis=1)]
  transfers between devices with their start and end apart: 9 -> 9, of which waited for: 7 -> 6; matrix products, arithmetic and copies ran while one was open for 46% -> 4% of each run, Pallas kernels for 0% -> 17%
where the time goes in v1:
time: 377 us; the launch traced here: 374 us
  waiting for transfers between devices  154 us (41%)
  Pallas kernels  66.5 us (18%)
  blocking collectives  55.7 us (15%)
  local copies, waits for them, and re-layouts  44.7 us (12%)
  starting transfers between devices  28.5 us (8%)
  between operations  14.1 us (4%)
  other arithmetic  10.1 us (3%)
    reduce_scatter x1, waiting for transfers between devices, on_device(): lax.psum_scatter(weight_grads, 'ctx', scatter_dimension=0, tiled=True)  73.9 us
    all_gather x1, waiting for transfers between devices, on_device(): everything = lax.all_gather(share, ('ctx', 'exp'), axis=0, tiled=True)  47.3 us
    unnamed x109, local copies, waits for them, and re-layouts  40.2 us
    all_to_all x1, blocking collectives, on_device(): lax.all_to_all(send, 'exp', split_axis=0, concat_axis=0, tiled=True)  23.7 us
    all_to_all x1, blocking collectives, on_device(): back = lax.all_to_all(dqkv, 'ctx', split_axis=0, concat_axis=0, tiled=True)  20.5 us
    all_to_all x1, waiting for transfers between devices, on_device(): qkv = lax.all_to_all(qkv, 'ctx', split_axis=0, concat_axis=0, tiled=True)  18.4 us
    pallas_call x1, Pallas kernels, on_device(): call(attend_back_kernel, (sds((n_ctx, 3 * HEAD_DIM, rows), bf16), sds((3...  15.3 us
    pallas_call x1, Pallas kernels, on_device(): call(attend_kernel, (sds((n_ctx, HEAD_DIM, rows), bf16), sds((tiles, HEAD...  13.8 us
  transfers between devices with their start and end apart: 9, of which 6 were waited for; matrix products, arithmetic and copies ran while one was open for 4% of the time, Pallas kernels for 17%

profile of v1, /device:TPU:1, one launch (start us, length us, event | category | flops | bytes accessed | tf_op | source)
XLA Modules:
  0.0 374.1 jit_solution(8128080223202374228)
XLA Ops:
  7.3 2.0 pad_maximum_fusion
  13.6 7.7 %all-to-all-start = ((bf16[16,224,128]{2,1,0:T(8,128)(2,1)}), bf16[16,224,128]{2,1,0:T(8,128)(2,1)S(1)}, u32[]{:S(2)}, u32[]{:S(2)}) async-start(bf16[16,224,128]{2,1,0:T(8,128)(2,1)} %get-tuple-element.37), calls=%async_computation | async-start | bytes 1835008 | tf_op jit(solution)/shard_map/all_to_all | solution.py:449
  22.3 18.4 %all-to-all-done.recv_ref = bf16[16,224,128]{2,1,0:T(8,128)(2,1)S(1)} async-done(((bf16[16,224,128]{2,1,0:T(8,128)(2,1)}), bf16[16,224,128]{2,1,0:T(8,128)(2,1)S(1)}, u32[]{:S(2)}, u32[]{:S(2)}) %all-to-all-start) | async-done | bytes 917536 | tf_op jit(solution)/shard_map/all_to_all | solution.py:449
  40.7 13.8 %shard_map.239 = (bf16[16,64,128]{2,1,0:T(8,128)(2,1)}, f32[8,64,256]{2,1,0:T(8,128)S(1)}, f32[8,1,256]{2,1,0:T(1,128)S(1)}) custom-call(bf16[16,224,128]{2,1,0:T(8,128)(2,1)S(1)} %all-to-all-done.recv_ref, s32[1,2048]{1,0:T(1,128)S(1)} %bitcast.57, f32[32,1]{1,0:T(8,128)S(1)} %pad_dynamic-slice_fusion.tab_ref), custom_call_target="tpu_custom_call" | custom-call | flops 8000000000 | bytes 10485760 | tf_op jit(solution)/shard_map/pallas_call | solution.py:453
  55.3 3.5 all-to-all-start.1
  59.2 10.3 %all-to-all-done.1.ot_ref = bf16[16,64,128]{2,1,0:T(8,128)(2,1)S(1)} async-done(((bf16[16,64,128]{2,1,0:T(8,128)(2,1)}), bf16[16,64,128]{2,1,0:T(8,128)(2,1)S(1)}, u32[]{:S(2)}, u32[]{:S(2)}) %all-to-all-start.1) | async-done | bytes 262176 | tf_op jit(solution)/shard_map/all_to_all | solution.py:464
  72.8 23.7 %all_to_all.53 = bf16[8,40,1536]{2,1,0:T(8,128)(2,1)S(1)} all-to-all(bf16[8,40,1536]{2,1,0:T(8,128)(2,1)S(1)} %bitcast.48), channel_id=1, replica_groups=mesh['ctx'=16,'exp'=8] {'exp'}, dimensions={0} | all-to-all | bytes 1966080 | tf_op jit(solution)/shard_map/all_to_all | solution.py:479
  96.5 2.4 all-gather.4.cloned.1.call-done.up_ref.down_ref
  98.9 11.0 %shard_map.241 = (bf16[320,1536]{1,0:T(8,128)(2,1)S(1)}, bf16[320,3072]{1,0:T(8,128)(2,1)S(1)}, bf16[320,3072]{1,0:T(8,128)(2,1)S(1)}) custom-call(bf16[320,1536]{1,0:T(8,128)(2,1)S(1)} %bitcast.42, bf16[768,6144]{1,0:T(8,128)(2,1)} %all-gather.4.cloned.1.call-done.up_ref.down_ref, bf16[768,6144]{1,0:T(8,128)(2,1)} %all-gather.4.cloned.1.call-done.up_ref.down_ref), custom_call_target="tpu_custom_call" | custom-call | flops 6039797760 | bytes 16777216 | tf_op jit(solution)/shard_map/pallas_call | solution.py:484
  113.4 5.1 %all-to-all-start.3 = ((bf16[8,40,1536]{2,1,0:T(8,128)(2,1)}), bf16[8,40,1536]{2,1,0:T(8,128)(2,1)S(1)}, u32[]{:S(2)}, u32[]{:S(2)}) async-start(bf16[8,40,1536]{2,1,0:T(8,128)(2,1)} %bitcast.47), calls=%async_computation.3 | async-start | bytes 1966080 | tf_op jit(solution)/shard_map/all_to_all | solution.py:506
  121.7 10.5 %shard_map.242 = bf16[768,6144]{1,0:T(8,128)(2,1)} custom-call(bf16[320,1536]{1,0:T(8,128)(2,1)S(1)} %bitcast.43, bf16[320,3072]{1,0:T(8,128)(2,1)S(1)} %copy-done.7, bf16[320,3072]{1,0:T(8,128)(2,1)S(1)} %copy-done.9), custom_call_target="tpu_custom_call" | custom-call | flops 3019898880 | bytes 16777216 | tf_op jit(solution)/shard_map/pallas_call | solution.py:507
  139.0 2.2 shard_map.243
  144.2 5.2 %all-to-all-start.4 = ((bf16[16,64,128]{2,1,0:T(8,128)(2,1)}), bf16[16,64,128]{2,1,0:T(8,128)(2,1)}, u32[]{:S(2)}, u32[]{:S(2)}) async-start(bf16[16,64,128]{2,1,0:T(8,128)(2,1)} %copy-done.24), calls=%async_computation.4 | async-start | bytes 524288 | tf_op jit(solution)/shard_map/all_to_all | solution.py:539
  156.2 1.7 pad_maximum_fusion.1.wt_ref
  157.9 6.6 %all-to-all-start.6 = ((bf16[16,48,768]{2,1,0:T(8,128)(2,1)}), bf16[16,48,768]{2,1,0:T(8,128)(2,1)}, u32[]{:S(2)}, u32[]{:S(2)}) async-start(bf16[16,48,768]{2,1,0:T(8,128)(2,1)} %bitcast.45), calls=%async_computation.6 | async-start | bytes 2359296 | tf_op jit(solution)/shard_map/all_to_all | solution.py:540
  168.4 15.3 %shard_map.244 = (bf16[16,192,128]{2,1,0:T(8,128)(2,1)S(1)}, bf16[192,2048]{1,0:T(8,128)(2,1)S(1)}, f32[8,128]{1,0:T(8,128)S(1)}) custom-call(bf16[16,224,128]{2,1,0:T(8,128)(2,1)S(1)} %copy-done.14, bf16[16,64,128]{2,1,0:T(8,128)(2,1)} %all-to-all-done.4.gt_ref, f32[8,64,256]{2,1,0:T(8,128)S(1)} %copy-done.42, f32[8,1,256]{2,1,0:T(1,128)S(1)} %copy-done.44, ...), custom_call_target="tpu_custom_call" | custom-call | flops 20000000000 | bytes 20971520 | tf_op jit(solution)/shard_map/pallas_call | solution.py:544
  185.5 1.9 copy-done.5
  190.3 2.2 shard_map.246
  192.5 11.5 %all_to_all.54 = bf16[8,32,768]{2,1,0:T(8,128)(2,1)} all-to-all(bf16[8,32,768]{2,1,0:T(8,128)(2,1)S(1)} %bitcast.44), channel_id=1, replica_groups=mesh['ctx'=16,'exp'=8] {'exp'}, dimensions={0} | all-to-all | bytes 786432 | tf_op jit(solution)/shard_map/all_to_all | solution.py:577
  206.3 20.5 %all_to_all.55.recv_ref = bf16[16,192,128]{2,1,0:T(8,128)(2,1)S(1)} all-to-all(bf16[16,192,128]{2,1,0:T(8,128)(2,1)} %copy-done.19), channel_id=1, replica_groups=mesh['ctx'=16,'exp'=8] {'ctx'}, dimensions={0} | all-to-all | bytes 1572864 | tf_op jit(solution)/shard_map/all_to_all | solution.py:584
  226.9 2.0 shard_map.245
  228.9 47.3 %all-gather.8.cloned.1.call-done = bf16[4096,768]{1,0:T(8,128)(2,1)} async-done(((bf16[32,768]{1,0:T(8,128)(2,1)}), bf16[4096,768]{1,0:T(8,128)(2,1)}) %all-gather.8.cloned.1.call-update) | async-done | bytes 6291472 | tf_op jit(solution)/shard_map/all_gather | solution.py:581
  277.6 6.7 %shard_map.247 = (f32[768,768]{1,0:T(8,128)}, f32[768,768]{1,0:T(8,128)}, f32[768,768]{1,0:T(8,128)}) custom-call(bf16[16,256,768]{2,1,0:T(8,128)(2,1)} %bitcast.60), custom_call_target="tpu_custom_call" | custom-call | bytes 16777216 | tf_op jit(solution)/shard_map/pallas_call | solution.py:594
  289.6 73.9 %reduce-scatter.2.cloned.1.call-done = bf16[48,6144]{1,0:T(8,128)(2,1)} async-done(((bf16[768,6144]{1,0:T(8,128)(2,1)}), bf16[48,6144]{1,0:T(8,128)(2,1)}) %reduce-scatter.2.cloned.1.call-update) | async-done | bytes 589840 | tf_op jit(solution)/shard_map/reduce_scatter | solution.py:522
  (137 shorter events, 54.4 us)
Async XLA Ops:
  7.2 91.7 %all-gather.4.cloned.1.call-start = ((), (), s32[]{:S(2)}) async-start(), calls=%async_computation.9 | async-start | bytes 10027008 | tf_op jit(solution)/shard_map/all_gather | solution.py:440
  13.6 8.5 %copy-start.46 = (f32[32,12]{0,1:T(8,128)S(1)}, f32[32,12]{0,1:T(8,128)}, u32[]{:S(2)}) copy-start(f32[32,12]{0,1:T(8,128)} %param.24) | copy-start | bytes 4612
  13.6 27.1 %copy-start.34 = (s32[2048]{0:T(1024)S(1)}, s32[2048]{0:T(1024)}, u32[]{:S(2)}) copy-start(s32[2048]{0:T(1024)} %param.17) | copy-start | bytes 24580
  13.6 27.1 %all-to-all-start = ((bf16[16,224,128]{2,1,0:T(8,128)(2,1)}), bf16[16,224,128]{2,1,0:T(8,128)(2,1)S(1)}, u32[]{:S(2)}, u32[]{:S(2)}) async-start(bf16[16,224,128]{2,1,0:T(8,128)(2,1)} %get-tuple-element.37), calls=%async_computation | async-start | bytes 1835008 | tf_op jit(solution)/shard_map/all_to_all | solution.py:449
  21.3 164.2 %all-gather.6.cloned.1.call-start = ((), (), s32[]{:S(2)}) async-start(), calls=%async_computation.10 | async-start | bytes 3342336 | tf_op jit(solution)/shard_map/all_gather | solution.py:450
  22.3 32.2 %copy-start.27 = (f32[32,1]{1,0:T(8,128)}, f32[32,1]{1,0:T(8,128)S(1)}, u32[]{:S(2)}) copy-start(f32[32,1]{1,0:T(8,128)S(1)} %pad_dynamic-slice_fusion.tab_ref) | copy-start | bytes 388
  40.7 13.8 %copy-start.13 = (bf16[16,224,128]{2,1,0:T(8,128)(2,1)}, bf16[16,224,128]{2,1,0:T(8,128)(2,1)S(1)}, u32[]{:S(2)}) copy-start(bf16[16,224,128]{2,1,0:T(8,128)(2,1)S(1)} %all-to-all-done.recv_ref) | copy-start | bytes 2752516
  40.7 18.2 %copy-start.48 = (f32[768]{0:T(1024)S(1)}, f32[768]{0:T(1024)}, u32[]{:S(2)}) copy-start(f32[768]{0:T(1024)} %param.25) | copy-start | bytes 9220
  40.7 18.2 %copy-start.49 = (s32[1,128,2]{1,2,0:T(2,128)S(1)}, s32[1,128,2]{1,2,0:T(2,128)}, u32[]{:S(2)}) copy-start(s32[1,128,2]{1,2,0:T(2,128)} %param.18) | copy-start | bytes 3076
  40.7 18.4 %copy-start.45 = (bf16[768,8]{0,1:T(8,128)(2,1)S(1)}, bf16[768,8]{0,1:T(8,128)(2,1)}, u32[]{:S(2)}) copy-start(bf16[768,8]{0,1:T(8,128)(2,1)} %param.26) | copy-start | bytes 36868
  40.7 28.9 %copy-start.32 = (bf16[1,128,768]{2,1,0:T(8,128)(2,1)S(1)}, bf16[1,128,768]{2,1,0:T(8,128)(2,1)}, u32[]{:S(2)}) copy-start(bf16[1,128,768]{2,1,0:T(8,128)(2,1)} %param.29) | copy-start | bytes 589828
  55.3 14.3 %copy-start.43 = (f32[8,1,256]{2,1,0:T(1,128)}, f32[8,1,256]{2,1,0:T(1,128)S(1)}, u32[]{:S(2)}) copy-start(f32[8,1,256]{2,1,0:T(1,128)S(1)} %get-tuple-element.50.lse_ref) | copy-start | bytes 24580
  55.3 14.3 %all-to-all-start.1 = ((bf16[16,64,128]{2,1,0:T(8,128)(2,1)}), bf16[16,64,128]{2,1,0:T(8,128)(2,1)S(1)}, u32[]{:S(2)}, u32[]{:S(2)}) async-start(bf16[16,64,128]{2,1,0:T(8,128)(2,1)} %get-tuple-element.38), calls=%async_computation.1 | async-start | bytes 524288 | tf_op jit(solution)/shard_map/all_to_all | solution.py:464
  72.8 37.1 %copy-start.37 = (bf16[128,768]{1,0:T(8,128)(2,1)}, bf16[128,768]{1,0:T(8,128)(2,1)S(1)}, u32[]{:S(2)}) copy-start(bf16[128,768]{1,0:T(8,128)(2,1)S(1)} %get-tuple-element.46.hid_ref) | copy-start | bytes 589828
  72.8 37.1 %copy-start.39 = (f32[128,256]{1,0:T(8,128)}, f32[128,256]{1,0:T(8,128)S(1)}, u32[]{:S(2)}) copy-start(f32[128,256]{1,0:T(8,128)S(1)} %get-tuple-element.45.gate_ref) | copy-start | bytes 393220
  113.4 19.5 %all-to-all-start.3 = ((bf16[8,40,1536]{2,1,0:T(8,128)(2,1)}), bf16[8,40,1536]{2,1,0:T(8,128)(2,1)S(1)}, u32[]{:S(2)}, u32[]{:S(2)}) async-start(bf16[8,40,1536]{2,1,0:T(8,128)(2,1)} %bitcast.47), calls=%async_computation.3 | async-start | bytes 1966080 | tf_op jit(solution)/shard_map/all_to_all | solution.py:506
  139.0 13.0 %copy-start.4 = (bf16[768,768]{1,0:T(8,128)(2,1)S(1)}, bf16[768,768]{1,0:T(8,128)(2,1)}, u32[]{:S(2)}) copy-start(bf16[768,768]{1,0:T(8,128)(2,1)} %wv_ref.3) | copy-start | bytes 3538948
  144.2 7.7 %copy-start.2 = (bf16[768,768]{1,0:T(8,128)(2,1)S(1)}, bf16[768,768]{1,0:T(8,128)(2,1)}, u32[]{:S(2)}) copy-start(bf16[768,768]{1,0:T(8,128)(2,1)} %wk_ref.3) | copy-start | bytes 3538948
  144.2 13.7 %all-to-all-start.4 = ((bf16[16,64,128]{2,1,0:T(8,128)(2,1)}), bf16[16,64,128]{2,1,0:T(8,128)(2,1)}, u32[]{:S(2)}, u32[]{:S(2)}) async-start(bf16[16,64,128]{2,1,0:T(8,128)(2,1)} %copy-done.24), calls=%async_computation.4 | async-start | bytes 524288 | tf_op jit(solution)/shard_map/all_to_all | solution.py:539
  157.9 27.6 %all-to-all-start.6 = ((bf16[16,48,768]{2,1,0:T(8,128)(2,1)}), bf16[16,48,768]{2,1,0:T(8,128)(2,1)}, u32[]{:S(2)}, u32[]{:S(2)}) async-start(bf16[16,48,768]{2,1,0:T(8,128)(2,1)} %bitcast.45), calls=%async_computation.6 | async-start | bytes 2359296 | tf_op jit(solution)/shard_map/all_to_all | solution.py:540
  164.6 111.6 %all-gather.8.cloned.1.call-start = ((), (), s32[]{:S(2)}) async-start(), calls=%async_computation.11 | async-start | bytes 6340608 | tf_op jit(solution)/shard_map/all_gather | solution.py:581
  205.7 157.8 %reduce-scatter.2.cloned.1.call-start = ((), (), s32[]{:S(2)}) async-start(), calls=%async_computation.12 | async-start | bytes 10027008 | tf_op jit(solution)/shard_map/reduce_scatter | solution.py:522
  206.3 20.6 %copy-start.16 = (bf16[1,128,768]{2,1,0:T(8,128)(2,1)S(1)}, bf16[1,128,768]{2,1,0:T(8,128)(2,1)}, u32[]{:S(2)}) copy-start(bf16[1,128,768]{2,1,0:T(8,128)(2,1)} %param.15) | copy-start | bytes 589828
  206.3 20.6 %copy-start.21 = (f32[128,768]{1,0:T(8,128)S(1)}, f32[128,768]{1,0:T(8,128)}, u32[]{:S(2)}) copy-start(f32[128,768]{1,0:T(8,128)} %copy-done.20) | copy-start | bytes 1179652
  (35 other events, 42.4 us)
Sparse Core Ops, SparseCore 0:
  10.8 88.1 all-gather.3
  101.0 47.2 all-gather.5
  205.9 70.3 all-gather.7
  279.5 83.9 reduce-scatter.1

commit v2 on v1

--- a/solution.py
+++ b/solution.py
@@ -30,7 +30,7 @@
     return lax.dot_general(a, b, (((0,), (0,)), ((), ())), preferred_element_type=f32)
 
 
-def call(kernel, out_shape, vmem=48, flops=0, moved=0, **kw):
+def call(kernel, out_shape, vmem=60, flops=0, moved=0, **kw):
     return pl.pallas_call(
         kernel,
         out_shape=out_shape,
@@ -410,12 +410,99 @@
     out_ref[...] = rgrad_ref[...] + inverse * (scaled - normed * average)
 
 
-def unpack_kernel(all_ref, q_ref, k_ref, v_ref):
+def unpack_kernel(where_ref, *refs):
+    pieces, (q_ref, k_ref, v_ref, wo_ref, tail_ref, bias_ref, all_ref) = refs[:20], refs[20:]
+    step = pl.program_id(0)
+    x, y, z, core = where_ref[0], where_ref[1], where_ref[2], where_ref[3]
+
+    @pl.when(step == 0)
+    def _():
+        for k in range(4):
+            own, ahead, far_one, far_two, behind = pieces[5 * k : 5 * k + 5]
+            full = all_ref.shape[3:]
+            for d, ref in ((0, own), (1, ahead), (3, behind)):
+                all_ref[k // 2, k % 2, d] = ref[...].reshape(full)
+            all_ref[k // 2, k % 2, 2, 0:2] = far_one[...].reshape(2, *full[1:])
+            all_ref[k // 2, k % 2, 2, 2:4] = far_two[...].reshape(2, *full[1:])
+
+    def rows(c, group):
+        exp, half = group // 2, group % 2
+        dx, dy = (x - c % 4 + 4) % 4, (y - c // 4 + 4) % 4
+        dz, other = (z - exp // 2 + 4) % 4, (core + exp % 2) % 2
+        first, second = (dy, dx) if half == 0 else (dx, dy)
+        return all_ref[other, half, first, second, dz]
+
+    def span(c, start, stop):
+        return jnp.concatenate([rows(c, g) for g in range(start // 16, stop // 16)], axis=0)
+
     for ref, at in ((q_ref, 0), (k_ref, HEAD_DIM), (v_ref, 2 * HEAD_DIM)):
-        both = jnp.concatenate(
-            [all_ref[0, at : at + HEAD_DIM, :], all_ref[1, at : at + HEAD_DIM, :]], axis=0
-        )
-        ref[...] = both.astype(f32).T
+        both = [span(2 * step, at, at + HEAD_DIM), span(2 * step + 1, at, at + HEAD_DIM)]
+        ref[...] = jnp.concatenate(both, axis=0).astype(f32).T
+    for k in (0, 1):
+        c = jnp.minimum(2 * step + k, 11)
+        bias_ref[0, 8 * k : 8 * k + 8, :] = rows(c, 15)[0:8, 0:128].astype(f32)
+    for k in (0, 1, 2):
+        c = jnp.minimum(3 * step + k, 15)
+        wo_ref[48 * k : 48 * k + 48, :] = span(c, 192, 240).astype(f32)
+
+    @pl.when(step == 0)
+    def _():
+        total = rows(0, 15).astype(f32)
+        for c in range(1, 16):
+            total = total + rows(c, 15).astype(f32)
+        tail_ref[...] = total
+
+
+def ring(axis, stride, size, block, distance):
+    def to(i):
+        place = (i // stride) % 4
+        return i + ((place + distance) % 4 - place) * stride
+
+    return lax.ppermute(block, axis, [(i, to(i)) for i in range(size)])
+
+
+def gather_ring(axis, stride, size, block):
+    half = block.shape[0] // 2
+    ahead = ring(axis, stride, size, block, 1)
+    behind = ring(axis, stride, size, block, -1)
+    far_one = ring(axis, stride, size, ahead[:half], 1)
+    far_two = ring(axis, stride, size, behind[half:], -1)
+    return [block, ahead, far_one, far_two, behind]
+
+
+def gather_near(axis, stride, size, block):
+    return [block] + [ring(axis, stride, size, block, d) for d in (1, 2, 3)]
+
+
+def split_kernel(*refs):
+    pieces, outs = refs[:4], refs[4:]
+    for half, out in enumerate(outs):
+        for d, ref in enumerate(pieces):
+            block = ref[...]
+            out[16 * d : 16 * d + 16, :] = block[16 * half : 16 * half + 16]
+
+
+def join_kernel(*refs):
+    for k in range(2):
+        for d, ref in enumerate(refs[4 * k : 4 * k + 4]):
+            size = ref.shape[0]
+            refs[8 + k][d * size : (d + 1) * size, :] = ref[...]
+
+
+def gather_near_all(share, n_ctx, n_exp):
+    width = share.shape[1]
+    along_z = gather_near("exp", 2, n_exp, share)
+    quarter = sds((64, width), bf16)
+    first, second = call(split_kernel, (quarter, quarter), vmem=8)(*along_z)
+    plane = gather_near("ctx", 1, n_ctx, first) + gather_near("ctx", 4, n_ctx, second)
+    side = sds((256, width), bf16)
+    return call(join_kernel, (side, side), vmem=8)(*plane)
+
+
+def gather_far(first, second, n_ctx, n_exp):
+    own = gather_ring("ctx", 4, n_ctx, first) + gather_ring("ctx", 1, n_ctx, second)
+    pairs = [(i, i ^ 1) for i in range(n_exp)]
+    return own + [lax.ppermute(piece, "exp", pairs) for piece in own]
 
 
 def on_device(
@@ -447,6 +534,15 @@
         moved=4 * MB,
     )(x, gain_one, segment_ids, query_weight, key_weight, value_weight)
     qkv = lax.all_to_all(qkv, "ctx", split_axis=0, concat_axis=0, tiled=True)
+    at = jnp.minimum(head, HEADS - 1) * HEAD_DIM
+    own_weights = jnp.concatenate(
+        [
+            lax.dynamic_slice_in_dim(w, at, HEAD_DIM, axis=1).T
+            for w in (query_weight, key_weight, value_weight)
+        ],
+        axis=0,
+    )
+    qkv, own_weights = lax.optimization_barrier((qkv, own_weights))
     hidden_all = lax.all_gather(hidden, "ctx", axis=0, tiled=True)
 
     tiles = length // TQ
@@ -519,7 +615,6 @@
         moved=16 * MB,
     )(received, pre, act)
     returned, weight_grads = lax.optimization_barrier((returned, weight_grads))
-    summed = lax.psum_scatter(weight_grads, "ctx", scatter_dimension=0, tiled=True)
 
     layer_out, residual_grad, gt, wo_grad, small = call(
         combine_kernel,
@@ -537,6 +632,8 @@
         router_weight.astype(f32).T, output_weight, ot,
     )
     gt = lax.all_to_all(gt, "ctx", split_axis=0, concat_axis=0, tiled=True)
+    weight_grads, hidden_all, gt = lax.optimization_barrier((weight_grads, hidden_all, gt))
+    summed = lax.psum_scatter(weight_grads, "ctx", scatter_dimension=0, tiled=True)
     wo_parts = lax.all_to_all(
         wo_grad.reshape(n_ctx, width // n_ctx, width), "ctx", split_axis=0, concat_axis=0, tiled=True
     )
@@ -560,14 +657,6 @@
         moved=20 * MB,
     )(qkv, gt, otf, lse, bucket_row, tab)
 
-    at = jnp.minimum(head, HEADS - 1) * HEAD_DIM
-    own_weights = jnp.concatenate(
-        [
-            lax.dynamic_slice_in_dim(w, at, HEAD_DIM, axis=1).T
-            for w in (query_weight, key_weight, value_weight)
-        ],
-        axis=0,
-    )
     packed = call(
         pack_kernel,
         sds((ROWS, width), bf16),
@@ -577,31 +666,51 @@
     parts = lax.all_to_all(
         packed.reshape(n_exp, ROWS // n_exp, width), "exp", split_axis=0, concat_axis=0, tiled=True
     )
+    parts, dqkv = lax.optimization_barrier((parts, dqkv))
+    back = lax.all_to_all(dqkv, "ctx", split_axis=0, concat_axis=0, tiled=True)
     share = jnp.sum(parts.astype(f32), axis=0).astype(bf16)
-    everything = lax.all_gather(share, ("ctx", "exp"), axis=0, tiled=True)
-    everything = everything.reshape(n_ctx, ROWS, width)
-
-    back = lax.all_to_all(dqkv, "ctx", split_axis=0, concat_axis=0, tiled=True)
     tokens_grad = call(
         tokens_kernel,
         sds((rows, width), f32),
         flops=6 * rows * width * width,
         moved=6 * MB,
     )(back, x, gain_one, residual_grad, query_weight, key_weight, value_weight)
+    first, second = gather_near_all(share, n_ctx, n_exp)
+    first, second, tokens_grad = lax.optimization_barrier((first, second, tokens_grad))
+    everything = gather_far(first, second, n_ctx, n_exp)
 
     full = sds((width, width), f32)
-    column = pl.BlockSpec((width, 128), lambda i: (0, i))
-    query_grad, key_grad, value_grad = call(
+    column = pl.BlockSpec((width, 128), lambda i, w: (0, i))
+    exp = lax.axis_index("exp")
+    where = jnp.stack([head % 4, head // 4, exp // 2, exp % 2]).astype(jnp.int32)
+    query_grad, key_grad, value_grad, output_grad, tails, bias_rows = call(
         unpack_kernel,
-        (full, full, full),
-        grid=(HEADS // 2,),
-        in_specs=[pl.BlockSpec((2, ROWS, width), lambda i: (i, 0, 0))],
-        out_specs=[column, column, column],
+        (
+            full,
+            full,
+            full,
+            full,
+            sds((16, width), f32),
+            sds((HEADS // 2, 16, 128), f32),
+        ),
+        grid_spec=pltpu.PrefetchScalarGridSpec(
+            num_scalar_prefetch=1,
+            grid=(HEADS // 2,),
+            in_specs=[pl.BlockSpec(piece.shape, lambda i, w: (0, 0)) for piece in everything],
+            out_specs=[
+                column,
+                column,
+                column,
+                pl.BlockSpec((144, width), lambda i, w: (i, 0)),
+                pl.BlockSpec((16, width), lambda i, w: (0, 0)),
+                pl.BlockSpec((1, 16, 128), lambda i, w: (i, 0, 0)),
+            ],
+            scratch_shapes=[pltpu.VMEM((2, 2, 4, 4, 4, 16, width), bf16)],
+        ),
+        vmem=40,
         moved=16 * MB,
-    )(everything)
-    output_grad = everything[:, 192:240].reshape(width, width).astype(f32)
-    tails = jnp.sum(everything[:, 240:256].astype(f32), axis=0)
-    table_grad = everything[:HEADS, 242, : bias_table.shape[0]].astype(f32).T
+    )(where, *everything)
+    table_grad = bias_rows.reshape(HEADS, 8, 128)[:, 2, : bias_table.shape[0]].T
     return (
         layer_out[None],
         tokens_grad[None],

time: 377 us -> 296 us (0.79)
  waiting for transfers between devices: 154 us -> 65.4 us
  starting transfers between devices: 28.5 us -> 60 us
  local copies, waits for them, and re-layouts: 44.7 us -> 25.7 us
  Pallas kernels: 66.5 us -> 81.6 us
  blocking collectives: 55.7 us -> 43.4 us
  other arithmetic: 10.1 us -> 4.55 us
    reduce_scatter x1, waiting for transfers between devices: 73.9 us -> 0.01 us  [on_device(): lax.psum_scatter(weight_grads, 'ctx', scatter_dimension=0, tiled=True)]
    all_gather x1 -> x0, waiting for transfers between devices: 47.3 us -> none  [on_device(): everything = lax.all_gather(share, ('ctx', 'exp'), axis=0, tiled=True)]
    ppermute x0 -> x27, starting transfers between devices: none -> 31 us  [the longest x10 15.9 us: gather_far(): return own + [lax.ppermute(piece, 'exp', pairs) for piece in own]]
    ppermute x0 -> x27, waiting for transfers between devices: none -> 26.3 us  [the longest x17 24.6 us: ring(): return lax.ppermute(block, axis, [(i, to(i)) for i in range(size)])]
    unnamed x109 -> x57, local copies, waits for them, and re-layouts: 40.2 us -> 19.6 us
    all_to_all x1 -> x0, blocking collectives: 20.5 us -> none  [on_device(): back = lax.all_to_all(dqkv, 'ctx', split_axis=0, concat_axis=0, tiled=True)]
    all_gather x1, waiting for transfers between devices: 0.01 us -> 8.43 us  [on_device(): hidden_all = lax.all_gather(hidden, 'ctx', axis=0, tiled=True)]
    all_to_all x1, waiting for transfers between devices: 0.01 us -> 5.56 us  [on_device(): lax.all_to_all(wo_grad.reshape(n_ctx, width // n_ctx, width), 'ctx', spli...]
  transfers between devices with their start and end apart: 9 -> 36, of which waited for: 6 -> 17; matrix products, arithmetic and copies ran while one was open for 4% -> 3% of each run, Pallas kernels for 17% -> 28%
where the time goes in v2:
time: 296 us; the launch traced here: 295 us
  Pallas kernels  81.6 us (28%)
  waiting for transfers between devices  65.4 us (22%)
  starting transfers between devices  60 us (20%)
  blocking collectives  43.4 us (15%)
  local copies, waits for them, and re-layouts  25.7 us (9%)
  between operations  14 us (5%)
  other arithmetic  4.55 us (2%)
    all_to_all x1, blocking collectives, on_device(): lax.all_to_all(send, 'exp', split_axis=0, concat_axis=0, tiled=True)  27.6 us
    ppermute x17, waiting for transfers between devices, ring(): return lax.ppermute(block, axis, [(i, to(i)) for i in range(size)])  24.6 us
    unnamed x57, local copies, waits for them, and re-layouts  19.6 us
    ppermute x10, starting transfers between devices, gather_far(): return own + [lax.ppermute(piece, 'exp', pairs) for piece in own]  15.9 us
    all_to_all x1, blocking collectives, on_device(): lax.all_to_all(packed.reshape(n_exp, ROWS // n_exp, width), 'exp', split_...  15.8 us
    ppermute x17, starting transfers between devices, ring(): return lax.ppermute(block, axis, [(i, to(i)) for i in range(size)])  15.1 us
    all_to_all x1, waiting for transfers between devices, on_device(): qkv = lax.all_to_all(qkv, 'ctx', split_axis=0, concat_axis=0, tiled=True)  15.1 us
    pallas_call x1, Pallas kernels, on_device(): call(attend_back_kernel, (sds((n_ctx, 3 * HEAD_DIM, rows), bf16), sds((3...  14.6 us
  transfers between devices with their start and end apart: 36, of which 17 were waited for; matrix products, arithmetic and copies ran while one was open for 3% of the time, Pallas kernels for 28%

profile of v2, /device:TPU:1, one launch (start us, length us, event | category | flops | bytes accessed | tf_op | source)
XLA Modules:
  0.0 294.6 jit_solution(14668557522412669584)
XLA Ops:
  13.6 7.6 %all-to-all-start = ((bf16[16,224,128]{2,1,0:T(8,128)(2,1)}), bf16[16,224,128]{2,1,0:T(8,128)(2,1)S(1)}, u32[]{:S(2)}, u32[]{:S(2)}) async-start(bf16[16,224,128]{2,1,0:T(8,128)(2,1)} %get-tuple-element.54), calls=%async_computation | async-start | bytes 1835008 | tf_op jit(solution)/shard_map/all_to_all | solution.py:536
  25.5 15.1 %all-to-all-done.recv_ref = bf16[16,224,128]{2,1,0:T(8,128)(2,1)S(1)} async-done(((bf16[16,224,128]{2,1,0:T(8,128)(2,1)}), bf16[16,224,128]{2,1,0:T(8,128)(2,1)S(1)}, u32[]{:S(2)}, u32[]{:S(2)}) %all-to-all-start) | async-done | bytes 917536 | tf_op jit(solution)/shard_map/all_to_all | solution.py:536
  41.5 12.8 %shard_map.239 = (bf16[16,64,128]{2,1,0:T(8,128)(2,1)}, f32[8,64,256]{2,1,0:T(8,128)}, f32[8,1,256]{2,1,0:T(1,128)}) custom-call(bf16[16,224,128]{2,1,0:T(8,128)(2,1)} %copy-done.15, s32[1,2048]{1,0:T(1,128)} %bitcast.65, f32[32,1]{1,0:T(8,128)} %pad_dynamic-slice_fusion.tab_ref), custom_call_target="tpu_custom_call" | custom-call | flops 8000000000 | bytes 10485760 | tf_op jit(solution)/shard_map/pallas_call | solution.py:549
  60.0 8.1 %all-to-all-done.1.ot_ref = bf16[16,64,128]{2,1,0:T(8,128)(2,1)S(1)} async-done(((bf16[16,64,128]{2,1,0:T(8,128)(2,1)}), bf16[16,64,128]{2,1,0:T(8,128)(2,1)S(1)}, u32[]{:S(2)}, u32[]{:S(2)}) %all-to-all-start.1) | async-done | bytes 262176 | tf_op jit(solution)/shard_map/all_to_all | solution.py:560
  72.6 27.6 %all_to_all.53 = bf16[8,40,1536]{2,1,0:T(8,128)(2,1)} all-to-all(bf16[8,40,1536]{2,1,0:T(8,128)(2,1)} %bitcast.49), channel_id=1, replica_groups=mesh['ctx'=16,'exp'=8] {'exp'}, dimensions={0} | all-to-all | bytes 1966080 | tf_op jit(solution)/shard_map/all_to_all | solution.py:575
  100.2 12.4 %shard_map.241 = (bf16[320,1536]{1,0:T(8,128)(2,1)}, bf16[320,3072]{1,0:T(8,128)(2,1)}, bf16[320,3072]{1,0:T(8,128)(2,1)}) custom-call(bf16[320,1536]{1,0:T(8,128)(2,1)} %bitcast.44, bf16[768,6144]{1,0:T(8,128)(2,1)} %all-gather.3.cloned.1.call-done.up_ref.down_ref, bf16[768,6144]{1,0:T(8,128)(2,1)} %all-gather.3.cloned.1.call-done.up_ref.down_ref), custom_call_target="tpu_custom_call" | custom-call | flops 6039797760 | bytes 16777216 | tf_op jit(solution)/shard_map/pallas_call | solution.py:580
  112.6 4.4 %all-to-all-start.3 = ((bf16[8,40,1536]{2,1,0:T(8,128)(2,1)}), bf16[8,40,1536]{2,1,0:T(8,128)(2,1)S(1)}, u32[]{:S(2)}, u32[]{:S(2)}) async-start(bf16[8,40,1536]{2,1,0:T(8,128)(2,1)} %bitcast.48), calls=%async_computation.3 | async-start | bytes 1966080 | tf_op jit(solution)/shard_map/all_to_all | solution.py:602
  117.6 13.0 %shard_map.242 = bf16[768,6144]{1,0:T(8,128)(2,1)} custom-call(bf16[320,1536]{1,0:T(8,128)(2,1)} %bitcast.45, bf16[320,3072]{1,0:T(8,128)(2,1)} %get-tuple-element.59.pre_ref, bf16[320,3072]{1,0:T(8,128)(2,1)} %get-tuple-element.60.act_ref), custom_call_target="tpu_custom_call" | custom-call | flops 3019898880 | bytes 16777216 | tf_op jit(solution)/shard_map/pallas_call | solution.py:603
  132.4 5.2 %shard_map.243 = (bf16[128,768]{1,0:T(8,128)(2,1)}, f32[128,768]{1,0:T(8,128)}, bf16[16,64,128]{2,1,0:T(8,128)(2,1)}, bf16[768,768]{1,0:T(8,128)(2,1)}, f32[16,768]{1,0:T(8,128)}) custom-call(bf16[320,1536]{1,0:T(8,128)(2,1)} %bitcast.47, f32[128,768]{1,0:T(8,128)} %get-tuple-element.62.res_ref, bf16[128,768]{1,0:T(8,128)(2,1)} %bitcast.64, ...), custom_call_target="tpu_custom_call" | custom-call | flops 1000000000 | bytes 6291456 | tf_op jit(solution)/shard_map/pallas_call | solution.py:619
  137.6 4.5 %all-to-all-start.4 = ((bf16[16,64,128]{2,1,0:T(8,128)(2,1)}), bf16[16,64,128]{2,1,0:T(8,128)(2,1)S(1)}, u32[]{:S(2)}, u32[]{:S(2)}) async-start(bf16[16,64,128]{2,1,0:T(8,128)(2,1)} %get-tuple-element.68), calls=%async_computation.4 | async-start | bytes 524288 | tf_op jit(solution)/shard_map/all_to_all | solution.py:634
  142.1 8.4 %all-gather.5.cloned.1.call-done.hid_ref = bf16[2048,768]{1,0:T(8,128)(2,1)} async-done(((bf16[128,768]{1,0:T(8,128)(2,1)}), bf16[2048,768]{1,0:T(8,128)(2,1)}) %all-gather.5.cloned.1.call-update) | async-done | bytes 3145744 | tf_op jit(solution)/shard_map/all_gather | solution.py:546
  152.4 3.9 %all-to-all-start.5 = ((bf16[16,48,768]{2,1,0:T(8,128)(2,1)}), bf16[16,48,768]{2,1,0:T(8,128)(2,1)S(1)}, u32[]{:S(2)}, u32[]{:S(2)}) async-start(bf16[16,48,768]{2,1,0:T(8,128)(2,1)} %bitcast.16), calls=%async_computation.5 | async-start | bytes 2359296 | tf_op jit(solution)/shard_map/all_to_all | solution.py:637
  156.3 14.6 %shard_map.244 = (bf16[16,192,128]{2,1,0:T(8,128)(2,1)}, bf16[192,2048]{1,0:T(8,128)(2,1)}, f32[8,128]{1,0:T(8,128)}) custom-call(bf16[16,224,128]{2,1,0:T(8,128)(2,1)} %copy-done.15, bf16[16,64,128]{2,1,0:T(8,128)(2,1)} %copy-done.17, f32[8,64,256]{2,1,0:T(8,128)} %get-tuple-element.70.otf_ref, f32[8,1,256]{2,1,0:T(1,128)} %get-tuple-element.71.lse_ref, ...), custom_call_target="tpu_custom_call" | custom-call | flops 20000000000 | bytes 20971520 | tf_op jit(solution)/shard_map/pallas_call | solution.py:641
  170.8 5.6 %all-to-all-done.5.wo_ref = bf16[16,48,768]{2,1,0:T(8,128)(2,1)S(1)} async-done(((bf16[16,48,768]{2,1,0:T(8,128)(2,1)}), bf16[16,48,768]{2,1,0:T(8,128)(2,1)S(1)}, u32[]{:S(2)}, u32[]{:S(2)}) %all-to-all-start.5) | async-done | bytes 1179680 | tf_op jit(solution)/shard_map/all_to_all | solution.py:637
  177.4 4.3 %shard_map.245 = bf16[256,768]{1,0:T(8,128)(2,1)} custom-call(bf16[192,2048]{1,0:T(8,128)(2,1)} %get-tuple-element.72.flat_ref, bf16[2048,768]{1,0:T(8,128)(2,1)} %all-gather.5.cloned.1.call-done.hid_ref, bf16[192,768]{1,0:T(8,128)(2,1)} %pad_maximum_fusion.1.wt_ref, f32[1,768]{1,0:T(1,128)} %reshape.46.gain_ref, bf16[16,48,768]{2,1,0:T(8,128)(2,1)} %copy-done.12, ...), custom_call_target="tpu_custom_call" | custom-call | flops 603979776 | bytes 6291456 | tf_op jit(solution)/shard_map/pallas_call | solution.py:660
  181.7 15.8 %all_to_all.54 = bf16[8,32,768]{2,1,0:T(8,128)(2,1)S(1)} all-to-all(bf16[8,32,768]{2,1,0:T(8,128)(2,1)} %bitcast.46), channel_id=1, replica_groups=mesh['ctx'=16,'exp'=8] {'exp'}, dimensions={0} | all-to-all | bytes 786432 | tf_op jit(solution)/shard_map/all_to_all | solution.py:666
  197.5 4.9 %all-to-all-start.7 = ((bf16[16,192,128]{2,1,0:T(8,128)(2,1)}), bf16[16,192,128]{2,1,0:T(8,128)(2,1)S(1)}, u32[]{:S(2)}, u32[]{:S(2)}) async-start(bf16[16,192,128]{2,1,0:T(8,128)(2,1)} %get-tuple-element.84), calls=%async_computation.7 | async-start | bytes 1572864 | tf_op jit(solution)/shard_map/all_to_all | solution.py:670
  216.0 7.5 %collective-permute-done.5.refs_3_ = bf16[64,768]{1,0:T(8,128)(2,1)S(1)} collective-permute-done((bf16[64,768]{1,0:T(8,128)(2,1)S(1)}, bf16[64,768]{1,0:T(8,128)(2,1)S(1)}, u32[]{:S(2)}, u32[]{:S(2)}) %collective-permute-start.5) | collective-permute-done | bytes 98336 | tf_op jit(solution)/shard_map/ppermute | solution.py:461
  224.6 4.3 %collective-permute-done.6.refs_5_ = bf16[64,768]{1,0:T(8,128)(2,1)S(1)} collective-permute-done((bf16[64,768]{1,0:T(8,128)(2,1)S(1)}, bf16[64,768]{1,0:T(8,128)(2,1)S(1)}, u32[]{:S(2)}, u32[]{:S(2)}) %collective-permute-start.6) | collective-permute-done | bytes 98336 | tf_op jit(solution)/shard_map/ppermute | solution.py:461
  229.8 4.5 %shard_map.248 = f32[128,768]{1,0:T(8,128)} custom-call(bf16[16,192,128]{2,1,0:T(8,128)(2,1)} %copy-done.13, bf16[128,768]{1,0:T(8,128)(2,1)} %bitcast.52, f32[1,768]{1,0:T(1,128)} %reshape.46.gain_ref, f32[128,768]{1,0:T(8,128)} %get-tuple-element.85.rgrad_ref, bf16[768,768]{1,0:T(8,128)(2,1)} %wq_ref.3, bf16[768,768]{1,0:T(8,128)(2,1)} %wk_ref.3, ...), custom_call_target="tpu_custom_call" | custom-call | flops 452984832 | bytes 6291456 | tf_op jit(solution)/shard_map/pallas_call | solution.py:672
  237.2 3.9 %collective-permute-start.17 = (bf16[256,768]{1,0:T(8,128)(2,1)S(1)}, bf16[256,768]{1,0:T(8,128)(2,1)S(1)}, u32[]{:S(2)}, u32[]{:S(2)}) collective-permute-start(bf16[256,768]{1,0:T(8,128)(2,1)S(1)} %get-tuple-element.87.refs_0_), channel_id=1, source_target_pairs={{0,1},{1,0},{2,3},{3,2},{4,5},{5,4},{6,7},{7,6},{8,9},{9,8},{10,11... | collective-permute-start | bytes 1179656 | tf_op jit(solution)/shard_map/ppermute | solution.py:505
  242.1 7.8 %collective-permute-start.22 = (bf16[256,768]{1,0:T(8,128)(2,1)S(1)}, bf16[256,768]{1,0:T(8,128)(2,1)S(1)}, u32[]{:S(2)}, u32[]{:S(2)}) collective-permute-start(bf16[256,768]{1,0:T(8,128)(2,1)S(1)} %get-tuple-element.88.refs_5_), channel_id=1, source_target_pairs={{0,1},{1,0},{2,3},{3,2},{4,5},{5,4},{6,7},{7,6},{8,9},{9,8},{10,11... | collective-permute-start | bytes 1179656 | tf_op jit(solution)/shard_map/ppermute | solution.py:505
  253.3 6.1 %collective-permute-done.12.refs_3_ = bf16[128,768]{1,0:T(8,128)(2,1)S(1)} collective-permute-done((bf16[128,768]{1,0:T(8,128)(2,1)S(1)}, bf16[128,768]{1,0:T(8,128)(2,1)S(1)}, u32[]{:S(2)}, u32[]{:S(2)}) %collective-permute-start.12) | collective-permute-done | bytes 196640 | tf_op jit(solution)/shard_map/ppermute | solution.py:461
  275.1 7.1 %shard_map.249 = (f32[768,768]{1,0:T(8,128)}, f32[768,768]{1,0:T(8,128)}, f32[768,768]{1,0:T(8,128)}, f32[768,768]{1,0:T(8,128)}, f32[16,768]{1,0:T(8,128)S(1)}, /*index=5*/f32[6,16,128]{2,1,0:T(8,128)S(1)}) custom-call(s32[4]{0:T(128)S(1)} %pad_add_fusion.where_ref, bf16[256,768]{1,0:T(8,128)(2,1)S(1)} %get-tuple-element.87.refs_0_, ...), custom_call_target="tpu_custom_call" | custom-call | bytes 16777216 | tf_op jit(solution)/shard_map/pallas_call | solution.py:686
  (141 shorter events, 71.1 us)
Async XLA Ops:
  7.2 93.0 %all-gather.3.cloned.1.call-start = ((), (), s32[]{:S(2)}) async-start(), calls=%async_computation.9 | async-start | bytes 10027008 | tf_op jit(solution)/shard_map/all_gather | solution.py:527
  9.2 141.4 %all-gather.5.cloned.1.call-start = ((), (), s32[]{:S(2)}) async-start(), calls=%async_computation.10 | async-start | bytes 3342336 | tf_op jit(solution)/shard_map/all_gather | solution.py:546
  13.6 26.9 %all-to-all-start = ((bf16[16,224,128]{2,1,0:T(8,128)(2,1)}), bf16[16,224,128]{2,1,0:T(8,128)(2,1)S(1)}, u32[]{:S(2)}, u32[]{:S(2)}) async-start(bf16[16,224,128]{2,1,0:T(8,128)(2,1)} %get-tuple-element.54), calls=%async_computation | async-start | bytes 1835008 | tf_op jit(solution)/shard_map/all_to_all | solution.py:536
  54.3 13.8 %all-to-all-start.1 = ((bf16[16,64,128]{2,1,0:T(8,128)(2,1)}), bf16[16,64,128]{2,1,0:T(8,128)(2,1)S(1)}, u32[]{:S(2)}, u32[]{:S(2)}) async-start(bf16[16,64,128]{2,1,0:T(8,128)(2,1)} %get-tuple-element.56), calls=%async_computation.1 | async-start | bytes 524288 | tf_op jit(solution)/shard_map/all_to_all | solution.py:560
  112.6 18.8 %all-to-all-start.3 = ((bf16[8,40,1536]{2,1,0:T(8,128)(2,1)}), bf16[8,40,1536]{2,1,0:T(8,128)(2,1)S(1)}, u32[]{:S(2)}, u32[]{:S(2)}) async-start(bf16[8,40,1536]{2,1,0:T(8,128)(2,1)} %bitcast.48), calls=%async_computation.3 | async-start | bytes 1966080 | tf_op jit(solution)/shard_map/all_to_all | solution.py:602
  137.6 14.1 %all-to-all-start.4 = ((bf16[16,64,128]{2,1,0:T(8,128)(2,1)}), bf16[16,64,128]{2,1,0:T(8,128)(2,1)S(1)}, u32[]{:S(2)}, u32[]{:S(2)}) async-start(bf16[16,64,128]{2,1,0:T(8,128)(2,1)} %get-tuple-element.68), calls=%async_computation.4 | async-start | bytes 524288 | tf_op jit(solution)/shard_map/all_to_all | solution.py:634
  142.1 142.0 %reduce-scatter.2.cloned.1.call-start = ((), (), s32[]{:S(2)}) async-start(), calls=%async_computation.11 | async-start | bytes 10027008 | tf_op jit(solution)/shard_map/reduce_scatter | solution.py:636
  152.4 24.0 %all-to-all-start.5 = ((bf16[16,48,768]{2,1,0:T(8,128)(2,1)}), bf16[16,48,768]{2,1,0:T(8,128)(2,1)S(1)}, u32[]{:S(2)}, u32[]{:S(2)}) async-start(bf16[16,48,768]{2,1,0:T(8,128)(2,1)} %bitcast.16), calls=%async_computation.5 | async-start | bytes 2359296 | tf_op jit(solution)/shard_map/all_to_all | solution.py:637
  197.5 31.4 %all-to-all-start.7 = ((bf16[16,192,128]{2,1,0:T(8,128)(2,1)}), bf16[16,192,128]{2,1,0:T(8,128)(2,1)S(1)}, u32[]{:S(2)}, u32[]{:S(2)}) async-start(bf16[16,192,128]{2,1,0:T(8,128)(2,1)} %get-tuple-element.84), calls=%async_computation.7 | async-start | bytes 1572864 | tf_op jit(solution)/shard_map/all_to_all | solution.py:670
  209.3 14.2 %collective-permute-start.5 = (bf16[64,768]{1,0:T(8,128)(2,1)S(1)}, bf16[64,768]{1,0:T(8,128)(2,1)S(1)}, u32[]{:S(2)}, u32[]{:S(2)}) collective-permute-start(bf16[64,768]{1,0:T(8,128)(2,1)S(1)} %get-tuple-element.80.refs_0_), channel_id=1, source_target_pairs={{0,24},{8,0},{16,8},{24,16},{32,56},{40,32},{48,40},{56,48},{64,88... | collective-permute-start | bytes 294920 | tf_op jit(solution)/shard_map/ppermute | solution.py:461
  212.0 12.1 %collective-permute-start.4 = (bf16[64,768]{1,0:T(8,128)(2,1)S(1)}, bf16[64,768]{1,0:T(8,128)(2,1)S(1)}, u32[]{:S(2)}, u32[]{:S(2)}) collective-permute-start(bf16[64,768]{1,0:T(8,128)(2,1)S(1)} %get-tuple-element.80.refs_0_), channel_id=1, source_target_pairs={{0,16},{8,24},{16,0},{24,8},{32,48},{40,56},{48,32},{56,40},{64,80... | collective-permute-start | bytes 294920 | tf_op jit(solution)/shard_map/ppermute | solution.py:461
  212.5 12.0 %collective-permute-start.3 = (bf16[64,768]{1,0:T(8,128)(2,1)S(1)}, bf16[64,768]{1,0:T(8,128)(2,1)S(1)}, u32[]{:S(2)}, u32[]{:S(2)}) collective-permute-start(bf16[64,768]{1,0:T(8,128)(2,1)S(1)} %get-tuple-element.80.refs_0_), channel_id=1, source_target_pairs={{0,8},{8,16},{16,24},{24,0},{32,40},{40,48},{48,56},{56,32},{64,72... | collective-permute-start | bytes 294920 | tf_op jit(solution)/shard_map/ppermute | solution.py:461
  213.1 11.5 %collective-permute-start.8 = (bf16[64,768]{1,0:T(8,128)(2,1)S(1)}, bf16[64,768]{1,0:T(8,128)(2,1)S(1)}, u32[]{:S(2)}, u32[]{:S(2)}) collective-permute-start(bf16[64,768]{1,0:T(8,128)(2,1)S(1)} %get-tuple-element.81.refs_4_), channel_id=1, source_target_pairs={{0,96},{8,104},{16,112},{24,120},{32,0},{40,8},{48,16},{56,24},{64... | collective-permute-start | bytes 294920 | tf_op jit(solution)/shard_map/ppermute | solution.py:461
  215.5 9.1 %collective-permute-start.7 = (bf16[64,768]{1,0:T(8,128)(2,1)S(1)}, bf16[64,768]{1,0:T(8,128)(2,1)S(1)}, u32[]{:S(2)}, u32[]{:S(2)}) collective-permute-start(bf16[64,768]{1,0:T(8,128)(2,1)S(1)} %get-tuple-element.81.refs_4_), channel_id=1, source_target_pairs={{0,64},{8,72},{16,80},{24,88},{32,96},{40,104},{48,112},{56,120},{... | collective-permute-start | bytes 294920 | tf_op jit(solution)/shard_map/ppermute | solution.py:461
  234.3 7.8 %collective-permute-start.11 = (bf16[256,768]{1,0:T(8,128)(2,1)S(1)}, bf16[256,768]{1,0:T(8,128)(2,1)S(1)}, u32[]{:S(2)}, u32[]{:S(2)}) collective-permute-start(bf16[256,768]{1,0:T(8,128)(2,1)S(1)} %get-tuple-element.87.refs_0_), channel_id=1, source_target_pairs={{0,96},{8,104},{16,112},{24,120},{32,0},{40,8},{48,16},{56,24},{64... | collective-permute-start | bytes 1179656 | tf_op jit(solution)/shard_map/ppermute | solution.py:461
  234.7 15.2 %collective-permute-start.9 = (bf16[256,768]{1,0:T(8,128)(2,1)S(1)}, bf16[256,768]{1,0:T(8,128)(2,1)S(1)}, u32[]{:S(2)}, u32[]{:S(2)}) collective-permute-start(bf16[256,768]{1,0:T(8,128)(2,1)S(1)} %get-tuple-element.87.refs_0_), channel_id=1, source_target_pairs={{0,32},{8,40},{16,48},{24,56},{32,64},{40,72},{48,80},{56,88},{64,... | collective-permute-start | bytes 1179656 | tf_op jit(solution)/shard_map/ppermute | solution.py:461
  235.8 15.8 %collective-permute-start.15 = (bf16[256,768]{1,0:T(8,128)(2,1)S(1)}, bf16[256,768]{1,0:T(8,128)(2,1)S(1)}, u32[]{:S(2)}, u32[]{:S(2)}) collective-permute-start(bf16[256,768]{1,0:T(8,128)(2,1)S(1)} %get-tuple-element.88.refs_5_), channel_id=1, source_target_pairs={{0,24},{8,0},{16,8},{24,16},{32,56},{40,32},{48,40},{56,48},{64,88... | collective-permute-start | bytes 1179656 | tf_op jit(solution)/shard_map/ppermute | solution.py:461
  236.0 15.6 %collective-permute-start.13 = (bf16[256,768]{1,0:T(8,128)(2,1)S(1)}, bf16[256,768]{1,0:T(8,128)(2,1)S(1)}, u32[]{:S(2)}, u32[]{:S(2)}) collective-permute-start(bf16[256,768]{1,0:T(8,128)(2,1)S(1)} %get-tuple-element.88.refs_5_), channel_id=1, source_target_pairs={{0,8},{8,16},{16,24},{24,0},{32,40},{40,48},{48,56},{56,32},{64,72... | collective-permute-start | bytes 1179656 | tf_op jit(solution)/shard_map/ppermute | solution.py:461
  237.2 15.0 %collective-permute-start.17 = (bf16[256,768]{1,0:T(8,128)(2,1)S(1)}, bf16[256,768]{1,0:T(8,128)(2,1)S(1)}, u32[]{:S(2)}, u32[]{:S(2)}) collective-permute-start(bf16[256,768]{1,0:T(8,128)(2,1)S(1)} %get-tuple-element.87.refs_0_), channel_id=1, source_target_pairs={{0,1},{1,0},{2,3},{3,2},{4,5},{5,4},{6,7},{7,6},{8,9},{9,8},{10,11... | collective-permute-start | bytes 1179656 | tf_op jit(solution)/shard_map/ppermute | solution.py:505
  242.1 21.3 %collective-permute-start.22 = (bf16[256,768]{1,0:T(8,128)(2,1)S(1)}, bf16[256,768]{1,0:T(8,128)(2,1)S(1)}, u32[]{:S(2)}, u32[]{:S(2)}) collective-permute-start(bf16[256,768]{1,0:T(8,128)(2,1)S(1)} %get-tuple-element.88.refs_5_), channel_id=1, source_target_pairs={{0,1},{1,0},{2,3},{3,2},{4,5},{5,4},{6,7},{7,6},{8,9},{9,8},{10,11... | collective-permute-start | bytes 1179656 | tf_op jit(solution)/shard_map/ppermute | solution.py:505
  249.9 9.5 %collective-permute-start.12 = (bf16[128,768]{1,0:T(8,128)(2,1)S(1)}, bf16[128,768]{1,0:T(8,128)(2,1)S(1)}, u32[]{:S(2)}, u32[]{:S(2)}) collective-permute-start(bf16[128,768]{1,0:T(8,128)(2,1)S(1)} %slice.41), channel_id=1, source_target_pairs={{0,96},{8,104},{16,112},{24,120},{32,0},{40,8},{48,16},{56,24},{64... | collective-permute-start | bytes 589832 | tf_op jit(solution)/shard_map/ppermute | solution.py:461
  251.5 9.7 %collective-permute-start.10 = (bf16[128,768]{1,0:T(8,128)(2,1)S(1)}, bf16[128,768]{1,0:T(8,128)(2,1)S(1)}, u32[]{:S(2)}, u32[]{:S(2)}) collective-permute-start(bf16[128,768]{1,0:T(8,128)(2,1)S(1)} %slice.40), channel_id=1, source_target_pairs={{0,32},{8,40},{16,48},{24,56},{32,64},{40,72},{48,80},{56,88},{64,... | collective-permute-start | bytes 589832 | tf_op jit(solution)/shard_map/ppermute | solution.py:461
  251.6 11.7 %collective-permute-start.16 = (bf16[128,768]{1,0:T(8,128)(2,1)S(1)}, bf16[128,768]{1,0:T(8,128)(2,1)S(1)}, u32[]{:S(2)}, u32[]{:S(2)}) collective-permute-start(bf16[128,768]{1,0:T(8,128)(2,1)S(1)} %slice.43), channel_id=1, source_target_pairs={{0,24},{8,0},{16,8},{24,16},{32,56},{40,32},{48,40},{56,48},{64,88... | collective-permute-start | bytes 589832 | tf_op jit(solution)/shard_map/ppermute | solution.py:461
  252.2 12.3 %collective-permute-start.14 = (bf16[128,768]{1,0:T(8,128)(2,1)S(1)}, bf16[128,768]{1,0:T(8,128)(2,1)}, u32[]{:S(2)}, u32[]{:S(2)}) collective-permute-start(bf16[128,768]{1,0:T(8,128)(2,1)S(1)} %slice.42), channel_id=1, source_target_pairs={{0,8},{8,16},{16,24},{24,0},{32,40},{40,48},{48,56},{56,32},{64,72... | collective-permute-start | bytes 589832 | tf_op jit(solution)/shard_map/ppermute | solution.py:461
  (36 other events, 136.6 us)
Sparse Core Ops, SparseCore 0:
  10.7 88.0 all-gather.2
  101.0 49.5 all-gather.4
  154.0 106.7 reduce-scatter.1

commit v3 on v2

--- a/solution.py
+++ b/solution.py
@@ -30,7 +30,7 @@
     return lax.dot_general(a, b, (((0,), (0,)), ((), ())), preferred_element_type=f32)
 
 
-def call(kernel, out_shape, vmem=60, flops=0, moved=0, **kw):
+def call(kernel, vmem, out_shape, flops=0, moved=0, **kw):
     return pl.pallas_call(
         kernel,
         out_shape=out_shape,
@@ -93,19 +93,21 @@
         x = jnp.where((row & bit) > 0, pltpu.roll(x, bit, axis=1), x)
     for bit in (8, 16, 32, 64):
         x = jnp.concatenate([x, pltpu.roll(x, bit, axis=1)], axis=0)
-    for d in range(length // TQ):
+    tiles = length // TQ
+    for d in range(tiles):
         at = (d + 1) * TQ
-        tile_ref[d, 0:128, :] = x[:, at : at + TQ]
-        tile_ref[d, 128:256, :] = x[:, at - 128 : at - 128 + TQ]
+        tile_ref[tiles - 1 - d, 0:128, :] = x[:, at : at + TQ]
+        tile_ref[tiles - 1 - d, 128:256, :] = x[:, at - 128 : at - 128 + TQ]
+    tile_ref[tiles] = jnp.full((TQ, TQ), NEG, f32)
 
 
 def transposed(block):
     return block.astype(f32).T.astype(bf16)
 
 
-def pair(ref, index, at, size):
+def pair(ref, index, at, size, count=2):
     return jnp.concatenate(
-        [ref[2 * index, at : at + size, :], ref[2 * index + 1, at : at + size, :]], axis=1
+        [ref[count * index + k, at : at + size, :] for k in range(count)], axis=1
     )
 
 
@@ -116,35 +118,38 @@
     return recv_ref.shape[0] * recv_ref.shape[2] + total.astype(jnp.int32)
 
 
-def first_tile(qb, edge):
-    return jnp.where(qb * TQ >= edge, edge // TQ, 0)
+def first_chunk(qb, edge):
+    return jnp.where(qb * TQ >= edge, edge // (2 * TQ), 0)
 
 
 def attend_kernel(recv_ref, bucket_ref, tab_ref, ot_ref, otf_ref, lse_ref, kn_ref, tile_ref):
     blocks = recv_ref.shape[0]
     bias_tiles(bucket_ref, tab_ref, tile_ref)
     for c in range(blocks):
-        kn_ref[c // 2, (c % 2) * 128 : (c % 2) * 128 + 128, :] = transposed(
+        kn_ref[c // 4, (c % 4) * 128 : (c % 4) * 128 + 128, :] = transposed(
             recv_ref[c, QA : 2 * QA, :]
         )
     edge = boundary(recv_ref)
+    last = blocks // 2 - 1
 
     def one_query_tile(qb, carry):
         qt = pair(recv_ref, qb, 0, QA)
 
         def one_key_tile(i, state):
             top, total, acc = state
-            kb = qb - i
-            s = nn(kn_ref[kb], qt) + tile_ref[i]
+            kc = qb // 2 - i
+            bias = tile_ref[pl.ds(last - qb + 2 * kc, 2)].reshape(2 * TQ, TQ)
+            s = nn(kn_ref[kc], qt) + bias
             new_top = jnp.maximum(top, jnp.max(s, axis=0, keepdims=True))
             p = jnp.exp(s - new_top)
             factor = jnp.exp(top - new_top)
             total = total * factor + jnp.sum(p, axis=0, keepdims=True)
-            acc = acc * factor + nn(pair(recv_ref, kb, 2 * QA, HEAD_DIM), p.astype(bf16))
+            acc = acc * factor + nn(pair(recv_ref, kc, 2 * QA, HEAD_DIM, 4), p.astype(bf16))
             return new_top, total, acc
 
         start = (jnp.full((1, TQ), NEG, f32), jnp.zeros((1, TQ), f32), jnp.zeros((HEAD_DIM, TQ), f32))
-        top, total, acc = lax.fori_loop(0, qb - first_tile(qb, edge) + 1, one_key_tile, start)
+        turns = qb // 2 - first_chunk(qb, edge) + 1
+        top, total, acc = lax.fori_loop(0, turns, one_key_tile, start)
         o = acc / total
         otf_ref[qb] = o
         lse_ref[qb] = top + jnp.log(total)
@@ -165,9 +170,9 @@
     tiles = blocks // 2
     bias_tiles(bucket_ref, tab_ref, tile_ref)
     for c in range(blocks):
-        at = (c % 2) * 128
-        kn_ref[c // 2, at : at + 128, :] = transposed(recv_ref[c, QA : 2 * QA, :])
-        vn_ref[c // 2, at : at + 128, :] = transposed(recv_ref[c, 2 * QA : 2 * QA + HEAD_DIM, :])
+        at = (c % 4) * 128
+        kn_ref[c // 4, at : at + 128, :] = transposed(recv_ref[c, QA : 2 * QA, :])
+        vn_ref[c // 4, at : at + 128, :] = transposed(recv_ref[c, 2 * QA : 2 * QA + HEAD_DIM, :])
     edge = boundary(recv_ref)
     dtile_ref[...] = jnp.zeros_like(dtile_ref)
     dk_ref[...] = jnp.zeros_like(dk_ref)
@@ -180,17 +185,18 @@
         delta = jnp.sum(gt.astype(f32) * otf_ref[qb], axis=0, keepdims=True)
 
         def one_key_tile(i, acc):
-            kb = qb - i
-            p = jnp.exp(nn(kn_ref[kb], qt) + tile_ref[i] - lse)
-            dp = nn(vn_ref[kb], gt)
+            kc = qb // 2 - i
+            place = pl.ds(tiles - 1 - qb + 2 * kc, 2)
+            p = jnp.exp(nn(kn_ref[kc], qt) + tile_ref[place].reshape(2 * TQ, TQ) - lse)
+            dp = nn(vn_ref[kc], gt)
             ds = (p * (dp - delta)).astype(bf16)
-            dtile_ref[i] += ds.astype(f32)
-            dv_ref[kb] += nt(gt, p.astype(bf16))
-            dk_ref[kb] += nt(qt[:HEAD_DIM], ds)
-            return acc + nn(pair(recv_ref, kb, QA, HEAD_DIM), ds)
+            dtile_ref[place] += ds.astype(f32).reshape(2, TQ, TQ)
+            dv_ref[kc] += nt(gt, p.astype(bf16))
+            dk_ref[kc] += nt(qt[:HEAD_DIM], ds)
+            return acc + nn(pair(recv_ref, kc, QA, HEAD_DIM, 4), ds)
 
         acc = lax.fori_loop(
-            0, qb - first_tile(qb, edge) + 1, one_key_tile, jnp.zeros((HEAD_DIM, TQ), f32)
+            0, qb // 2 - first_chunk(qb, edge) + 1, one_key_tile, jnp.zeros((HEAD_DIM, TQ), f32)
         )
         low = (acc * SCALE).astype(bf16)
         out_ref[2 * qb, 0:HEAD_DIM, :] = low[:, :128]
@@ -198,15 +204,14 @@
         return carry
 
     lax.fori_loop(0, tiles, one_query_tile, 0)
-    for kb in range(tiles):
+    for c in range(blocks):
         for ref, at in ((dk_ref, HEAD_DIM), (dv_ref, 2 * HEAD_DIM)):
-            low = ref[kb].astype(bf16)
-            out_ref[2 * kb, at : at + HEAD_DIM, :] = low[:, :128]
-            out_ref[2 * kb + 1, at : at + HEAD_DIM, :] = low[:, 128:]
+            lanes = slice((c % 4) * 128, (c % 4) * 128 + 128)
+            out_ref[c, at : at + HEAD_DIM, :] = ref[c // 4, :, lanes].astype(bf16)
     for c in range(blocks):
         flat_ref[:, c * 128 : (c + 1) * 128] = out_ref[c]
-    upper = jnp.concatenate([dtile_ref[d, 0:128, :] for d in range(tiles)], axis=1)
-    lower = jnp.concatenate([dtile_ref[d, 128:256, :] for d in range(tiles)], axis=1)
+    upper = jnp.concatenate([dtile_ref[tiles - 1 - d, 0:128, :] for d in range(tiles)], axis=1)
+    lower = jnp.concatenate([dtile_ref[tiles - 1 - d, 128:256, :] for d in range(tiles)], axis=1)
     pad = jnp.zeros((128, 128), f32)
     x = jnp.concatenate([pad, pad, upper], axis=1) + jnp.concatenate([pad, lower, pad], axis=1)
     wide = x.shape[1]
@@ -377,21 +382,40 @@
         out_ref[...] = nn(left_ref[...], act_ref[...]).astype(bf16)
 
 
-def pack_kernel(flat_ref, hid_ref, wt_ref, gain_ref, wo_ref, small_ref, bias_ref, out_ref):
+def pack_kernel(
+    flat_ref, hid_ref, wt_ref, gain_ref, wo_ref, small_ref, bias_ref, out_ref, grad_ref, sum_ref
+):
+    step = pl.program_id(0)
     width = hid_ref.shape[1]
-    grad = nn(flat_ref[...], hid_ref[...])
-    part = jnp.sum(grad * wt_ref[...].astype(f32), axis=0, keepdims=True) / gain_ref[...]
-    out_ref[0:192, :] = grad.astype(bf16)
+    part = nn(flat_ref[...], hid_ref[...])
     wo = wo_ref[0].astype(f32)
     for c in range(1, wo_ref.shape[0]):
         wo = wo + wo_ref[c].astype(f32)
-    out_ref[192:240, :] = wo.astype(bf16)
-    bias = jnp.concatenate([bias_ref[...], jnp.zeros((8, width - 128), f32)], axis=1)
-    row = lax.broadcasted_iota(jnp.int32, (8, width), 0)
-    first = jnp.where(
-        row == 0, jnp.broadcast_to(part, (8, width)), jnp.where(row == 1, small_ref[0:8, :], bias)
-    )
-    out_ref[240:256, :] = jnp.concatenate([first, small_ref[8:16, :]], axis=0).astype(bf16)
+
+    @pl.when(step == 0)
+    def _():
+        grad_ref[...] = part
+        sum_ref[...] = wo
+
+    @pl.when(step > 0)
+    def _():
+        grad_ref[...] += part
+        sum_ref[...] += wo
+
+    @pl.when(step == pl.num_programs(0) - 1)
+    def _():
+        grad = grad_ref[...]
+        gain = jnp.sum(grad * wt_ref[...].astype(f32), axis=0, keepdims=True) / gain_ref[...]
+        out_ref[0:192, :] = grad.astype(bf16)
+        out_ref[192:240, :] = sum_ref[...].astype(bf16)
+        bias = jnp.concatenate([bias_ref[...], jnp.zeros((8, width - 128), f32)], axis=1)
+        row = lax.broadcasted_iota(jnp.int32, (8, width), 0)
+        first = jnp.where(
+            row == 0,
+            jnp.broadcast_to(gain, (8, width)),
+            jnp.where(row == 1, small_ref[0:8, :], bias),
+        )
+        out_ref[240:256, :] = jnp.concatenate([first, small_ref[8:16, :]], axis=0).astype(bf16)
 
 
 def tokens_kernel(recv_ref, tok_ref, gain_ref, rgrad_ref, wq_ref, wk_ref, wv_ref, out_ref):
@@ -410,20 +434,36 @@
     out_ref[...] = rgrad_ref[...] + inverse * (scaled - normed * average)
 
 
+def widen_kernel(in_ref, up_ref, down_ref):
+    units = up_ref.shape[2]
+    up_ref[:, 0, :] = in_ref[:, 0:units].astype(f32)
+    down_ref[:, 0, :] = in_ref[:, units:].astype(f32)
+
+
+def ring_rows(piece):
+    rows, width = piece.shape
+    shape = (4, 4, 16, width) if rows == 256 else (2, 4, 16, width)
+    return piece.reshape(shape)
+
+
 def unpack_kernel(where_ref, *refs):
-    pieces, (q_ref, k_ref, v_ref, wo_ref, tail_ref, bias_ref, all_ref) = refs[:20], refs[20:]
+    pieces, (q_ref, k_ref, v_ref, wo_ref, tail_ref, bias_ref, all_ref, sems) = refs[:20], refs[20:]
     step = pl.program_id(0)
     x, y, z, core = where_ref[0], where_ref[1], where_ref[2], where_ref[3]
 
     @pl.when(step == 0)
     def _():
+        copies = []
         for k in range(4):
-            own, ahead, far_one, far_two, behind = pieces[5 * k : 5 * k + 5]
-            full = all_ref.shape[3:]
-            for d, ref in ((0, own), (1, ahead), (3, behind)):
-                all_ref[k // 2, k % 2, d] = ref[...].reshape(full)
-            all_ref[k // 2, k % 2, 2, 0:2] = far_one[...].reshape(2, *full[1:])
-            all_ref[k // 2, k % 2, 2, 2:4] = far_two[...].reshape(2, *full[1:])
+            slot = all_ref.at[k // 2, k % 2]
+            places = [slot.at[0], slot.at[1], slot.at[2, 0:2], slot.at[2, 2:4], slot.at[3]]
+            for j, place in enumerate(places):
+                n = 5 * k + j
+                copies.append(pltpu.make_async_copy(pieces[n], place, sems.at[n]))
+        for copy in copies:
+            copy.start()
+        for copy in copies:
+            copy.wait()
 
     def rows(c, group):
         exp, half = group // 2, group % 2
@@ -493,16 +533,20 @@
     width = share.shape[1]
     along_z = gather_near("exp", 2, n_exp, share)
     quarter = sds((64, width), bf16)
-    first, second = call(split_kernel, (quarter, quarter), vmem=8)(*along_z)
+    first, second = call(split_kernel, 8, (quarter, quarter))(*along_z)
     plane = gather_near("ctx", 1, n_ctx, first) + gather_near("ctx", 4, n_ctx, second)
     side = sds((256, width), bf16)
-    return call(join_kernel, (side, side), vmem=8)(*plane)
-
-
-def gather_far(first, second, n_ctx, n_exp):
+    return call(join_kernel, 8, (side, side))(*plane)
+
+
+def gather_far(first, second, n_ctx, n_exp, done):
     own = gather_ring("ctx", 4, n_ctx, first) + gather_ring("ctx", 1, n_ctx, second)
+    own[0], own[5], tokens_grad = lax.optimization_barrier((own[0], own[5], done[0]))
+    tied = lax.optimization_barrier((own[2], own[3], own[7], own[8], *done[1:]))
+    own[2], own[3], own[7], own[8] = tied[:4]
     pairs = [(i, i ^ 1) for i in range(n_exp)]
-    return own + [lax.ppermute(piece, "exp", pairs) for piece in own]
+    other = [lax.ppermute(piece, "exp", pairs) for piece in own]
+    return own + other, (tokens_grad, *tied[4:])
 
 
 def on_device(
@@ -529,6 +573,7 @@
     x = tokens[0]
     qkv, hidden = call(
         project_kernel,
+        60,
         (sds((n_ctx, 2 * QA + HEAD_DIM, rows), bf16), sds((rows, width), bf16)),
         flops=6 * rows * width * width,
         moved=4 * MB,
@@ -548,12 +593,16 @@
     tiles = length // TQ
     ot, otf, lse = call(
         attend_kernel,
+        60,
         (
             sds((n_ctx, HEAD_DIM, rows), bf16),
             sds((tiles, HEAD_DIM, TQ), f32),
             sds((tiles, 1, TQ), f32),
         ),
-        scratch_shapes=[pltpu.VMEM((tiles, TQ, QA), bf16), pltpu.VMEM((tiles, TQ, TQ), f32)],
+        scratch_shapes=[
+            pltpu.VMEM((tiles // 2, 2 * TQ, QA), bf16),
+            pltpu.VMEM((tiles + 1, TQ, TQ), f32),
+        ],
         flops=8 * 10**9,
         moved=10 * MB,
     )(qkv, bucket_row, tab)
@@ -563,6 +612,7 @@
     grads_in = out_grad[0]
     send, residual, gates, hidden_two = call(
         route_kernel,
+        60,
         (
             sds((slots, 2 * width), bf16),
             sds((rows, width), f32),
@@ -579,6 +629,7 @@
     whole = lambda shape: pl.BlockSpec(shape, lambda i: (0, 0))
     result, pre, act = call(
         expert_kernel,
+        60,
         (
             sds((slots, 2 * width), bf16),
             sds((slots, hidden_units), bf16),
@@ -602,6 +653,7 @@
     returned = lax.all_to_all(result, "exp", split_axis=0, concat_axis=0, tiled=True)
     weight_grads = call(
         expert_grad_kernel,
+        60,
         sds((width, 2 * hidden_units), bf16),
         grid=(2 * steps,),
         in_specs=[
@@ -618,6 +670,7 @@
 
     layer_out, residual_grad, gt, wo_grad, small = call(
         combine_kernel,
+        60,
         (
             sds((rows, width), bf16),
             sds((rows, width), f32),
@@ -640,18 +693,19 @@
 
     dqkv, flat, bias_grad = call(
         attend_back_kernel,
+        60,
         (
             sds((n_ctx, 3 * HEAD_DIM, rows), bf16),
             sds((3 * HEAD_DIM, length), bf16),
             sds((8, 128), f32),
         ),
         scratch_shapes=[
-            pltpu.VMEM((tiles, TQ, QA), bf16),
-            pltpu.VMEM((tiles, TQ, HEAD_DIM), bf16),
-            pltpu.VMEM((tiles, TQ, TQ), f32),
-            pltpu.VMEM((tiles, TQ, TQ), f32),
-            pltpu.VMEM((tiles, HEAD_DIM, TQ), f32),
-            pltpu.VMEM((tiles, HEAD_DIM, TQ), f32),
+            pltpu.VMEM((tiles // 2, 2 * TQ, QA), bf16),
+            pltpu.VMEM((tiles // 2, 2 * TQ, HEAD_DIM), bf16),
+            pltpu.VMEM((tiles + 1, TQ, TQ), f32),
+            pltpu.VMEM((tiles + 1, TQ, TQ), f32),
+            pltpu.VMEM((tiles // 2, HEAD_DIM, 2 * TQ), f32),
+            pltpu.VMEM((tiles // 2, HEAD_DIM, 2 * TQ), f32),
         ],
         flops=20 * 10**9,
         moved=20 * MB,
@@ -659,7 +713,23 @@
 
     packed = call(
         pack_kernel,
+        60,
         sds((ROWS, width), bf16),
+        grid=(4,),
+        in_specs=[
+            pl.BlockSpec((3 * HEAD_DIM, length // 4), lambda i: (0, i)),
+            pl.BlockSpec((length // 4, width), lambda i: (i, 0)),
+            whole((3 * HEAD_DIM, width)),
+            whole((1, width)),
+            pl.BlockSpec((n_ctx // 4, width // n_ctx, width), lambda i: (i, 0, 0)),
+            whole((16, width)),
+            whole((8, 128)),
+        ],
+        out_specs=whole((ROWS, width)),
+        scratch_shapes=[
+            pltpu.VMEM((3 * HEAD_DIM, width), f32),
+            pltpu.VMEM((width // n_ctx, width), f32),
+        ],
         flops=6 * length * width * HEAD_DIM,
         moved=6 * MB,
     )(flat, hidden_all, own_weights, gain_one, wo_parts, small, bias_grad)
@@ -669,15 +739,28 @@
     parts, dqkv = lax.optimization_barrier((parts, dqkv))
     back = lax.all_to_all(dqkv, "ctx", split_axis=0, concat_axis=0, tiled=True)
     share = jnp.sum(parts.astype(f32), axis=0).astype(bf16)
+    first, second = gather_near_all(share, n_ctx, n_exp)
+    first, second, back = lax.optimization_barrier((first, second, back))
     tokens_grad = call(
         tokens_kernel,
+        60,
         sds((rows, width), f32),
         flops=6 * rows * width * width,
         moved=6 * MB,
     )(back, x, gain_one, residual_grad, query_weight, key_weight, value_weight)
-    first, second = gather_near_all(share, n_ctx, n_exp)
-    first, second, tokens_grad = lax.optimization_barrier((first, second, tokens_grad))
-    everything = gather_far(first, second, n_ctx, n_exp)
+    own_rows = sds((summed.shape[0], 1, hidden_units), f32)
+    ups, downs = call(
+        widen_kernel,
+        60,
+        (own_rows, own_rows),
+        grid=(summed.shape[0] // 16,),
+        in_specs=[pl.BlockSpec((16, 2 * hidden_units), lambda i: (i, 0))],
+        out_specs=[pl.BlockSpec((16, 1, hidden_units), lambda i: (i, 0, 0))] * 2,
+        moved=2 * MB,
+    )(summed)
+    everything, (tokens_grad, ups, downs) = gather_far(
+        first, second, n_ctx, n_exp, (tokens_grad, ups, downs)
+    )
 
     full = sds((width, width), f32)
     column = pl.BlockSpec((width, 128), lambda i, w: (0, i))
@@ -685,6 +768,7 @@
     where = jnp.stack([head % 4, head // 4, exp // 2, exp % 2]).astype(jnp.int32)
     query_grad, key_grad, value_grad, output_grad, tails, bias_rows = call(
         unpack_kernel,
+        60,
         (
             full,
             full,
@@ -696,7 +780,7 @@
         grid_spec=pltpu.PrefetchScalarGridSpec(
             num_scalar_prefetch=1,
             grid=(HEADS // 2,),
-            in_specs=[pl.BlockSpec(piece.shape, lambda i, w: (0, 0)) for piece in everything],
+            in_specs=[pl.BlockSpec(memory_space=pl.ANY) for _ in everything],
             out_specs=[
                 column,
                 column,
@@ -705,11 +789,13 @@
                 pl.BlockSpec((16, width), lambda i, w: (0, 0)),
                 pl.BlockSpec((1, 16, 128), lambda i, w: (i, 0, 0)),
             ],
-            scratch_shapes=[pltpu.VMEM((2, 2, 4, 4, 4, 16, width), bf16)],
+            scratch_shapes=[
+                pltpu.VMEM((2, 2, 4, 4, 4, 16, width), bf16),
+                pltpu.SemaphoreType.DMA((20,)),
+            ],
         ),
-        vmem=40,
         moved=16 * MB,
-    )(where, *everything)
+    )(where, *[ring_rows(piece) for piece in everything])
     table_grad = bias_rows.reshape(HEADS, 8, 128)[:, 2, : bias_table.shape[0]].T
     return (
         layer_out[None],
@@ -722,8 +808,8 @@
         table_grad,
         tails[1],
         tails[8:].T,
-        summed[:, :hidden_units].astype(f32)[:, None],
-        summed[:, hidden_units:].astype(f32)[:, None],
+        ups,
+        downs,
     )
 
 

time: 296 us -> 289 us (0.976)
  local copies, waits for them, and re-layouts: 25.7 us -> 15.9 us
  Pallas kernels: 81.6 us -> 85.1 us
    unnamed x57 -> x61, local copies, waits for them, and re-layouts: 19.6 us -> 7.48 us
    ppermute x17, starting transfers between devices: 15.1 us -> 24.8 us  [ring(): return lax.ppermute(block, axis, [(i, to(i)) for i in range(size)])]
    ppermute x10, starting transfers between devices: 15.9 us -> 7.5 us  [gather_far(): other = [lax.ppermute(piece, 'exp', pairs) for piece in own]]
    pallas_call x12 -> x13, Pallas kernels: 81.6 us -> 85.1 us  [the longest x1 14.4 us: on_device(): call(attend_back_kernel, 60, (sds((n_ctx, 3 * HEAD_DIM, rows), bf16), sds...]
  transfers between devices with their start and end apart: 36 -> 36, of which waited for: 17 -> 16; matrix products, arithmetic and copies ran while one was open for 3% -> 3% of each run, Pallas kernels for 28% -> 27%
where the time goes in v3:
time: 289 us; the launch traced here: 288 us
  Pallas kernels  85.1 us (29%)
  waiting for transfers between devices  63.1 us (22%)
  starting transfers between devices  62 us (21%)
  blocking collectives  44 us (15%)
  local copies, waits for them, and re-layouts  15.9 us (6%)
  between operations  14.1 us (5%)
  other arithmetic  3.97 us (1%)
    all_to_all x1, blocking collectives, on_device(): lax.all_to_all(send, 'exp', split_axis=0, concat_axis=0, tiled=True)  28.1 us
    ppermute x17, starting transfers between devices, ring(): return lax.ppermute(block, axis, [(i, to(i)) for i in range(size)])  24.8 us
    ppermute x17, waiting for transfers between devices, ring(): return lax.ppermute(block, axis, [(i, to(i)) for i in range(size)])  23 us
    all_to_all x1, blocking collectives, on_device(): lax.all_to_all(packed.reshape(n_exp, ROWS // n_exp, width), 'exp', split_...  15.9 us
    all_to_all x1, waiting for transfers between devices, on_device(): qkv = lax.all_to_all(qkv, 'ctx', split_axis=0, concat_axis=0, tiled=True)  15.1 us
    pallas_call x1, Pallas kernels, on_device(): call(attend_back_kernel, 60, (sds((n_ctx, 3 * HEAD_DIM, rows), bf16), sds...  14.4 us
    pallas_call x1, Pallas kernels, on_device(): call(expert_grad_kernel, 60, sds((width, 2 * hidden_units), bf16), grid=(...  13.1 us
    pallas_call x1, Pallas kernels, on_device(): call(expert_kernel, 60, (sds((slots, 2 * width), bf16), sds((slots, hidde...  12.4 us
  transfers between devices with their start and end apart: 36, of which 16 were waited for; matrix products, arithmetic and copies ran while one was open for 3% of the time, Pallas kernels for 27%

profile of v3, /device:TPU:1, one launch (start us, length us, event | category | flops | bytes accessed | tf_op | source)
XLA Modules:
  0.0 288.2 jit_solution(17114286024430510186)
XLA Ops:
  9.8 3.8 %shard_map.238 = (bf16[16,224,128]{2,1,0:T(8,128)(2,1)}, bf16[128,768]{1,0:T(8,128)(2,1)}) custom-call(bf16[128,768]{1,0:T(8,128)(2,1)} %bitcast.65, f32[1,768]{1,0:T(1,128)} %reshape.106.gain_ref, s32[1,128]{1,0:T(1,128)} %seg_ref.1, bf16[768,768]{1,0:T(8,128)(2,1)} %wq_ref.3, bf16[768,768]{1,0:T(8,128)(2,1)} %wk_ref.3, bf16[768,768]{1,0:T(8,128)(2,1)} %wv_ref.3), custom_call_target="tpu_custom_call" | custom-call | flops 452984832 | bytes 4194304 | tf_op jit(solution)/shard_map/pallas_call | solution.py:574
  13.6 7.6 %all-to-all-start = ((bf16[16,224,128]{2,1,0:T(8,128)(2,1)}), bf16[16,224,128]{2,1,0:T(8,128)(2,1)S(1)}, u32[]{:S(2)}, u32[]{:S(2)}) async-start(bf16[16,224,128]{2,1,0:T(8,128)(2,1)} %get-tuple-element.65), calls=%async_computation | async-start | bytes 1835008 | tf_op jit(solution)/shard_map/all_to_all | solution.py:581
  25.4 15.1 %all-to-all-done.recv_ref = bf16[16,224,128]{2,1,0:T(8,128)(2,1)S(1)} async-done(((bf16[16,224,128]{2,1,0:T(8,128)(2,1)}), bf16[16,224,128]{2,1,0:T(8,128)(2,1)S(1)}, u32[]{:S(2)}, u32[]{:S(2)}) %all-to-all-start) | async-done | bytes 917536 | tf_op jit(solution)/shard_map/all_to_all | solution.py:581
  41.5 11.5 %shard_map.239 = (bf16[16,64,128]{2,1,0:T(8,128)(2,1)}, f32[8,64,256]{2,1,0:T(8,128)}, f32[8,1,256]{2,1,0:T(1,128)}) custom-call(bf16[16,224,128]{2,1,0:T(8,128)(2,1)} %copy-done.5, s32[1,2048]{1,0:T(1,128)} %bitcast.90, f32[32,1]{1,0:T(8,128)} %pad_dynamic-slice_fusion.tab_ref), custom_call_target="tpu_custom_call" | custom-call | flops 8000000000 | bytes 10485760 | tf_op jit(solution)/shard_map/pallas_call | solution.py:594
  58.7 8.1 %all-to-all-done.1.ot_ref = bf16[16,64,128]{2,1,0:T(8,128)(2,1)S(1)} async-done(((bf16[16,64,128]{2,1,0:T(8,128)(2,1)}), bf16[16,64,128]{2,1,0:T(8,128)(2,1)S(1)}, u32[]{:S(2)}, u32[]{:S(2)}) %all-to-all-start.1) | async-done | bytes 262176 | tf_op jit(solution)/shard_map/all_to_all | solution.py:609
  67.5 3.7 %shard_map.240 = (bf16[320,1536]{1,0:T(8,128)(2,1)}, f32[128,768]{1,0:T(8,128)}, f32[128,256]{1,0:T(8,128)}, bf16[128,768]{1,0:T(8,128)(2,1)}) custom-call(bf16[16,64,128]{2,1,0:T(8,128)(2,1)} %copy-done.14, bf16[128,768]{1,0:T(8,128)(2,1)} %bitcast.66, bf16[768,768]{1,0:T(8,128)(2,1)} %wo_ref.3, f32[1,768]{1,0:T(1,128)} %reshape.108.gain_ref, ...), custom_call_target="tpu_custom_call" | custom-call | flops 1000000000 | bytes 4194304 | tf_op jit(solution)/shard_map/pallas_call | solution.py:613
  71.2 28.1 %all_to_all.53 = bf16[8,40,1536]{2,1,0:T(8,128)(2,1)} all-to-all(bf16[8,40,1536]{2,1,0:T(8,128)(2,1)} %bitcast.60), channel_id=1, replica_groups=mesh['ctx'=16,'exp'=8] {'exp'}, dimensions={0} | all-to-all | bytes 1966080 | tf_op jit(solution)/shard_map/all_to_all | solution.py:625
  99.4 12.4 %shard_map.241 = (bf16[320,1536]{1,0:T(8,128)(2,1)}, bf16[320,3072]{1,0:T(8,128)(2,1)}, bf16[320,3072]{1,0:T(8,128)(2,1)}) custom-call(bf16[320,1536]{1,0:T(8,128)(2,1)} %bitcast.55, bf16[768,6144]{1,0:T(8,128)(2,1)} %all-gather.3.cloned.1.call-done.up_ref.down_ref, bf16[768,6144]{1,0:T(8,128)(2,1)} %all-gather.3.cloned.1.call-done.up_ref.down_ref), custom_call_target="tpu_custom_call" | custom-call | flops 6039797760 | bytes 16777216 | tf_op jit(solution)/shard_map/pallas_call | solution.py:630
  111.7 4.6 %all-to-all-start.3 = ((bf16[8,40,1536]{2,1,0:T(8,128)(2,1)}), bf16[8,40,1536]{2,1,0:T(8,128)(2,1)S(1)}, u32[]{:S(2)}, u32[]{:S(2)}) async-start(bf16[8,40,1536]{2,1,0:T(8,128)(2,1)} %bitcast.59), calls=%async_computation.3 | async-start | bytes 1966080 | tf_op jit(solution)/shard_map/all_to_all | solution.py:653
  117.0 13.1 %shard_map.242 = bf16[768,6144]{1,0:T(8,128)(2,1)} custom-call(bf16[320,1536]{1,0:T(8,128)(2,1)} %bitcast.56, bf16[320,3072]{1,0:T(8,128)(2,1)} %get-tuple-element.70.pre_ref, bf16[320,3072]{1,0:T(8,128)(2,1)} %get-tuple-element.71.act_ref), custom_call_target="tpu_custom_call" | custom-call | flops 3019898880 | bytes 16777216 | tf_op jit(solution)/shard_map/pallas_call | solution.py:654
  131.7 5.2 %shard_map.243 = (bf16[128,768]{1,0:T(8,128)(2,1)}, f32[128,768]{1,0:T(8,128)}, bf16[16,64,128]{2,1,0:T(8,128)(2,1)}, bf16[768,768]{1,0:T(8,128)(2,1)}, f32[16,768]{1,0:T(8,128)}) custom-call(bf16[320,1536]{1,0:T(8,128)(2,1)} %bitcast.58, f32[128,768]{1,0:T(8,128)} %get-tuple-element.73.res_ref, bf16[128,768]{1,0:T(8,128)(2,1)} %bitcast.89, ...), custom_call_target="tpu_custom_call" | custom-call | flops 1000000000 | bytes 6291456 | tf_op jit(solution)/shard_map/pallas_call | solution.py:671
  136.9 5.2 %all-to-all-start.4 = ((bf16[16,64,128]{2,1,0:T(8,128)(2,1)}), bf16[16,64,128]{2,1,0:T(8,128)(2,1)S(1)}, u32[]{:S(2)}, u32[]{:S(2)}) async-start(bf16[16,64,128]{2,1,0:T(8,128)(2,1)} %get-tuple-element.79), calls=%async_computation.4 | async-start | bytes 524288 | tf_op jit(solution)/shard_map/all_to_all | solution.py:687
  142.2 8.4 %all-gather.5.cloned.1.call-done.hid_ref = bf16[2048,768]{1,0:T(8,128)(2,1)} async-done(((bf16[128,768]{1,0:T(8,128)(2,1)}), bf16[2048,768]{1,0:T(8,128)(2,1)}) %all-gather.5.cloned.1.call-update) | async-done | bytes 3145744 | tf_op jit(solution)/shard_map/all_gather | solution.py:591
  152.4 3.9 %all-to-all-start.5 = ((bf16[16,48,768]{2,1,0:T(8,128)(2,1)}), bf16[16,48,768]{2,1,0:T(8,128)(2,1)S(1)}, u32[]{:S(2)}, u32[]{:S(2)}) async-start(bf16[16,48,768]{2,1,0:T(8,128)(2,1)} %bitcast.16), calls=%async_computation.5 | async-start | bytes 2359296 | tf_op jit(solution)/shard_map/all_to_all | solution.py:690
  156.3 14.4 %shard_map.244 = (bf16[16,192,128]{2,1,0:T(8,128)(2,1)}, bf16[192,2048]{1,0:T(8,128)(2,1)}, f32[8,128]{1,0:T(8,128)}) custom-call(bf16[16,224,128]{2,1,0:T(8,128)(2,1)} %copy-done.5, bf16[16,64,128]{2,1,0:T(8,128)(2,1)} %copy-done.15, f32[8,64,256]{2,1,0:T(8,128)} %get-tuple-element.81.otf_ref, f32[8,1,256]{2,1,0:T(1,128)} %get-tuple-element.82.lse_ref, ...), custom_call_target="tpu_custom_call" | custom-call | flops 20000000000 | bytes 20971520 | tf_op jit(solution)/shard_map/pallas_call | solution.py:694
  170.7 5.7 %all-to-all-done.5.wo_ref = bf16[16,48,768]{2,1,0:T(8,128)(2,1)S(1)} async-done(((bf16[16,48,768]{2,1,0:T(8,128)(2,1)}), bf16[16,48,768]{2,1,0:T(8,128)(2,1)S(1)}, u32[]{:S(2)}, u32[]{:S(2)}) %all-to-all-start.5) | async-done | bytes 1179680 | tf_op jit(solution)/shard_map/all_to_all | solution.py:690
  177.4 5.1 %shard_map.245 = bf16[256,768]{1,0:T(8,128)(2,1)} custom-call(bf16[192,2048]{1,0:T(8,128)(2,1)} %get-tuple-element.83.flat_ref, bf16[2048,768]{1,0:T(8,128)(2,1)} %all-gather.5.cloned.1.call-done.hid_ref, bf16[192,768]{1,0:T(8,128)(2,1)} %pad_maximum_fusion.1.wt_ref, f32[1,768]{1,0:T(1,128)} %reshape.106.gain_ref, bf16[16,48,768]{2,1,0:T(8,128)(2,1)} %copy-done.2, ...), custom_call_target="tpu_custom_call" | custom-call | flops 603979776 | bytes 6291456 | tf_op jit(solution)/shard_map/pallas_call | solution.py:714
  182.6 15.9 %all_to_all.54 = bf16[8,32,768]{2,1,0:T(8,128)(2,1)S(1)} all-to-all(bf16[8,32,768]{2,1,0:T(8,128)(2,1)} %bitcast.57), channel_id=1, replica_groups=mesh['ctx'=16,'exp'=8] {'exp'}, dimensions={0} | all-to-all | bytes 786432 | tf_op jit(solution)/shard_map/all_to_all | solution.py:736
  198.4 4.7 %all-to-all-start.7 = ((bf16[16,192,128]{2,1,0:T(8,128)(2,1)}), bf16[16,192,128]{2,1,0:T(8,128)(2,1)S(1)}, u32[]{:S(2)}, u32[]{:S(2)}) async-start(bf16[16,192,128]{2,1,0:T(8,128)(2,1)} %get-tuple-element.95), calls=%async_computation.7 | async-start | bytes 1572864 | tf_op jit(solution)/shard_map/all_to_all | solution.py:740
  217.5 6.0 %collective-permute-done.3.refs_1_ = bf16[64,768]{1,0:T(8,128)(2,1)S(1)} collective-permute-done((bf16[64,768]{1,0:T(8,128)(2,1)S(1)}, bf16[64,768]{1,0:T(8,128)(2,1)S(1)}, u32[]{:S(2)}, u32[]{:S(2)}) %collective-permute-start.3) | collective-permute-done | bytes 98336 | tf_op jit(solution)/shard_map/ppermute | solution.py:501
  233.8 4.5 %shard_map.248 = f32[128,768]{1,0:T(8,128)} custom-call(bf16[16,192,128]{2,1,0:T(8,128)(2,1)} %copy-done.3, bf16[128,768]{1,0:T(8,128)(2,1)} %bitcast.67, f32[1,768]{1,0:T(1,128)} %reshape.106.gain_ref, f32[128,768]{1,0:T(8,128)} %get-tuple-element.99.rgrad_ref, bf16[768,768]{1,0:T(8,128)(2,1)} %wq_ref.3, bf16[768,768]{1,0:T(8,128)(2,1)} %wk_ref.3, ...), custom_call_target="tpu_custom_call" | custom-call | flops 452984832 | bytes 6291456 | tf_op jit(solution)/shard_map/pallas_call | solution.py:744
  246.8 6.5 %collective-permute-done.10 = bf16[128,768]{1,0:T(8,128)(2,1)S(1)} collective-permute-done((bf16[128,768]{1,0:T(8,128)(2,1)S(1)}, bf16[128,768]{1,0:T(8,128)(2,1)S(1)}, u32[]{:S(2)}, u32[]{:S(2)}) %collective-permute-start.10) | collective-permute-done | bytes 196640 | tf_op jit(solution)/shard_map/ppermute | solution.py:501
  256.3 5.4 %collective-permute-done.16 = bf16[128,768]{1,0:T(8,128)(2,1)S(1)} collective-permute-done((bf16[128,768]{1,0:T(8,128)(2,1)S(1)}, bf16[128,768]{1,0:T(8,128)(2,1)S(1)}, u32[]{:S(2)}, u32[]{:S(2)}) %collective-permute-start.16) | collective-permute-done | bytes 196640 | tf_op jit(solution)/shard_map/ppermute | solution.py:501
  269.1 8.4 %shard_map.250 = (f32[768,768]{1,0:T(8,128)}, f32[768,768]{1,0:T(8,128)}, f32[768,768]{1,0:T(8,128)}, f32[768,768]{1,0:T(8,128)}, f32[16,768]{1,0:T(8,128)}, /*index=5*/f32[6,16,128]{2,1,0:T(8,128)}) custom-call(s32[4]{0:T(128)} %pad_add_fusion.where_ref, bf16[4,4,16,768]{3,2,1,0:T(8,128)(2,1)} %bitcast.53, bf16[4,4,16,768]{3,2,1,0:T(8,128)(2,1)} %bitcast.61, ...), custom_call_target="tpu_custom_call" | custom-call | bytes 16777216 | tf_op jit(solution)/shard_map/pallas_call | solution.py:769
  (145 shorter events, 66.6 us)
Async XLA Ops:
  7.2 92.2 %all-gather.3.cloned.1.call-start = ((), (), s32[]{:S(2)}) async-start(), calls=%async_computation.9 | async-start | bytes 10027008 | tf_op jit(solution)/shard_map/all_gather | solution.py:571
  9.2 141.4 %all-gather.5.cloned.1.call-start = ((), (), s32[]{:S(2)}) async-start(), calls=%async_computation.10 | async-start | bytes 3342336 | tf_op jit(solution)/shard_map/all_gather | solution.py:591
  13.6 26.9 %all-to-all-start = ((bf16[16,224,128]{2,1,0:T(8,128)(2,1)}), bf16[16,224,128]{2,1,0:T(8,128)(2,1)S(1)}, u32[]{:S(2)}, u32[]{:S(2)}) async-start(bf16[16,224,128]{2,1,0:T(8,128)(2,1)} %get-tuple-element.65), calls=%async_computation | async-start | bytes 1835008 | tf_op jit(solution)/shard_map/all_to_all | solution.py:581
  53.0 13.8 %all-to-all-start.1 = ((bf16[16,64,128]{2,1,0:T(8,128)(2,1)}), bf16[16,64,128]{2,1,0:T(8,128)(2,1)S(1)}, u32[]{:S(2)}, u32[]{:S(2)}) async-start(bf16[16,64,128]{2,1,0:T(8,128)(2,1)} %get-tuple-element.67), calls=%async_computation.1 | async-start | bytes 524288 | tf_op jit(solution)/shard_map/all_to_all | solution.py:609
  111.7 19.0 %all-to-all-start.3 = ((bf16[8,40,1536]{2,1,0:T(8,128)(2,1)}), bf16[8,40,1536]{2,1,0:T(8,128)(2,1)S(1)}, u32[]{:S(2)}, u32[]{:S(2)}) async-start(bf16[8,40,1536]{2,1,0:T(8,128)(2,1)} %bitcast.59), calls=%async_computation.3 | async-start | bytes 1966080 | tf_op jit(solution)/shard_map/all_to_all | solution.py:653
  136.9 14.8 %all-to-all-start.4 = ((bf16[16,64,128]{2,1,0:T(8,128)(2,1)}), bf16[16,64,128]{2,1,0:T(8,128)(2,1)S(1)}, u32[]{:S(2)}, u32[]{:S(2)}) async-start(bf16[16,64,128]{2,1,0:T(8,128)(2,1)} %get-tuple-element.79), calls=%async_computation.4 | async-start | bytes 524288 | tf_op jit(solution)/shard_map/all_to_all | solution.py:687
  142.1 121.2 %reduce-scatter.2.cloned.1.call-start = ((), (), s32[]{:S(2)}) async-start(), calls=%async_computation.11 | async-start | bytes 10027008 | tf_op jit(solution)/shard_map/reduce_scatter | solution.py:689
  152.4 24.0 %all-to-all-start.5 = ((bf16[16,48,768]{2,1,0:T(8,128)(2,1)}), bf16[16,48,768]{2,1,0:T(8,128)(2,1)S(1)}, u32[]{:S(2)}, u32[]{:S(2)}) async-start(bf16[16,48,768]{2,1,0:T(8,128)(2,1)} %bitcast.16), calls=%async_computation.5 | async-start | bytes 2359296 | tf_op jit(solution)/shard_map/all_to_all | solution.py:690
  198.4 29.6 %all-to-all-start.7 = ((bf16[16,192,128]{2,1,0:T(8,128)(2,1)}), bf16[16,192,128]{2,1,0:T(8,128)(2,1)S(1)}, u32[]{:S(2)}, u32[]{:S(2)}) async-start(bf16[16,192,128]{2,1,0:T(8,128)(2,1)} %get-tuple-element.95), calls=%async_computation.7 | async-start | bytes 1572864 | tf_op jit(solution)/shard_map/all_to_all | solution.py:740
  208.9 14.6 %collective-permute-start.3 = (bf16[64,768]{1,0:T(8,128)(2,1)S(1)}, bf16[64,768]{1,0:T(8,128)(2,1)S(1)}, u32[]{:S(2)}, u32[]{:S(2)}) collective-permute-start(bf16[64,768]{1,0:T(8,128)(2,1)S(1)} %get-tuple-element.91.refs_0_), channel_id=1, source_target_pairs={{0,8},{8,16},{16,24},{24,0},{32,40},{40,48},{48,56},{56,32},{64,72... | collective-permute-start | bytes 294920 | tf_op jit(solution)/shard_map/ppermute | solution.py:501
  210.4 17.6 %collective-permute-start.4 = (bf16[64,768]{1,0:T(8,128)(2,1)S(1)}, bf16[64,768]{1,0:T(8,128)(2,1)S(1)}, u32[]{:S(2)}, u32[]{:S(2)}) collective-permute-start(bf16[64,768]{1,0:T(8,128)(2,1)S(1)} %get-tuple-element.91.refs_0_), channel_id=1, source_target_pairs={{0,16},{8,24},{16,0},{24,8},{32,48},{40,56},{48,32},{56,40},{64,80... | collective-permute-start | bytes 294920 | tf_op jit(solution)/shard_map/ppermute | solution.py:501
  212.8 15.2 %collective-permute-start.5 = (bf16[64,768]{1,0:T(8,128)(2,1)S(1)}, bf16[64,768]{1,0:T(8,128)(2,1)S(1)}, u32[]{:S(2)}, u32[]{:S(2)}) collective-permute-start(bf16[64,768]{1,0:T(8,128)(2,1)S(1)} %get-tuple-element.91.refs_0_), channel_id=1, source_target_pairs={{0,24},{8,0},{16,8},{24,16},{32,56},{40,32},{48,40},{56,48},{64,88... | collective-permute-start | bytes 294920 | tf_op jit(solution)/shard_map/ppermute | solution.py:501
  213.9 14.0 %collective-permute-start.6 = (bf16[64,768]{1,0:T(8,128)(2,1)S(1)}, bf16[64,768]{1,0:T(8,128)(2,1)S(1)}, u32[]{:S(2)}, u32[]{:S(2)}) collective-permute-start(bf16[64,768]{1,0:T(8,128)(2,1)S(1)} %get-tuple-element.92.refs_4_), channel_id=1, source_target_pairs={{0,32},{8,40},{16,48},{24,56},{32,64},{40,72},{48,80},{56,88},{64,... | collective-permute-start | bytes 294920 | tf_op jit(solution)/shard_map/ppermute | solution.py:501
  215.1 12.8 %collective-permute-start.7 = (bf16[64,768]{1,0:T(8,128)(2,1)S(1)}, bf16[64,768]{1,0:T(8,128)(2,1)S(1)}, u32[]{:S(2)}, u32[]{:S(2)}) collective-permute-start(bf16[64,768]{1,0:T(8,128)(2,1)S(1)} %get-tuple-element.92.refs_4_), channel_id=1, source_target_pairs={{0,64},{8,72},{16,80},{24,88},{32,96},{40,104},{48,112},{56,120},{... | collective-permute-start | bytes 294920 | tf_op jit(solution)/shard_map/ppermute | solution.py:501
  228.1 13.3 %collective-permute-start.9 = (bf16[256,768]{1,0:T(8,128)(2,1)S(1)}, bf16[256,768]{1,0:T(8,128)(2,1)S(1)}, u32[]{:S(2)}, u32[]{:S(2)}) collective-permute-start(bf16[256,768]{1,0:T(8,128)(2,1)S(1)} %get-tuple-element.101), channel_id=1, source_target_pairs={{0,32},{8,40},{16,48},{24,56},{32,64},{40,72},{48,80},{56,88},{64,... | collective-permute-start | bytes 1179656 | tf_op jit(solution)/shard_map/ppermute | solution.py:501
  228.9 12.5 %collective-permute-start.11 = (bf16[256,768]{1,0:T(8,128)(2,1)S(1)}, bf16[256,768]{1,0:T(8,128)(2,1)S(1)}, u32[]{:S(2)}, u32[]{:S(2)}) collective-permute-start(bf16[256,768]{1,0:T(8,128)(2,1)S(1)} %get-tuple-element.101), channel_id=1, source_target_pairs={{0,96},{8,104},{16,112},{24,120},{32,0},{40,8},{48,16},{56,24},{64... | collective-permute-start | bytes 1179656 | tf_op jit(solution)/shard_map/ppermute | solution.py:501
  231.1 13.1 %collective-permute-start.13 = (bf16[256,768]{1,0:T(8,128)(2,1)S(1)}, bf16[256,768]{1,0:T(8,128)(2,1)S(1)}, u32[]{:S(2)}, u32[]{:S(2)}) collective-permute-start(bf16[256,768]{1,0:T(8,128)(2,1)S(1)} %get-tuple-element.107), channel_id=1, source_target_pairs={{0,8},{8,16},{16,24},{24,0},{32,40},{40,48},{48,56},{56,32},{64,72... | collective-permute-start | bytes 1179656 | tf_op jit(solution)/shard_map/ppermute | solution.py:501
  232.0 13.3 %collective-permute-start.15 = (bf16[256,768]{1,0:T(8,128)(2,1)S(1)}, bf16[256,768]{1,0:T(8,128)(2,1)S(1)}, u32[]{:S(2)}, u32[]{:S(2)}) collective-permute-start(bf16[256,768]{1,0:T(8,128)(2,1)S(1)} %get-tuple-element.107), channel_id=1, source_target_pairs={{0,24},{8,0},{16,8},{24,16},{32,56},{40,32},{48,40},{56,48},{64,88... | collective-permute-start | bytes 1179656 | tf_op jit(solution)/shard_map/ppermute | solution.py:501
  241.4 12.0 %collective-permute-start.10 = (bf16[128,768]{1,0:T(8,128)(2,1)S(1)}, bf16[128,768]{1,0:T(8,128)(2,1)S(1)}, u32[]{:S(2)}, u32[]{:S(2)}) collective-permute-start(bf16[128,768]{1,0:T(8,128)(2,1)S(1)} %slice.32), channel_id=1, source_target_pairs={{0,32},{8,40},{16,48},{24,56},{32,64},{40,72},{48,80},{56,88},{64,... | collective-permute-start | bytes 589832 | tf_op jit(solution)/shard_map/ppermute | solution.py:501
  241.5 13.4 %collective-permute-start.12 = (bf16[128,768]{1,0:T(8,128)(2,1)S(1)}, bf16[128,768]{1,0:T(8,128)(2,1)}, u32[]{:S(2)}, u32[]{:S(2)}) collective-permute-start(bf16[128,768]{1,0:T(8,128)(2,1)S(1)} %slice.33), channel_id=1, source_target_pairs={{0,96},{8,104},{16,112},{24,120},{32,0},{40,8},{48,16},{56,24},{64... | collective-permute-start | bytes 589832 | tf_op jit(solution)/shard_map/ppermute | solution.py:501
  245.2 21.1 %collective-permute-start.22 = (bf16[256,768]{1,0:T(8,128)(2,1)S(1)}, bf16[256,768]{1,0:T(8,128)(2,1)S(1)}, u32[]{:S(2)}, u32[]{:S(2)}) collective-permute-start(bf16[256,768]{1,0:T(8,128)(2,1)S(1)} %get-tuple-element.107), channel_id=1, source_target_pairs={{0,1},{1,0},{2,3},{3,2},{4,5},{5,4},{6,7},{7,6},{8,9},{9,8},{10,11... | collective-permute-start | bytes 1179656 | tf_op jit(solution)/shard_map/ppermute | solution.py:548
  246.7 19.7 %collective-permute-start.18 = (bf16[256,768]{1,0:T(8,128)(2,1)S(1)}, bf16[256,768]{1,0:T(8,128)(2,1)S(1)}, u32[]{:S(2)}, u32[]{:S(2)}) collective-permute-start(bf16[256,768]{1,0:T(8,128)(2,1)S(1)} %collective-permute-done.9), channel_id=1, source_target_pairs={{0,1},{1,0},{2,3},{3,2},{4,5},{5,4},{6,7},{7,6},{8,9},{9,8},{10,11... | collective-permute-start | bytes 1179656 | tf_op jit(solution)/shard_map/ppermute | solution.py:548
  254.9 12.0 %collective-permute-start.21 = (bf16[256,768]{1,0:T(8,128)(2,1)S(1)}, bf16[256,768]{1,0:T(8,128)(2,1)S(1)}, u32[]{:S(2)}, u32[]{:S(2)}) collective-permute-start(bf16[256,768]{1,0:T(8,128)(2,1)S(1)} %collective-permute-done.11), channel_id=1, source_target_pairs={{0,1},{1,0},{2,3},{3,2},{4,5},{5,4},{6,7},{7,6},{8,9},{9,8},{10,11... | collective-permute-start | bytes 1179656 | tf_op jit(solution)/shard_map/ppermute | solution.py:548
  255.6 11.4 %collective-permute-start.23 = (bf16[256,768]{1,0:T(8,128)(2,1)S(1)}, bf16[256,768]{1,0:T(8,128)(2,1)}, u32[]{:S(2)}, u32[]{:S(2)}) collective-permute-start(bf16[256,768]{1,0:T(8,128)(2,1)S(1)} %collective-permute-done.13), channel_id=1, source_target_pairs={{0,1},{1,0},{2,3},{3,2},{4,5},{5,4},{6,7},{7,6},{8,9},{9,8},{10,11... | collective-permute-start | bytes 1179656 | tf_op jit(solution)/shard_map/ppermute | solution.py:548
  (39 other events, 297.0 us)
Sparse Core Ops, SparseCore 0:
  10.7 88.0 all-gather.2
  101.0 49.6 all-gather.4
  154.1 106.1 reduce-scatter.1

commit v4 on v3

--- a/solution.py
+++ b/solution.py
@@ -382,40 +382,21 @@
         out_ref[...] = nn(left_ref[...], act_ref[...]).astype(bf16)
 
 
-def pack_kernel(
-    flat_ref, hid_ref, wt_ref, gain_ref, wo_ref, small_ref, bias_ref, out_ref, grad_ref, sum_ref
-):
-    step = pl.program_id(0)
+def pack_kernel(flat_ref, hid_ref, wt_ref, gain_ref, wo_ref, small_ref, bias_ref, out_ref):
     width = hid_ref.shape[1]
-    part = nn(flat_ref[...], hid_ref[...])
+    grad = nn(flat_ref[...], hid_ref[...])
+    part = jnp.sum(grad * wt_ref[...].astype(f32), axis=0, keepdims=True) / gain_ref[...]
+    out_ref[0:192, :] = grad.astype(bf16)
     wo = wo_ref[0].astype(f32)
     for c in range(1, wo_ref.shape[0]):
         wo = wo + wo_ref[c].astype(f32)
-
-    @pl.when(step == 0)
-    def _():
-        grad_ref[...] = part
-        sum_ref[...] = wo
-
-    @pl.when(step > 0)
-    def _():
-        grad_ref[...] += part
-        sum_ref[...] += wo
-
-    @pl.when(step == pl.num_programs(0) - 1)
-    def _():
-        grad = grad_ref[...]
-        gain = jnp.sum(grad * wt_ref[...].astype(f32), axis=0, keepdims=True) / gain_ref[...]
-        out_ref[0:192, :] = grad.astype(bf16)
-        out_ref[192:240, :] = sum_ref[...].astype(bf16)
-        bias = jnp.concatenate([bias_ref[...], jnp.zeros((8, width - 128), f32)], axis=1)
-        row = lax.broadcasted_iota(jnp.int32, (8, width), 0)
-        first = jnp.where(
-            row == 0,
-            jnp.broadcast_to(gain, (8, width)),
-            jnp.where(row == 1, small_ref[0:8, :], bias),
-        )
-        out_ref[240:256, :] = jnp.concatenate([first, small_ref[8:16, :]], axis=0).astype(bf16)
+    out_ref[192:240, :] = wo.astype(bf16)
+    bias = jnp.concatenate([bias_ref[...], jnp.zeros((8, width - 128), f32)], axis=1)
+    row = lax.broadcasted_iota(jnp.int32, (8, width), 0)
+    first = jnp.where(
+        row == 0, jnp.broadcast_to(part, (8, width)), jnp.where(row == 1, small_ref[0:8, :], bias)
+    )
+    out_ref[240:256, :] = jnp.concatenate([first, small_ref[8:16, :]], axis=0).astype(bf16)
 
 
 def tokens_kernel(recv_ref, tok_ref, gain_ref, rgrad_ref, wq_ref, wk_ref, wv_ref, out_ref):
@@ -434,20 +415,18 @@
     out_ref[...] = rgrad_ref[...] + inverse * (scaled - normed * average)
 
 
-def widen_kernel(in_ref, up_ref, down_ref):
-    units = up_ref.shape[2]
-    up_ref[:, 0, :] = in_ref[:, 0:units].astype(f32)
-    down_ref[:, 0, :] = in_ref[:, units:].astype(f32)
-
-
 def ring_rows(piece):
     rows, width = piece.shape
     shape = (4, 4, 16, width) if rows == 256 else (2, 4, 16, width)
     return piece.reshape(shape)
 
 
-def unpack_kernel(where_ref, *refs):
-    pieces, (q_ref, k_ref, v_ref, wo_ref, tail_ref, bias_ref, all_ref, sems) = refs[:20], refs[20:]
+def unpack_kernel(where_ref, sum_ref, *refs):
+    pieces, (q_ref, k_ref, v_ref, wo_ref, gain_ref, router_ref, table_ref) = refs[:20], refs[20:27]
+    up_ref, down_ref, all_ref, sems = refs[27:]
+    units = up_ref.shape[2]
+    up_ref[:, 0, :] = sum_ref[:, 0:units].astype(f32)
+    down_ref[:, 0, :] = sum_ref[:, units:].astype(f32)
     step = pl.program_id(0)
     x, y, z, core = where_ref[0], where_ref[1], where_ref[2], where_ref[3]
 
@@ -478,19 +457,23 @@
     for ref, at in ((q_ref, 0), (k_ref, HEAD_DIM), (v_ref, 2 * HEAD_DIM)):
         both = [span(2 * step, at, at + HEAD_DIM), span(2 * step + 1, at, at + HEAD_DIM)]
         ref[...] = jnp.concatenate(both, axis=0).astype(f32).T
-    for k in (0, 1):
-        c = jnp.minimum(2 * step + k, 11)
-        bias_ref[0, 8 * k : 8 * k + 8, :] = rows(c, 15)[0:8, 0:128].astype(f32)
-    for k in (0, 1, 2):
-        c = jnp.minimum(3 * step + k, 15)
-        wo_ref[48 * k : 48 * k + 48, :] = span(c, 192, 240).astype(f32)
+    @pl.when(step < 4)
+    def _():
+        for k in range(4):
+            wo_ref[48 * k : 48 * k + 48, :] = span(4 * step + k, 192, 240).astype(f32)
 
     @pl.when(step == 0)
     def _():
-        total = rows(0, 15).astype(f32)
-        for c in range(1, 16):
-            total = total + rows(c, 15).astype(f32)
-        tail_ref[...] = total
+        tails = [rows(c, 15).astype(f32) for c in range(16)]
+        total = tails[0]
+        for part in tails[1:]:
+            total = total + part
+        gain_ref[...] = total[0:8]
+        router_ref[...] = jnp.concatenate([total, total], axis=0).T[:, 8:16]
+        table = jnp.concatenate(
+            [part[2:3, 0:128] for part in tails[:HEADS]] + [jnp.zeros((128 - HEADS, 128), f32)], axis=0
+        )
+        table_ref[...] = table.T[0 : table_ref.shape[0], 0:HEADS]
 
 
 def ring(axis, stride, size, block, distance):
@@ -541,12 +524,9 @@
 
 def gather_far(first, second, n_ctx, n_exp, done):
     own = gather_ring("ctx", 4, n_ctx, first) + gather_ring("ctx", 1, n_ctx, second)
-    own[0], own[5], tokens_grad = lax.optimization_barrier((own[0], own[5], done[0]))
-    tied = lax.optimization_barrier((own[2], own[3], own[7], own[8], *done[1:]))
-    own[2], own[3], own[7], own[8] = tied[:4]
+    own[0], own[5], done = lax.optimization_barrier((own[0], own[5], done))
     pairs = [(i, i ^ 1) for i in range(n_exp)]
-    other = [lax.ppermute(piece, "exp", pairs) for piece in own]
-    return own + other, (tokens_grad, *tied[4:])
+    return own + [lax.ppermute(piece, "exp", pairs) for piece in own], done
 
 
 def on_device(
@@ -715,21 +695,6 @@
         pack_kernel,
         60,
         sds((ROWS, width), bf16),
-        grid=(4,),
-        in_specs=[
-            pl.BlockSpec((3 * HEAD_DIM, length // 4), lambda i: (0, i)),
-            pl.BlockSpec((length // 4, width), lambda i: (i, 0)),
-            whole((3 * HEAD_DIM, width)),
-            whole((1, width)),
-            pl.BlockSpec((n_ctx // 4, width // n_ctx, width), lambda i: (i, 0, 0)),
-            whole((16, width)),
-            whole((8, 128)),
-        ],
-        out_specs=whole((ROWS, width)),
-        scratch_shapes=[
-            pltpu.VMEM((3 * HEAD_DIM, width), f32),
-            pltpu.VMEM((width // n_ctx, width), f32),
-        ],
         flops=6 * length * width * HEAD_DIM,
         moved=6 * MB,
     )(flat, hidden_all, own_weights, gain_one, wo_parts, small, bias_grad)
@@ -748,46 +713,44 @@
         flops=6 * rows * width * width,
         moved=6 * MB,
     )(back, x, gain_one, residual_grad, query_weight, key_weight, value_weight)
-    own_rows = sds((summed.shape[0], 1, hidden_units), f32)
-    ups, downs = call(
-        widen_kernel,
-        60,
-        (own_rows, own_rows),
-        grid=(summed.shape[0] // 16,),
-        in_specs=[pl.BlockSpec((16, 2 * hidden_units), lambda i: (i, 0))],
-        out_specs=[pl.BlockSpec((16, 1, hidden_units), lambda i: (i, 0, 0))] * 2,
-        moved=2 * MB,
-    )(summed)
-    everything, (tokens_grad, ups, downs) = gather_far(
-        first, second, n_ctx, n_exp, (tokens_grad, ups, downs)
-    )
+    everything, tokens_grad = gather_far(first, second, n_ctx, n_exp, tokens_grad)
 
     full = sds((width, width), f32)
     column = pl.BlockSpec((width, 128), lambda i, w: (0, i))
     exp = lax.axis_index("exp")
     where = jnp.stack([head % 4, head // 4, exp // 2, exp % 2]).astype(jnp.int32)
-    query_grad, key_grad, value_grad, output_grad, tails, bias_rows = call(
+    own_rows = sds((summed.shape[0], 1, hidden_units), f32)
+    own_block = pl.BlockSpec((16, 1, hidden_units), lambda i, w: (jnp.minimum(i, 2), 0, 0))
+    once = lambda shape: pl.BlockSpec(shape, lambda i, w: (0, 0))
+    query_grad, key_grad, value_grad, output_grad, gains, router_grad, table_grad, ups, downs = call(
         unpack_kernel,
-        60,
+        32,
         (
             full,
             full,
             full,
             full,
-            sds((16, width), f32),
-            sds((HEADS // 2, 16, 128), f32),
+            sds((8, width), f32),
+            sds(router_weight.shape, f32),
+            sds(bias_table.shape, f32),
+            own_rows,
+            own_rows,
         ),
         grid_spec=pltpu.PrefetchScalarGridSpec(
             num_scalar_prefetch=1,
             grid=(HEADS // 2,),
-            in_specs=[pl.BlockSpec(memory_space=pl.ANY) for _ in everything],
+            in_specs=[pl.BlockSpec((16, 2 * hidden_units), lambda i, w: (jnp.minimum(i, 2), 0))]
+            + [pl.BlockSpec(memory_space=pl.ANY) for _ in everything],
             out_specs=[
                 column,
                 column,
                 column,
-                pl.BlockSpec((144, width), lambda i, w: (i, 0)),
-                pl.BlockSpec((16, width), lambda i, w: (0, 0)),
-                pl.BlockSpec((1, 16, 128), lambda i, w: (i, 0, 0)),
+                pl.BlockSpec((192, width), lambda i, w: (jnp.minimum(i, 3), 0)),
+                once((8, width)),
+                once(router_weight.shape),
+                once(bias_table.shape),
+                own_block,
+                own_block,
             ],
             scratch_shapes=[
                 pltpu.VMEM((2, 2, 4, 4, 4, 16, width), bf16),
@@ -795,19 +758,18 @@
             ],
         ),
         moved=16 * MB,
-    )(where, *[ring_rows(piece) for piece in everything])
-    table_grad = bias_rows.reshape(HEADS, 8, 128)[:, 2, : bias_table.shape[0]].T
+    )(where, summed, *[ring_rows(piece) for piece in everything])
     return (
         layer_out[None],
         tokens_grad[None],
-        tails[0],
+        gains[0],
         query_grad,
         key_grad,
         value_grad,
         output_grad,
         table_grad,
-        tails[1],
-        tails[8:].T,
+        gains[1],
+        router_grad,
         ups,
         downs,
     )

time: 289 us -> 292 us (1.010)
  local copies, waits for them, and re-layouts: 15.9 us -> 25.5 us
  waiting for transfers between devices: 63.1 us -> 57.6 us
    unnamed x61 -> x64, local copies, waits for them, and re-layouts: 7.48 us -> 20.1 us
    ppermute x17, waiting for transfers between devices: 23 us -> 16.9 us  [ring(): return lax.ppermute(block, axis, [(i, to(i)) for i in range(size)])]
    pallas_call x3 -> x2, Pallas kernels: 16.5 us -> 15.5 us  [the longest x1 11.2 us: on_device(): call(unpack_kernel, 32, (full, full, full, full, sds((8, width), f32), sd...]
  transfers between devices with their start and end apart: 36 -> 36, of which waited for: 16 -> 13; matrix products, arithmetic and copies ran while one was open for 3% -> 3% of each run, Pallas kernels for 27% -> 25%
where the time goes in v4:
time: 292 us; the launch traced here: 290 us
  Pallas kernels  83.1 us (28%)
  starting transfers between devices  62.3 us (21%)
  waiting for transfers between devices  57.6 us (20%)
  blocking collectives  43.9 us (15%)
  local copies, waits for them, and re-layouts  25.5 us (9%)
  between operations  14.1 us (5%)
  other arithmetic  3.91 us (1%)
    all_to_all x1, blocking collectives, on_device(): lax.all_to_all(send, 'exp', split_axis=0, concat_axis=0, tiled=True)  28.1 us
    ppermute x17, starting transfers between devices, ring(): return lax.ppermute(block, axis, [(i, to(i)) for i in range(size)])  25.5 us
    unnamed x64, local copies, waits for them, and re-layouts  20.1 us
    ppermute x17, waiting for transfers between devices, ring(): return lax.ppermute(block, axis, [(i, to(i)) for i in range(size)])  16.9 us
    all_to_all x1, blocking collectives, on_device(): lax.all_to_all(packed.reshape(n_exp, ROWS // n_exp, width), 'exp', split_...  15.8 us
    all_to_all x1, waiting for transfers between devices, on_device(): qkv = lax.all_to_all(qkv, 'ctx', split_axis=0, concat_axis=0, tiled=True)  15.1 us
    pallas_call x1, Pallas kernels, on_device(): call(attend_back_kernel, 60, (sds((n_ctx, 3 * HEAD_DIM, rows), bf16), sds...  13.8 us
    pallas_call x1, Pallas kernels, on_device(): call(expert_grad_kernel, 60, sds((width, 2 * hidden_units), bf16), grid=(...  13.1 us
  transfers between devices with their start and end apart: 36, of which 13 were waited for; matrix products, arithmetic and copies ran while one was open for 3% of the time, Pallas kernels for 25%

profile of v4, /device:TPU:1, one launch (start us, length us, event | category | flops | bytes accessed | tf_op | source)
XLA Modules:
  0.0 290.4 jit_solution(13664628222922981545)
XLA Ops:
  9.8 3.8 %shard_map.238 = (bf16[16,224,128]{2,1,0:T(8,128)(2,1)}, bf16[128,768]{1,0:T(8,128)(2,1)}) custom-call(bf16[128,768]{1,0:T(8,128)(2,1)} %bitcast.66, f32[1,768]{1,0:T(1,128)} %reshape.103.gain_ref, s32[1,128]{1,0:T(1,128)} %seg_ref.1, bf16[768,768]{1,0:T(8,128)(2,1)} %wq_ref.3, bf16[768,768]{1,0:T(8,128)(2,1)} %wk_ref.3, bf16[768,768]{1,0:T(8,128)(2,1)} %wv_ref.3), custom_call_target="tpu_custom_call" | custom-call | flops 452984832 | bytes 4194304 | tf_op jit(solution)/shard_map/pallas_call | solution.py:554
  13.6 7.6 %all-to-all-start = ((bf16[16,224,128]{2,1,0:T(8,128)(2,1)}), bf16[16,224,128]{2,1,0:T(8,128)(2,1)S(1)}, u32[]{:S(2)}, u32[]{:S(2)}) async-start(bf16[16,224,128]{2,1,0:T(8,128)(2,1)} %get-tuple-element.60), calls=%async_computation | async-start | bytes 1835008 | tf_op jit(solution)/shard_map/all_to_all | solution.py:561
  25.4 15.1 %all-to-all-done.recv_ref = bf16[16,224,128]{2,1,0:T(8,128)(2,1)S(1)} async-done(((bf16[16,224,128]{2,1,0:T(8,128)(2,1)}), bf16[16,224,128]{2,1,0:T(8,128)(2,1)S(1)}, u32[]{:S(2)}, u32[]{:S(2)}) %all-to-all-start) | async-done | bytes 917536 | tf_op jit(solution)/shard_map/all_to_all | solution.py:561
  41.5 11.1 %shard_map.239 = (bf16[16,64,128]{2,1,0:T(8,128)(2,1)}, f32[8,64,256]{2,1,0:T(8,128)}, f32[8,1,256]{2,1,0:T(1,128)}) custom-call(bf16[16,224,128]{2,1,0:T(8,128)(2,1)} %copy-done.19, s32[1,2048]{1,0:T(1,128)} %bitcast.80, f32[32,1]{1,0:T(8,128)} %pad_dynamic-slice_fusion.tab_ref), custom_call_target="tpu_custom_call" | custom-call | flops 8000000000 | bytes 10485760 | tf_op jit(solution)/shard_map/pallas_call | solution.py:574
  52.5 3.5 %all-to-all-start.1 = ((bf16[16,64,128]{2,1,0:T(8,128)(2,1)}), bf16[16,64,128]{2,1,0:T(8,128)(2,1)S(1)}, u32[]{:S(2)}, u32[]{:S(2)}) async-start(bf16[16,64,128]{2,1,0:T(8,128)(2,1)} %get-tuple-element.62), calls=%async_computation.1 | async-start | bytes 524288 | tf_op jit(solution)/shard_map/all_to_all | solution.py:589
  58.2 8.1 %all-to-all-done.1.ot_ref = bf16[16,64,128]{2,1,0:T(8,128)(2,1)S(1)} async-done(((bf16[16,64,128]{2,1,0:T(8,128)(2,1)}), bf16[16,64,128]{2,1,0:T(8,128)(2,1)S(1)}, u32[]{:S(2)}, u32[]{:S(2)}) %all-to-all-start.1) | async-done | bytes 262176 | tf_op jit(solution)/shard_map/all_to_all | solution.py:589
  67.1 3.7 %shard_map.240 = (bf16[320,1536]{1,0:T(8,128)(2,1)}, f32[128,768]{1,0:T(8,128)}, f32[128,256]{1,0:T(8,128)}, bf16[128,768]{1,0:T(8,128)(2,1)}) custom-call(bf16[16,64,128]{2,1,0:T(8,128)(2,1)} %copy-done.20, bf16[128,768]{1,0:T(8,128)(2,1)} %bitcast.67, bf16[768,768]{1,0:T(8,128)(2,1)} %wo_ref.3, f32[1,768]{1,0:T(1,128)} %reshape.105.gain_ref, ...), custom_call_target="tpu_custom_call" | custom-call | flops 1000000000 | bytes 4194304 | tf_op jit(solution)/shard_map/pallas_call | solution.py:593
  70.8 28.1 %all_to_all.53 = bf16[8,40,1536]{2,1,0:T(8,128)(2,1)} all-to-all(bf16[8,40,1536]{2,1,0:T(8,128)(2,1)} %bitcast.65), channel_id=1, replica_groups=mesh['ctx'=16,'exp'=8] {'exp'}, dimensions={0} | all-to-all | bytes 1966080 | tf_op jit(solution)/shard_map/all_to_all | solution.py:605
  98.9 12.4 %shard_map.241 = (bf16[320,1536]{1,0:T(8,128)(2,1)}, bf16[320,3072]{1,0:T(8,128)(2,1)}, bf16[320,3072]{1,0:T(8,128)(2,1)}) custom-call(bf16[320,1536]{1,0:T(8,128)(2,1)} %bitcast.60, bf16[768,6144]{1,0:T(8,128)(2,1)} %all-gather.3.cloned.1.call-done.up_ref.down_ref, bf16[768,6144]{1,0:T(8,128)(2,1)} %all-gather.3.cloned.1.call-done.up_ref.down_ref), custom_call_target="tpu_custom_call" | custom-call | flops 6039797760 | bytes 16777216 | tf_op jit(solution)/shard_map/pallas_call | solution.py:610
  111.2 5.1 %all-to-all-start.3 = ((bf16[8,40,1536]{2,1,0:T(8,128)(2,1)}), bf16[8,40,1536]{2,1,0:T(8,128)(2,1)S(1)}, u32[]{:S(2)}, u32[]{:S(2)}) async-start(bf16[8,40,1536]{2,1,0:T(8,128)(2,1)} %bitcast.64), calls=%async_computation.3 | async-start | bytes 1966080 | tf_op jit(solution)/shard_map/all_to_all | solution.py:633
  117.0 13.1 %shard_map.242 = bf16[768,6144]{1,0:T(8,128)(2,1)} custom-call(bf16[320,1536]{1,0:T(8,128)(2,1)} %bitcast.61, bf16[320,3072]{1,0:T(8,128)(2,1)} %get-tuple-element.65.pre_ref, bf16[320,3072]{1,0:T(8,128)(2,1)} %get-tuple-element.66.act_ref), custom_call_target="tpu_custom_call" | custom-call | flops 3019898880 | bytes 16777216 | tf_op jit(solution)/shard_map/pallas_call | solution.py:634
  131.7 5.2 %shard_map.243 = (bf16[128,768]{1,0:T(8,128)(2,1)}, f32[128,768]{1,0:T(8,128)}, bf16[16,64,128]{2,1,0:T(8,128)(2,1)}, bf16[768,768]{1,0:T(8,128)(2,1)}, f32[16,768]{1,0:T(8,128)}) custom-call(bf16[320,1536]{1,0:T(8,128)(2,1)} %bitcast.63, f32[128,768]{1,0:T(8,128)} %get-tuple-element.68.res_ref, bf16[128,768]{1,0:T(8,128)(2,1)} %bitcast.79, ...), custom_call_target="tpu_custom_call" | custom-call | flops 1000000000 | bytes 6291456 | tf_op jit(solution)/shard_map/pallas_call | solution.py:651
  136.9 5.2 %all-to-all-start.4 = ((bf16[16,64,128]{2,1,0:T(8,128)(2,1)}), bf16[16,64,128]{2,1,0:T(8,128)(2,1)S(1)}, u32[]{:S(2)}, u32[]{:S(2)}) async-start(bf16[16,64,128]{2,1,0:T(8,128)(2,1)} %get-tuple-element.74), calls=%async_computation.4 | async-start | bytes 524288 | tf_op jit(solution)/shard_map/all_to_all | solution.py:667
  142.2 8.4 %all-gather.5.cloned.1.call-done.hid_ref = bf16[2048,768]{1,0:T(8,128)(2,1)} async-done(((bf16[128,768]{1,0:T(8,128)(2,1)}), bf16[2048,768]{1,0:T(8,128)(2,1)}) %all-gather.5.cloned.1.call-update) | async-done | bytes 3145744 | tf_op jit(solution)/shard_map/all_gather | solution.py:571
  152.4 3.9 %all-to-all-start.5 = ((bf16[16,48,768]{2,1,0:T(8,128)(2,1)}), bf16[16,48,768]{2,1,0:T(8,128)(2,1)S(1)}, u32[]{:S(2)}, u32[]{:S(2)}) async-start(bf16[16,48,768]{2,1,0:T(8,128)(2,1)} %bitcast.16), calls=%async_computation.5 | async-start | bytes 2359296 | tf_op jit(solution)/shard_map/all_to_all | solution.py:670
  156.3 13.8 %shard_map.244 = (bf16[16,192,128]{2,1,0:T(8,128)(2,1)}, bf16[192,2048]{1,0:T(8,128)(2,1)}, f32[8,128]{1,0:T(8,128)}) custom-call(bf16[16,224,128]{2,1,0:T(8,128)(2,1)} %copy-done.19, bf16[16,64,128]{2,1,0:T(8,128)(2,1)} %copy-done.21, f32[8,64,256]{2,1,0:T(8,128)} %get-tuple-element.76.otf_ref, f32[8,1,256]{2,1,0:T(1,128)} %get-tuple-element.77.lse_ref, ...), custom_call_target="tpu_custom_call" | custom-call | flops 20000000000 | bytes 20971520 | tf_op jit(solution)/shard_map/pallas_call | solution.py:674
  170.1 6.3 %all-to-all-done.5.wo_ref = bf16[16,48,768]{2,1,0:T(8,128)(2,1)S(1)} async-done(((bf16[16,48,768]{2,1,0:T(8,128)(2,1)}), bf16[16,48,768]{2,1,0:T(8,128)(2,1)S(1)}, u32[]{:S(2)}, u32[]{:S(2)}) %all-to-all-start.5) | async-done | bytes 1179680 | tf_op jit(solution)/shard_map/all_to_all | solution.py:670
  177.4 4.3 %shard_map.245 = bf16[256,768]{1,0:T(8,128)(2,1)} custom-call(bf16[192,2048]{1,0:T(8,128)(2,1)} %get-tuple-element.78.flat_ref, bf16[2048,768]{1,0:T(8,128)(2,1)} %all-gather.5.cloned.1.call-done.hid_ref, bf16[192,768]{1,0:T(8,128)(2,1)} %pad_maximum_fusion.1.wt_ref, f32[1,768]{1,0:T(1,128)} %reshape.103.gain_ref, bf16[16,48,768]{2,1,0:T(8,128)(2,1)} %copy-done.16, ...), custom_call_target="tpu_custom_call" | custom-call | flops 603979776 | bytes 6291456 | tf_op jit(solution)/shard_map/pallas_call | solution.py:694
  181.8 15.8 %all_to_all.54 = bf16[8,32,768]{2,1,0:T(8,128)(2,1)S(1)} all-to-all(bf16[8,32,768]{2,1,0:T(8,128)(2,1)} %bitcast.62), channel_id=1, replica_groups=mesh['ctx'=16,'exp'=8] {'exp'}, dimensions={0} | all-to-all | bytes 786432 | tf_op jit(solution)/shard_map/all_to_all | solution.py:701
  197.5 5.3 %all-to-all-start.7 = ((bf16[16,192,128]{2,1,0:T(8,128)(2,1)}), bf16[16,192,128]{2,1,0:T(8,128)(2,1)S(1)}, u32[]{:S(2)}, u32[]{:S(2)}) async-start(bf16[16,192,128]{2,1,0:T(8,128)(2,1)} %get-tuple-element.90), calls=%async_computation.7 | async-start | bytes 1572864 | tf_op jit(solution)/shard_map/all_to_all | solution.py:705
  217.2 5.8 %collective-permute-done.3.refs_1_ = bf16[64,768]{1,0:T(8,128)(2,1)S(1)} collective-permute-done((bf16[64,768]{1,0:T(8,128)(2,1)S(1)}, bf16[64,768]{1,0:T(8,128)(2,1)S(1)}, u32[]{:S(2)}, u32[]{:S(2)}) %collective-permute-start.3) | collective-permute-done | bytes 98336 | tf_op jit(solution)/shard_map/ppermute | solution.py:484
  233.4 4.5 %shard_map.248 = f32[128,768]{1,0:T(8,128)} custom-call(bf16[16,192,128]{2,1,0:T(8,128)(2,1)} %copy-done.17, bf16[128,768]{1,0:T(8,128)(2,1)} %bitcast.68, f32[1,768]{1,0:T(1,128)} %reshape.103.gain_ref, f32[128,768]{1,0:T(8,128)} %get-tuple-element.94.rgrad_ref, bf16[768,768]{1,0:T(8,128)(2,1)} %wq_ref.3, bf16[768,768]{1,0:T(8,128)(2,1)} %wk_ref.3, ...), custom_call_target="tpu_custom_call" | custom-call | flops 452984832 | bytes 6291456 | tf_op jit(solution)/shard_map/pallas_call | solution.py:709
  246.9 6.4 %collective-permute-done.10 = bf16[128,768]{1,0:T(8,128)(2,1)S(1)} collective-permute-done((bf16[128,768]{1,0:T(8,128)(2,1)S(1)}, bf16[128,768]{1,0:T(8,128)(2,1)S(1)}, u32[]{:S(2)}, u32[]{:S(2)}) %collective-permute-start.10) | collective-permute-done | bytes 196640 | tf_op jit(solution)/shard_map/ppermute | solution.py:484
  270.7 11.2 %shard_map.249 = (f32[768,768]{1,0:T(8,128)}, f32[768,768]{1,0:T(8,128)}, f32[768,768]{1,0:T(8,128)}, f32[768,768]{1,0:T(8,128)}, f32[8,768]{1,0:T(8,128)S(1)}, ...) custom-call(s32[4]{0:T(128)S(1)} %copy-done.15, ...), custom_call_target="tpu_custom_call" | custom-call | bytes 16777216 | tf_op jit(solution)/shard_map/pallas_call | solution.py:725
  (145 shorter events, 68.8 us)
Async XLA Ops:
  7.2 91.7 %all-gather.3.cloned.1.call-start = ((), (), s32[]{:S(2)}) async-start(), calls=%async_computation.9 | async-start | bytes 10027008 | tf_op jit(solution)/shard_map/all_gather | solution.py:551
  9.2 141.4 %all-gather.5.cloned.1.call-start = ((), (), s32[]{:S(2)}) async-start(), calls=%async_computation.10 | async-start | bytes 3342336 | tf_op jit(solution)/shard_map/all_gather | solution.py:571
  13.6 26.9 %all-to-all-start = ((bf16[16,224,128]{2,1,0:T(8,128)(2,1)}), bf16[16,224,128]{2,1,0:T(8,128)(2,1)S(1)}, u32[]{:S(2)}, u32[]{:S(2)}) async-start(bf16[16,224,128]{2,1,0:T(8,128)(2,1)} %get-tuple-element.60), calls=%async_computation | async-start | bytes 1835008 | tf_op jit(solution)/shard_map/all_to_all | solution.py:561
  52.5 13.8 %all-to-all-start.1 = ((bf16[16,64,128]{2,1,0:T(8,128)(2,1)}), bf16[16,64,128]{2,1,0:T(8,128)(2,1)S(1)}, u32[]{:S(2)}, u32[]{:S(2)}) async-start(bf16[16,64,128]{2,1,0:T(8,128)(2,1)} %get-tuple-element.62), calls=%async_computation.1 | async-start | bytes 524288 | tf_op jit(solution)/shard_map/all_to_all | solution.py:589
  111.2 19.5 %all-to-all-start.3 = ((bf16[8,40,1536]{2,1,0:T(8,128)(2,1)}), bf16[8,40,1536]{2,1,0:T(8,128)(2,1)S(1)}, u32[]{:S(2)}, u32[]{:S(2)}) async-start(bf16[8,40,1536]{2,1,0:T(8,128)(2,1)} %bitcast.64), calls=%async_computation.3 | async-start | bytes 1966080 | tf_op jit(solution)/shard_map/all_to_all | solution.py:633
  136.9 14.8 %all-to-all-start.4 = ((bf16[16,64,128]{2,1,0:T(8,128)(2,1)}), bf16[16,64,128]{2,1,0:T(8,128)(2,1)S(1)}, u32[]{:S(2)}, u32[]{:S(2)}) async-start(bf16[16,64,128]{2,1,0:T(8,128)(2,1)} %get-tuple-element.74), calls=%async_computation.4 | async-start | bytes 524288 | tf_op jit(solution)/shard_map/all_to_all | solution.py:667
  142.1 120.3 %reduce-scatter.2.cloned.1.call-start = ((), (), s32[]{:S(2)}) async-start(), calls=%async_computation.11 | async-start | bytes 10027008 | tf_op jit(solution)/shard_map/reduce_scatter | solution.py:669
  152.4 24.0 %all-to-all-start.5 = ((bf16[16,48,768]{2,1,0:T(8,128)(2,1)}), bf16[16,48,768]{2,1,0:T(8,128)(2,1)S(1)}, u32[]{:S(2)}, u32[]{:S(2)}) async-start(bf16[16,48,768]{2,1,0:T(8,128)(2,1)} %bitcast.16), calls=%async_computation.5 | async-start | bytes 2359296 | tf_op jit(solution)/shard_map/all_to_all | solution.py:670
  197.5 30.0 %all-to-all-start.7 = ((bf16[16,192,128]{2,1,0:T(8,128)(2,1)}), bf16[16,192,128]{2,1,0:T(8,128)(2,1)S(1)}, u32[]{:S(2)}, u32[]{:S(2)}) async-start(bf16[16,192,128]{2,1,0:T(8,128)(2,1)} %get-tuple-element.90), calls=%async_computation.7 | async-start | bytes 1572864 | tf_op jit(solution)/shard_map/all_to_all | solution.py:705
  208.6 14.4 %collective-permute-start.3 = (bf16[64,768]{1,0:T(8,128)(2,1)S(1)}, bf16[64,768]{1,0:T(8,128)(2,1)S(1)}, u32[]{:S(2)}, u32[]{:S(2)}) collective-permute-start(bf16[64,768]{1,0:T(8,128)(2,1)S(1)} %get-tuple-element.86.refs_0_), channel_id=1, source_target_pairs={{0,8},{8,16},{16,24},{24,0},{32,40},{40,48},{48,56},{56,32},{64,72... | collective-permute-start | bytes 294920 | tf_op jit(solution)/shard_map/ppermute | solution.py:484
  210.0 17.4 %collective-permute-start.4 = (bf16[64,768]{1,0:T(8,128)(2,1)S(1)}, bf16[64,768]{1,0:T(8,128)(2,1)S(1)}, u32[]{:S(2)}, u32[]{:S(2)}) collective-permute-start(bf16[64,768]{1,0:T(8,128)(2,1)S(1)} %get-tuple-element.86.refs_0_), channel_id=1, source_target_pairs={{0,16},{8,24},{16,0},{24,8},{32,48},{40,56},{48,32},{56,40},{64,80... | collective-permute-start | bytes 294920 | tf_op jit(solution)/shard_map/ppermute | solution.py:484
  212.4 15.0 %collective-permute-start.5 = (bf16[64,768]{1,0:T(8,128)(2,1)S(1)}, bf16[64,768]{1,0:T(8,128)(2,1)S(1)}, u32[]{:S(2)}, u32[]{:S(2)}) collective-permute-start(bf16[64,768]{1,0:T(8,128)(2,1)S(1)} %get-tuple-element.86.refs_0_), channel_id=1, source_target_pairs={{0,24},{8,0},{16,8},{24,16},{32,56},{40,32},{48,40},{56,48},{64,88... | collective-permute-start | bytes 294920 | tf_op jit(solution)/shard_map/ppermute | solution.py:484
  213.6 13.8 %collective-permute-start.6 = (bf16[64,768]{1,0:T(8,128)(2,1)S(1)}, bf16[64,768]{1,0:T(8,128)(2,1)S(1)}, u32[]{:S(2)}, u32[]{:S(2)}) collective-permute-start(bf16[64,768]{1,0:T(8,128)(2,1)S(1)} %get-tuple-element.87.refs_4_), channel_id=1, source_target_pairs={{0,32},{8,40},{16,48},{24,56},{32,64},{40,72},{48,80},{56,88},{64,... | collective-permute-start | bytes 294920 | tf_op jit(solution)/shard_map/ppermute | solution.py:484
  214.8 12.7 %collective-permute-start.7 = (bf16[64,768]{1,0:T(8,128)(2,1)S(1)}, bf16[64,768]{1,0:T(8,128)(2,1)S(1)}, u32[]{:S(2)}, u32[]{:S(2)}) collective-permute-start(bf16[64,768]{1,0:T(8,128)(2,1)S(1)} %get-tuple-element.87.refs_4_), channel_id=1, source_target_pairs={{0,64},{8,72},{16,80},{24,88},{32,96},{40,104},{48,112},{56,120},{... | collective-permute-start | bytes 294920 | tf_op jit(solution)/shard_map/ppermute | solution.py:484
  227.5 13.6 %collective-permute-start.9 = (bf16[256,768]{1,0:T(8,128)(2,1)S(1)}, bf16[256,768]{1,0:T(8,128)(2,1)S(1)}, u32[]{:S(2)}, u32[]{:S(2)}) collective-permute-start(bf16[256,768]{1,0:T(8,128)(2,1)S(1)} %get-tuple-element.97), channel_id=1, source_target_pairs={{0,32},{8,40},{16,48},{24,56},{32,64},{40,72},{48,80},{56,88},{64,... | collective-permute-start | bytes 1179656 | tf_op jit(solution)/shard_map/ppermute | solution.py:484
  228.6 12.6 %collective-permute-start.11 = (bf16[256,768]{1,0:T(8,128)(2,1)S(1)}, bf16[256,768]{1,0:T(8,128)(2,1)S(1)}, u32[]{:S(2)}, u32[]{:S(2)}) collective-permute-start(bf16[256,768]{1,0:T(8,128)(2,1)S(1)} %get-tuple-element.97), channel_id=1, source_target_pairs={{0,96},{8,104},{16,112},{24,120},{32,0},{40,8},{48,16},{56,24},{64... | collective-permute-start | bytes 1179656 | tf_op jit(solution)/shard_map/ppermute | solution.py:484
  230.7 10.6 %collective-permute-start.13 = (bf16[256,768]{1,0:T(8,128)(2,1)S(1)}, bf16[256,768]{1,0:T(8,128)(2,1)S(1)}, u32[]{:S(2)}, u32[]{:S(2)}) collective-permute-start(bf16[256,768]{1,0:T(8,128)(2,1)S(1)} %get-tuple-element.98), channel_id=1, source_target_pairs={{0,8},{8,16},{16,24},{24,0},{32,40},{40,48},{48,56},{56,32},{64,72... | collective-permute-start | bytes 1179656 | tf_op jit(solution)/shard_map/ppermute | solution.py:484
  232.2 11.9 %collective-permute-start.15 = (bf16[256,768]{1,0:T(8,128)(2,1)S(1)}, bf16[256,768]{1,0:T(8,128)(2,1)S(1)}, u32[]{:S(2)}, u32[]{:S(2)}) collective-permute-start(bf16[256,768]{1,0:T(8,128)(2,1)S(1)} %get-tuple-element.98), channel_id=1, source_target_pairs={{0,24},{8,0},{16,8},{24,16},{32,56},{40,32},{48,40},{56,48},{64,88... | collective-permute-start | bytes 1179656 | tf_op jit(solution)/shard_map/ppermute | solution.py:484
  237.9 7.3 %collective-permute-start.17 = (bf16[256,768]{1,0:T(8,128)(2,1)S(1)}, bf16[256,768]{1,0:T(8,128)(2,1)S(1)}, u32[]{:S(2)}, u32[]{:S(2)}) collective-permute-start(bf16[256,768]{1,0:T(8,128)(2,1)S(1)} %get-tuple-element.97), channel_id=1, source_target_pairs={{0,1},{1,0},{2,3},{3,2},{4,5},{5,4},{6,7},{7,6},{8,9},{9,8},{10,11... | collective-permute-start | bytes 1179656 | tf_op jit(solution)/shard_map/ppermute | solution.py:529
  241.1 14.5 %collective-permute-start.22 = (bf16[256,768]{1,0:T(8,128)(2,1)S(1)}, bf16[256,768]{1,0:T(8,128)(2,1)S(1)}, u32[]{:S(2)}, u32[]{:S(2)}) collective-permute-start(bf16[256,768]{1,0:T(8,128)(2,1)S(1)} %get-tuple-element.98), channel_id=1, source_target_pairs={{0,1},{1,0},{2,3},{3,2},{4,5},{5,4},{6,7},{7,6},{8,9},{9,8},{10,11... | collective-permute-start | bytes 1179656 | tf_op jit(solution)/shard_map/ppermute | solution.py:529
  241.2 12.1 %collective-permute-start.10 = (bf16[128,768]{1,0:T(8,128)(2,1)S(1)}, bf16[128,768]{1,0:T(8,128)(2,1)S(1)}, u32[]{:S(2)}, u32[]{:S(2)}) collective-permute-start(bf16[128,768]{1,0:T(8,128)(2,1)S(1)} %slice.24), channel_id=1, source_target_pairs={{0,32},{8,40},{16,48},{24,56},{32,64},{40,72},{48,80},{56,88},{64,... | collective-permute-start | bytes 589832 | tf_op jit(solution)/shard_map/ppermute | solution.py:484
  241.3 13.6 %collective-permute-start.12 = (bf16[128,768]{1,0:T(8,128)(2,1)S(1)}, bf16[128,768]{1,0:T(8,128)(2,1)S(1)}, u32[]{:S(2)}, u32[]{:S(2)}) collective-permute-start(bf16[128,768]{1,0:T(8,128)(2,1)S(1)} %slice.25), channel_id=1, source_target_pairs={{0,96},{8,104},{16,112},{24,120},{32,0},{40,8},{48,16},{56,24},{64... | collective-permute-start | bytes 589832 | tf_op jit(solution)/shard_map/ppermute | solution.py:484
  244.1 12.0 %collective-permute-start.14 = (bf16[128,768]{1,0:T(8,128)(2,1)S(1)}, bf16[128,768]{1,0:T(8,128)(2,1)S(1)}, u32[]{:S(2)}, u32[]{:S(2)}) collective-permute-start(bf16[128,768]{1,0:T(8,128)(2,1)S(1)} %slice.26), channel_id=1, source_target_pairs={{0,8},{8,16},{16,24},{24,0},{32,40},{40,48},{48,56},{56,32},{64,72... | collective-permute-start | bytes 589832 | tf_op jit(solution)/shard_map/ppermute | solution.py:484
  245.2 11.9 %collective-permute-start.16 = (bf16[128,768]{1,0:T(8,128)(2,1)S(1)}, bf16[128,768]{1,0:T(8,128)(2,1)}, u32[]{:S(2)}, u32[]{:S(2)}) collective-permute-start(bf16[128,768]{1,0:T(8,128)(2,1)S(1)} %slice.27), channel_id=1, source_target_pairs={{0,24},{8,0},{16,8},{24,16},{32,56},{40,32},{48,40},{56,48},{64,88... | collective-permute-start | bytes 589832 | tf_op jit(solution)/shard_map/ppermute | solution.py:484
  (40 other events, 131.6 us)
Sparse Core Ops, SparseCore 0:
  10.7 88.0 all-gather.2
  101.0 49.6 all-gather.4
  154.1 106.9 reduce-scatter.1

commit v5 on v4

--- a/solution.py
+++ b/solution.py
@@ -274,8 +274,10 @@
 
 def combine_kernel(
     ret_ref, res_ref, grad_ref, gate_ref, hid_ref, rcol_ref, gain_ref, router_t_ref, wo_ref, ot_ref,
-    layer_ref, rgrad_ref, gt_ref, wo_grad_ref, small_ref,
+    layer_ref, rgrad_ref, gt_ref, wo_grad_ref, small_ref, weight_ref, sem,
 ):
+    weight_copy = pltpu.make_async_copy(wo_ref, weight_ref, sem)
+    weight_copy.start()
     tokens, width = res_ref.shape
     experts = router_t_ref.shape[0]
     slots_all = ret_ref.shape[0]
@@ -321,7 +323,8 @@
     residual_grad = upstream + inverse * (scaled - normed * average)
     rgrad_ref[...] = residual_grad
     branch = residual_grad.astype(bf16)
-    gt = nt(wo_ref[...], branch).astype(bf16)
+    weight_copy.wait()
+    gt = nt(weight_ref[...], branch).astype(bf16)
     gt_ref[0:HEADS] = gt.reshape(HEADS, HEAD_DIM, tokens)
     gt_ref[HEADS:] = jnp.zeros((gt_ref.shape[0] - HEADS, HEAD_DIM, tokens), bf16)
     att = ot_ref[0:HEADS].reshape(width, tokens)
@@ -417,30 +420,36 @@
 
 def ring_rows(piece):
     rows, width = piece.shape
-    shape = (4, 4, 16, width) if rows == 256 else (2, 4, 16, width)
+    shape = (4, 4, 16, width) if rows == 256 else (2, 4, 4, 16, width)
     return piece.reshape(shape)
 
 
 def unpack_kernel(where_ref, sum_ref, *refs):
-    pieces, (q_ref, k_ref, v_ref, wo_ref, gain_ref, router_ref, table_ref) = refs[:20], refs[20:27]
-    up_ref, down_ref, all_ref, sems = refs[27:]
-    units = up_ref.shape[2]
-    up_ref[:, 0, :] = sum_ref[:, 0:units].astype(f32)
-    down_ref[:, 0, :] = sum_ref[:, units:].astype(f32)
+    pieces, (q_ref, k_ref, v_ref, wo_ref, gain_ref, router_ref, table_ref) = refs[:14], refs[14:21]
+    up_ref, down_ref, all_ref, sems = refs[21:]
     step = pl.program_id(0)
     x, y, z, core = where_ref[0], where_ref[1], where_ref[2], where_ref[3]
+    copies = []
+    for k in range(2):
+        part = pieces[7 * k : 7 * k + 7]
+        moves = [(part[3 * half + j], all_ref.at[k, half, d]) for half in (0, 1) for j, d in enumerate((0, 1, 3))]
+        moves += [(part[6].at[half], all_ref.at[k, half, 2]) for half in (0, 1)]
+        for j, (source, place) in enumerate(moves):
+            copies.append(pltpu.make_async_copy(source, place, sems.at[8 * k + j]))
 
     @pl.when(step == 0)
     def _():
-        copies = []
-        for k in range(4):
-            slot = all_ref.at[k // 2, k % 2]
-            places = [slot.at[0], slot.at[1], slot.at[2, 0:2], slot.at[2, 2:4], slot.at[3]]
-            for j, place in enumerate(places):
-                n = 5 * k + j
-                copies.append(pltpu.make_async_copy(pieces[n], place, sems.at[n]))
         for copy in copies:
             copy.start()
+
+    @pl.when(step < 3)
+    def _():
+        units = up_ref.shape[2]
+        up_ref[:, 0, :] = sum_ref[:, 0:units].astype(f32)
+        down_ref[:, 0, :] = sum_ref[:, units:].astype(f32)
+
+    @pl.when(step == 0)
+    def _():
         for copy in copies:
             copy.wait()
 
@@ -522,9 +531,18 @@
     return call(join_kernel, 8, (side, side))(*plane)
 
 
+def far_kernel(*refs):
+    size = refs[0].shape[0]
+    for k, ref in enumerate(refs[:4]):
+        refs[4][k * size : (k + 1) * size, :] = ref[...]
+
+
 def gather_far(first, second, n_ctx, n_exp, done):
-    own = gather_ring("ctx", 4, n_ctx, first) + gather_ring("ctx", 1, n_ctx, second)
-    own[0], own[5], done = lax.optimization_barrier((own[0], own[5], done))
+    a = gather_ring("ctx", 4, n_ctx, first)
+    b = gather_ring("ctx", 1, n_ctx, second)
+    far = call(far_kernel, 8, sds((2 * first.shape[0], first.shape[1]), bf16))(a[2], a[3], b[2], b[3])
+    own = [a[0], a[1], a[4], b[0], b[1], b[4], far]
+    own[0], own[3], done = lax.optimization_barrier((own[0], own[3], done))
     pairs = [(i, i ^ 1) for i in range(n_exp)]
     return own + [lax.ppermute(piece, "exp", pairs) for piece in own], done
 
@@ -658,6 +676,9 @@
             sds((width, width), bf16),
             sds((16, width), f32),
         ),
+        in_specs=[pl.BlockSpec(memory_space=pltpu.VMEM)] * 8
+        + [pl.BlockSpec(memory_space=pl.ANY), pl.BlockSpec(memory_space=pltpu.VMEM)],
+        scratch_shapes=[pltpu.VMEM((width, width), bf16), pltpu.SemaphoreType.DMA(())],
         flops=10**9,
         moved=6 * MB,
     )(
@@ -724,7 +745,7 @@
     once = lambda shape: pl.BlockSpec(shape, lambda i, w: (0, 0))
     query_grad, key_grad, value_grad, output_grad, gains, router_grad, table_grad, ups, downs = call(
         unpack_kernel,
-        32,
+        60,
         (
             full,
             full,
@@ -754,7 +775,7 @@
             ],
             scratch_shapes=[
                 pltpu.VMEM((2, 2, 4, 4, 4, 16, width), bf16),
-                pltpu.SemaphoreType.DMA((20,)),
+                pltpu.SemaphoreType.DMA((16,)),
             ],
         ),
         moved=16 * MB,

time: 292 us -> 286 us (0.979)
  local copies, waits for them, and re-layouts: 25.5 us -> 20.1 us
  Pallas kernels: 83.1 us -> 79.9 us
    unnamed x64 -> x56, local copies, waits for them, and re-layouts: 20.1 us -> 10.9 us
    ppermute x10 -> x7, starting transfers between devices: 6.08 us -> 7.47 us  [gather_far(): return (own + [lax.ppermute(piece, 'exp', pairs) for piece in own], done)]
    pallas_call x1 -> x2, Pallas kernels: 11.2 us -> 10.2 us  [the longest x1 10.2 us: on_device(): call(unpack_kernel, 60, (full, full, full, full, sds((8, width), f32), sd...]
  transfers between devices with their start and end apart: 36 -> 33, of which waited for: 13 -> 17; matrix products, arithmetic and copies ran while one was open for 3% -> 4% of each run, Pallas kernels for 25% -> 25%
where the time goes in v5:
time: 286 us; the launch traced here: 284 us
  Pallas kernels  79.9 us (28%)
  starting transfers between devices  63.3 us (22%)
  waiting for transfers between devices  58.3 us (20%)
  blocking collectives  44.4 us (16%)
  local copies, waits for them, and re-layouts  20.1 us (7%)
  between operations  14 us (5%)
  other arithmetic  3.93 us (1%)
    all_to_all x1, blocking collectives, on_device(): lax.all_to_all(send, 'exp', split_axis=0, concat_axis=0, tiled=True)  28.4 us
    ppermute x17, starting transfers between devices, ring(): return lax.ppermute(block, axis, [(i, to(i)) for i in range(size)])  25 us
    all_to_all x1, blocking collectives, on_device(): lax.all_to_all(packed.reshape(n_exp, ROWS // n_exp, width), 'exp', split_...  16 us
    all_to_all x1, waiting for transfers between devices, on_device(): qkv = lax.all_to_all(qkv, 'ctx', split_axis=0, concat_axis=0, tiled=True)  15.1 us
    ppermute x17, waiting for transfers between devices, ring(): return lax.ppermute(block, axis, [(i, to(i)) for i in range(size)])  15 us
    pallas_call x1, Pallas kernels, on_device(): call(expert_grad_kernel, 60, sds((width, 2 * hidden_units), bf16), grid=(...  13.1 us
    pallas_call x1, Pallas kernels, on_device(): call(attend_back_kernel, 60, (sds((n_ctx, 3 * HEAD_DIM, rows), bf16), sds...  12.7 us
    pallas_call x1, Pallas kernels, on_device(): call(expert_kernel, 60, (sds((slots, 2 * width), bf16), sds((slots, hidde...  12.3 us
  transfers between devices with their start and end apart: 33, of which 17 were waited for; matrix products, arithmetic and copies ran while one was open for 4% of the time, Pallas kernels for 25%

profile of v5, /device:TPU:1, one launch (start us, length us, event | category | flops | bytes accessed | tf_op | source)
XLA Modules:
  0.0 283.9 jit_solution(7914038087299108600)
XLA Ops:
  9.8 3.8 %shard_map.238 = (bf16[16,224,128]{2,1,0:T(8,128)(2,1)}, bf16[128,768]{1,0:T(8,128)(2,1)}) custom-call(bf16[128,768]{1,0:T(8,128)(2,1)} %bitcast.52, f32[1,768]{1,0:T(1,128)} %reshape.85.gain_ref, s32[1,128]{1,0:T(1,128)} %seg_ref.1, bf16[768,768]{1,0:T(8,128)(2,1)} %wq_ref.3, bf16[768,768]{1,0:T(8,128)(2,1)} %wk_ref.3, bf16[768,768]{1,0:T(8,128)(2,1)} %wv_ref.3), custom_call_target="tpu_custom_call" | custom-call | flops 452984832 | bytes 4194304 | tf_op jit(solution)/shard_map/pallas_call | solution.py:572
  13.6 7.6 %all-to-all-start = ((bf16[16,224,128]{2,1,0:T(8,128)(2,1)}), bf16[16,224,128]{2,1,0:T(8,128)(2,1)S(1)}, u32[]{:S(2)}, u32[]{:S(2)}) async-start(bf16[16,224,128]{2,1,0:T(8,128)(2,1)} %get-tuple-element.60), calls=%async_computation | async-start | bytes 1835008 | tf_op jit(solution)/shard_map/all_to_all | solution.py:579
  25.4 15.1 %all-to-all-done.recv_ref = bf16[16,224,128]{2,1,0:T(8,128)(2,1)S(1)} async-done(((bf16[16,224,128]{2,1,0:T(8,128)(2,1)}), bf16[16,224,128]{2,1,0:T(8,128)(2,1)S(1)}, u32[]{:S(2)}, u32[]{:S(2)}) %all-to-all-start) | async-done | bytes 917536 | tf_op jit(solution)/shard_map/all_to_all | solution.py:579
  41.5 10.1 %shard_map.239 = (bf16[16,64,128]{2,1,0:T(8,128)(2,1)}, f32[8,64,256]{2,1,0:T(8,128)}, f32[8,1,256]{2,1,0:T(1,128)}) custom-call(bf16[16,224,128]{2,1,0:T(8,128)(2,1)} %copy-done.6, s32[1,2048]{1,0:T(1,128)} %bitcast.71, f32[32,1]{1,0:T(8,128)} %pad_dynamic-slice_fusion.tab_ref), custom_call_target="tpu_custom_call" | custom-call | flops 8000000000 | bytes 10485760 | tf_op jit(solution)/shard_map/pallas_call | solution.py:592
  57.3 7.9 %all-to-all-done.1.ot_ref = bf16[16,64,128]{2,1,0:T(8,128)(2,1)S(1)} async-done(((bf16[16,64,128]{2,1,0:T(8,128)(2,1)}), bf16[16,64,128]{2,1,0:T(8,128)(2,1)S(1)}, u32[]{:S(2)}, u32[]{:S(2)}) %all-to-all-start.1) | async-done | bytes 262176 | tf_op jit(solution)/shard_map/all_to_all | solution.py:607
  65.9 3.7 %shard_map.240 = (bf16[320,1536]{1,0:T(8,128)(2,1)}, f32[128,768]{1,0:T(8,128)}, f32[128,256]{1,0:T(8,128)}, bf16[128,768]{1,0:T(8,128)(2,1)}) custom-call(bf16[16,64,128]{2,1,0:T(8,128)(2,1)} %copy-done.16, bf16[128,768]{1,0:T(8,128)(2,1)} %bitcast.53, bf16[768,768]{1,0:T(8,128)(2,1)} %wo_ref.3, f32[1,768]{1,0:T(1,128)} %reshape.87.gain_ref, ...), custom_call_target="tpu_custom_call" | custom-call | flops 1000000000 | bytes 4194304 | tf_op jit(solution)/shard_map/pallas_call | solution.py:611
  69.6 28.4 %all_to_all.53 = bf16[8,40,1536]{2,1,0:T(8,128)(2,1)} all-to-all(bf16[8,40,1536]{2,1,0:T(8,128)(2,1)} %bitcast.47), channel_id=1, replica_groups=mesh['ctx'=16,'exp'=8] {'exp'}, dimensions={0} | all-to-all | bytes 1966080 | tf_op jit(solution)/shard_map/all_to_all | solution.py:623
  98.8 12.3 %shard_map.241 = (bf16[320,1536]{1,0:T(8,128)(2,1)}, bf16[320,3072]{1,0:T(8,128)(2,1)}, bf16[320,3072]{1,0:T(8,128)(2,1)}) custom-call(bf16[320,1536]{1,0:T(8,128)(2,1)} %bitcast.42, bf16[768,6144]{1,0:T(8,128)(2,1)} %all-gather.3.cloned.1.call-done.up_ref.down_ref, bf16[768,6144]{1,0:T(8,128)(2,1)} %all-gather.3.cloned.1.call-done.up_ref.down_ref), custom_call_target="tpu_custom_call" | custom-call | flops 6039797760 | bytes 16777216 | tf_op jit(solution)/shard_map/pallas_call | solution.py:628
  111.2 5.2 %all-to-all-start.3 = ((bf16[8,40,1536]{2,1,0:T(8,128)(2,1)}), bf16[8,40,1536]{2,1,0:T(8,128)(2,1)S(1)}, u32[]{:S(2)}, u32[]{:S(2)}) async-start(bf16[8,40,1536]{2,1,0:T(8,128)(2,1)} %bitcast.46), calls=%async_computation.3 | async-start | bytes 1966080 | tf_op jit(solution)/shard_map/all_to_all | solution.py:651
  117.0 13.1 %shard_map.242 = bf16[768,6144]{1,0:T(8,128)(2,1)} custom-call(bf16[320,1536]{1,0:T(8,128)(2,1)} %bitcast.43, bf16[320,3072]{1,0:T(8,128)(2,1)} %get-tuple-element.65.pre_ref, bf16[320,3072]{1,0:T(8,128)(2,1)} %get-tuple-element.66.act_ref), custom_call_target="tpu_custom_call" | custom-call | flops 3019898880 | bytes 16777216 | tf_op jit(solution)/shard_map/pallas_call | solution.py:652
  131.7 4.9 %shard_map.243 = (bf16[128,768]{1,0:T(8,128)(2,1)}, f32[128,768]{1,0:T(8,128)}, bf16[16,64,128]{2,1,0:T(8,128)(2,1)}, bf16[768,768]{1,0:T(8,128)(2,1)}, f32[16,768]{1,0:T(8,128)}) custom-call(bf16[320,1536]{1,0:T(8,128)(2,1)} %bitcast.45, f32[128,768]{1,0:T(8,128)} %get-tuple-element.68.res_ref, bf16[128,768]{1,0:T(8,128)(2,1)} %bitcast.70, ...), custom_call_target="tpu_custom_call" | custom-call | flops 1000000000 | bytes 6291456 | tf_op jit(solution)/shard_map/pallas_call | solution.py:669
  136.6 5.0 %all-to-all-start.4 = ((bf16[16,64,128]{2,1,0:T(8,128)(2,1)}), bf16[16,64,128]{2,1,0:T(8,128)(2,1)S(1)}, u32[]{:S(2)}, u32[]{:S(2)}) async-start(bf16[16,64,128]{2,1,0:T(8,128)(2,1)} %get-tuple-element.74), calls=%async_computation.4 | async-start | bytes 524288 | tf_op jit(solution)/shard_map/all_to_all | solution.py:688
  141.7 9.3 %all-gather.5.cloned.1.call-done.hid_ref = bf16[2048,768]{1,0:T(8,128)(2,1)} async-done(((bf16[128,768]{1,0:T(8,128)(2,1)}), bf16[2048,768]{1,0:T(8,128)(2,1)}) %all-gather.5.cloned.1.call-update) | async-done | bytes 3145744 | tf_op jit(solution)/shard_map/all_gather | solution.py:589
  152.4 3.9 %all-to-all-start.5 = ((bf16[16,48,768]{2,1,0:T(8,128)(2,1)}), bf16[16,48,768]{2,1,0:T(8,128)(2,1)S(1)}, u32[]{:S(2)}, u32[]{:S(2)}) async-start(bf16[16,48,768]{2,1,0:T(8,128)(2,1)} %bitcast.16), calls=%async_computation.5 | async-start | bytes 2359296 | tf_op jit(solution)/shard_map/all_to_all | solution.py:691
  156.2 12.7 %shard_map.244 = (bf16[16,192,128]{2,1,0:T(8,128)(2,1)}, bf16[192,2048]{1,0:T(8,128)(2,1)}, f32[8,128]{1,0:T(8,128)}) custom-call(bf16[16,224,128]{2,1,0:T(8,128)(2,1)} %copy-done.6, bf16[16,64,128]{2,1,0:T(8,128)(2,1)} %copy-done.17, f32[8,64,256]{2,1,0:T(8,128)} %get-tuple-element.76.otf_ref, f32[8,1,256]{2,1,0:T(1,128)} %get-tuple-element.77.lse_ref, ...), custom_call_target="tpu_custom_call" | custom-call | flops 20000000000 | bytes 20971520 | tf_op jit(solution)/shard_map/pallas_call | solution.py:695
  169.0 7.3 %all-to-all-done.5.wo_ref = bf16[16,48,768]{2,1,0:T(8,128)(2,1)S(1)} async-done(((bf16[16,48,768]{2,1,0:T(8,128)(2,1)}), bf16[16,48,768]{2,1,0:T(8,128)(2,1)S(1)}, u32[]{:S(2)}, u32[]{:S(2)}) %all-to-all-start.5) | async-done | bytes 1179680 | tf_op jit(solution)/shard_map/all_to_all | solution.py:691
  177.3 4.3 %shard_map.245 = bf16[256,768]{1,0:T(8,128)(2,1)} custom-call(bf16[192,2048]{1,0:T(8,128)(2,1)} %get-tuple-element.78.flat_ref, bf16[2048,768]{1,0:T(8,128)(2,1)} %all-gather.5.cloned.1.call-done.hid_ref, bf16[192,768]{1,0:T(8,128)(2,1)} %pad_maximum_fusion.1.wt_ref, f32[1,768]{1,0:T(1,128)} %reshape.85.gain_ref, bf16[16,48,768]{2,1,0:T(8,128)(2,1)} %copy-done.3, ...), custom_call_target="tpu_custom_call" | custom-call | flops 603979776 | bytes 6291456 | tf_op jit(solution)/shard_map/pallas_call | solution.py:715
  181.6 16.0 %all_to_all.54 = bf16[8,32,768]{2,1,0:T(8,128)(2,1)S(1)} all-to-all(bf16[8,32,768]{2,1,0:T(8,128)(2,1)} %bitcast.44), channel_id=1, replica_groups=mesh['ctx'=16,'exp'=8] {'exp'}, dimensions={0} | all-to-all | bytes 786432 | tf_op jit(solution)/shard_map/all_to_all | solution.py:722
  197.6 5.5 %all-to-all-start.7 = ((bf16[16,192,128]{2,1,0:T(8,128)(2,1)}), bf16[16,192,128]{2,1,0:T(8,128)(2,1)S(1)}, u32[]{:S(2)}, u32[]{:S(2)}) async-start(bf16[16,192,128]{2,1,0:T(8,128)(2,1)} %get-tuple-element.90), calls=%async_computation.7 | async-start | bytes 1572864 | tf_op jit(solution)/shard_map/all_to_all | solution.py:726
  217.5 6.0 %collective-permute-done.3.refs_1_ = bf16[64,768]{1,0:T(8,128)(2,1)S(1)} collective-permute-done((bf16[64,768]{1,0:T(8,128)(2,1)S(1)}, bf16[64,768]{1,0:T(8,128)(2,1)S(1)}, u32[]{:S(2)}, u32[]{:S(2)}) %collective-permute-start.3) | collective-permute-done | bytes 98336 | tf_op jit(solution)/shard_map/ppermute | solution.py:493
  233.8 4.2 %collective-permute-done.9 = bf16[256,768]{1,0:T(8,128)(2,1)S(1)} collective-permute-done((bf16[256,768]{1,0:T(8,128)(2,1)S(1)}, bf16[256,768]{1,0:T(8,128)(2,1)S(1)}, u32[]{:S(2)}, u32[]{:S(2)}) %collective-permute-start.9) | collective-permute-done | bytes 393248 | tf_op jit(solution)/shard_map/ppermute | solution.py:493
  246.4 4.6 %shard_map.248 = f32[128,768]{1,0:T(8,128)} custom-call(bf16[16,192,128]{2,1,0:T(8,128)(2,1)} %copy-done.4, bf16[128,768]{1,0:T(8,128)(2,1)} %bitcast.54, f32[1,768]{1,0:T(1,128)} %reshape.85.gain_ref, f32[128,768]{1,0:T(8,128)} %get-tuple-element.94.rgrad_ref, bf16[768,768]{1,0:T(8,128)(2,1)} %wq_ref.3, bf16[768,768]{1,0:T(8,128)(2,1)} %wk_ref.3, ...), custom_call_target="tpu_custom_call" | custom-call | flops 452984832 | bytes 6291456 | tf_op jit(solution)/shard_map/pallas_call | solution.py:730
  250.9 4.3 %collective-permute-start.17 = (bf16[256,768]{1,0:T(8,128)(2,1)S(1)}, bf16[256,768]{1,0:T(8,128)(2,1)S(1)}, u32[]{:S(2)}, u32[]{:S(2)}) collective-permute-start(bf16[256,768]{1,0:T(8,128)(2,1)S(1)} %get-tuple-element.97), channel_id=1, source_target_pairs={{0,1},{1,0},{2,3},{3,2},{4,5},{5,4},{6,7},{7,6},{8,9},{9,8},{10,11... | collective-permute-start | bytes 1179656 | tf_op jit(solution)/shard_map/ppermute | solution.py:547
  262.6 10.2 %shard_map.250 = (f32[768,768]{1,0:T(8,128)}, f32[768,768]{1,0:T(8,128)}, f32[768,768]{1,0:T(8,128)}, f32[768,768]{1,0:T(8,128)}, f32[8,768]{1,0:T(8,128)}, /*in...) custom-call(s32[4]{0:T(128)} %pad_add_fusion.where_ref, ...), custom_call_target="tpu_custom_call" | custom-call | bytes 16777216 | tf_op jit(solution)/shard_map/pallas_call | solution.py:746
  (132 shorter events, 64.6 us)
Async XLA Ops:
  7.2 91.7 %all-gather.3.cloned.1.call-start = ((), (), s32[]{:S(2)}) async-start(), calls=%async_computation.9 | async-start | bytes 10027008 | tf_op jit(solution)/shard_map/all_gather | solution.py:569
  9.2 141.8 %all-gather.5.cloned.1.call-start = ((), (), s32[]{:S(2)}) async-start(), calls=%async_computation.10 | async-start | bytes 3342336 | tf_op jit(solution)/shard_map/all_gather | solution.py:589
  13.6 26.9 %all-to-all-start = ((bf16[16,224,128]{2,1,0:T(8,128)(2,1)}), bf16[16,224,128]{2,1,0:T(8,128)(2,1)S(1)}, u32[]{:S(2)}, u32[]{:S(2)}) async-start(bf16[16,224,128]{2,1,0:T(8,128)(2,1)} %get-tuple-element.60), calls=%async_computation | async-start | bytes 1835008 | tf_op jit(solution)/shard_map/all_to_all | solution.py:579
  51.6 13.6 %all-to-all-start.1 = ((bf16[16,64,128]{2,1,0:T(8,128)(2,1)}), bf16[16,64,128]{2,1,0:T(8,128)(2,1)S(1)}, u32[]{:S(2)}, u32[]{:S(2)}) async-start(bf16[16,64,128]{2,1,0:T(8,128)(2,1)} %get-tuple-element.62), calls=%async_computation.1 | async-start | bytes 524288 | tf_op jit(solution)/shard_map/all_to_all | solution.py:607
  111.2 19.6 %all-to-all-start.3 = ((bf16[8,40,1536]{2,1,0:T(8,128)(2,1)}), bf16[8,40,1536]{2,1,0:T(8,128)(2,1)S(1)}, u32[]{:S(2)}, u32[]{:S(2)}) async-start(bf16[8,40,1536]{2,1,0:T(8,128)(2,1)} %bitcast.46), calls=%async_computation.3 | async-start | bytes 1966080 | tf_op jit(solution)/shard_map/all_to_all | solution.py:651
  136.6 15.0 %all-to-all-start.4 = ((bf16[16,64,128]{2,1,0:T(8,128)(2,1)}), bf16[16,64,128]{2,1,0:T(8,128)(2,1)S(1)}, u32[]{:S(2)}, u32[]{:S(2)}) async-start(bf16[16,64,128]{2,1,0:T(8,128)(2,1)} %get-tuple-element.74), calls=%async_computation.4 | async-start | bytes 524288 | tf_op jit(solution)/shard_map/all_to_all | solution.py:688
  141.6 120.2 %reduce-scatter.2.cloned.1.call-start = ((), (), s32[]{:S(2)}) async-start(), calls=%async_computation.11 | async-start | bytes 10027008 | tf_op jit(solution)/shard_map/reduce_scatter | solution.py:690
  152.4 23.9 %all-to-all-start.5 = ((bf16[16,48,768]{2,1,0:T(8,128)(2,1)}), bf16[16,48,768]{2,1,0:T(8,128)(2,1)S(1)}, u32[]{:S(2)}, u32[]{:S(2)}) async-start(bf16[16,48,768]{2,1,0:T(8,128)(2,1)} %bitcast.16), calls=%async_computation.5 | async-start | bytes 2359296 | tf_op jit(solution)/shard_map/all_to_all | solution.py:691
  197.6 30.3 %all-to-all-start.7 = ((bf16[16,192,128]{2,1,0:T(8,128)(2,1)}), bf16[16,192,128]{2,1,0:T(8,128)(2,1)S(1)}, u32[]{:S(2)}, u32[]{:S(2)}) async-start(bf16[16,192,128]{2,1,0:T(8,128)(2,1)} %get-tuple-element.90), calls=%async_computation.7 | async-start | bytes 1572864 | tf_op jit(solution)/shard_map/all_to_all | solution.py:726
  208.9 14.6 %collective-permute-start.3 = (bf16[64,768]{1,0:T(8,128)(2,1)S(1)}, bf16[64,768]{1,0:T(8,128)(2,1)S(1)}, u32[]{:S(2)}, u32[]{:S(2)}) collective-permute-start(bf16[64,768]{1,0:T(8,128)(2,1)S(1)} %get-tuple-element.86.refs_0_), channel_id=1, source_target_pairs={{0,8},{8,16},{16,24},{24,0},{32,40},{40,48},{48,56},{56,32},{64,72... | collective-permute-start | bytes 294920 | tf_op jit(solution)/shard_map/ppermute | solution.py:493
  210.3 17.4 %collective-permute-start.4 = (bf16[64,768]{1,0:T(8,128)(2,1)S(1)}, bf16[64,768]{1,0:T(8,128)(2,1)S(1)}, u32[]{:S(2)}, u32[]{:S(2)}) collective-permute-start(bf16[64,768]{1,0:T(8,128)(2,1)S(1)} %get-tuple-element.86.refs_0_), channel_id=1, source_target_pairs={{0,16},{8,24},{16,0},{24,8},{32,48},{40,56},{48,32},{56,40},{64,80... | collective-permute-start | bytes 294920 | tf_op jit(solution)/shard_map/ppermute | solution.py:493
  212.7 15.1 %collective-permute-start.5 = (bf16[64,768]{1,0:T(8,128)(2,1)S(1)}, bf16[64,768]{1,0:T(8,128)(2,1)S(1)}, u32[]{:S(2)}, u32[]{:S(2)}) collective-permute-start(bf16[64,768]{1,0:T(8,128)(2,1)S(1)} %get-tuple-element.86.refs_0_), channel_id=1, source_target_pairs={{0,24},{8,0},{16,8},{24,16},{32,56},{40,32},{48,40},{56,48},{64,88... | collective-permute-start | bytes 294920 | tf_op jit(solution)/shard_map/ppermute | solution.py:493
  213.9 13.9 %collective-permute-start.6 = (bf16[64,768]{1,0:T(8,128)(2,1)S(1)}, bf16[64,768]{1,0:T(8,128)(2,1)S(1)}, u32[]{:S(2)}, u32[]{:S(2)}) collective-permute-start(bf16[64,768]{1,0:T(8,128)(2,1)S(1)} %get-tuple-element.87.refs_4_), channel_id=1, source_target_pairs={{0,32},{8,40},{16,48},{24,56},{32,64},{40,72},{48,80},{56,88},{64,... | collective-permute-start | bytes 294920 | tf_op jit(solution)/shard_map/ppermute | solution.py:493
  215.1 12.7 %collective-permute-start.7 = (bf16[64,768]{1,0:T(8,128)(2,1)S(1)}, bf16[64,768]{1,0:T(8,128)(2,1)S(1)}, u32[]{:S(2)}, u32[]{:S(2)}) collective-permute-start(bf16[64,768]{1,0:T(8,128)(2,1)S(1)} %get-tuple-element.87.refs_4_), channel_id=1, source_target_pairs={{0,64},{8,72},{16,80},{24,88},{32,96},{40,104},{48,112},{56,120},{... | collective-permute-start | bytes 294920 | tf_op jit(solution)/shard_map/ppermute | solution.py:493
  227.9 10.1 %collective-permute-start.9 = (bf16[256,768]{1,0:T(8,128)(2,1)S(1)}, bf16[256,768]{1,0:T(8,128)(2,1)S(1)}, u32[]{:S(2)}, u32[]{:S(2)}) collective-permute-start(bf16[256,768]{1,0:T(8,128)(2,1)S(1)} %get-tuple-element.97), channel_id=1, source_target_pairs={{0,32},{8,40},{16,48},{24,56},{32,64},{40,72},{48,80},{56,88},{64,... | collective-permute-start | bytes 1179656 | tf_op jit(solution)/shard_map/ppermute | solution.py:493
  229.1 9.7 %collective-permute-start.10 = (bf16[256,768]{1,0:T(8,128)(2,1)S(1)}, bf16[256,768]{1,0:T(8,128)(2,1)S(1)}, u32[]{:S(2)}, u32[]{:S(2)}) collective-permute-start(bf16[256,768]{1,0:T(8,128)(2,1)S(1)} %get-tuple-element.97), channel_id=1, source_target_pairs={{0,96},{8,104},{16,112},{24,120},{32,0},{40,8},{48,16},{56,24},{64... | collective-permute-start | bytes 1179656 | tf_op jit(solution)/shard_map/ppermute | solution.py:493
  231.2 11.0 %collective-permute-start.11 = (bf16[256,768]{1,0:T(8,128)(2,1)S(1)}, bf16[256,768]{1,0:T(8,128)(2,1)S(1)}, u32[]{:S(2)}, u32[]{:S(2)}) collective-permute-start(bf16[256,768]{1,0:T(8,128)(2,1)S(1)} %get-tuple-element.98), channel_id=1, source_target_pairs={{0,8},{8,16},{16,24},{24,0},{32,40},{40,48},{48,56},{56,32},{64,72... | collective-permute-start | bytes 1179656 | tf_op jit(solution)/shard_map/ppermute | solution.py:493
  232.1 11.1 %collective-permute-start.12 = (bf16[256,768]{1,0:T(8,128)(2,1)S(1)}, bf16[256,768]{1,0:T(8,128)(2,1)S(1)}, u32[]{:S(2)}, u32[]{:S(2)}) collective-permute-start(bf16[256,768]{1,0:T(8,128)(2,1)S(1)} %get-tuple-element.98), channel_id=1, source_target_pairs={{0,24},{8,0},{16,8},{24,16},{32,56},{40,32},{48,40},{56,48},{64,88... | collective-permute-start | bytes 1179656 | tf_op jit(solution)/shard_map/ppermute | solution.py:493
  238.8 16.5 %collective-permute-start.13 = (bf16[128,768]{1,0:T(8,128)(2,1)}, bf16[128,768]{1,0:T(8,128)(2,1)S(1)}, u32[]{:S(2)}, u32[]{:S(2)}) collective-permute-start(bf16[128,768]{1,0:T(8,128)(2,1)} %slice.24), channel_id=1, source_target_pairs={{0,32},{8,40},{16,48},{24,56},{32,64},{40,72},{48,80},{56,88},{64,... | collective-permute-start | bytes 589832 | tf_op jit(solution)/shard_map/ppermute | solution.py:493
  239.5 15.8 %collective-permute-start.14 = (bf16[128,768]{1,0:T(8,128)(2,1)}, bf16[128,768]{1,0:T(8,128)(2,1)S(1)}, u32[]{:S(2)}, u32[]{:S(2)}) collective-permute-start(bf16[128,768]{1,0:T(8,128)(2,1)} %slice.25), channel_id=1, source_target_pairs={{0,96},{8,104},{16,112},{24,120},{32,0},{40,8},{48,16},{56,24},{64... | collective-permute-start | bytes 589832 | tf_op jit(solution)/shard_map/ppermute | solution.py:493
  242.9 12.4 %collective-permute-start.15 = (bf16[128,768]{1,0:T(8,128)(2,1)}, bf16[128,768]{1,0:T(8,128)(2,1)S(1)}, u32[]{:S(2)}, u32[]{:S(2)}) collective-permute-start(bf16[128,768]{1,0:T(8,128)(2,1)} %slice.26), channel_id=1, source_target_pairs={{0,8},{8,16},{16,24},{24,0},{32,40},{40,48},{48,56},{56,32},{64,72... | collective-permute-start | bytes 589832 | tf_op jit(solution)/shard_map/ppermute | solution.py:493
  243.9 11.4 %collective-permute-start.16 = (bf16[128,768]{1,0:T(8,128)(2,1)}, bf16[128,768]{1,0:T(8,128)(2,1)S(1)}, u32[]{:S(2)}, u32[]{:S(2)}) collective-permute-start(bf16[128,768]{1,0:T(8,128)(2,1)} %slice.27), channel_id=1, source_target_pairs={{0,24},{8,0},{16,8},{24,16},{32,56},{40,32},{48,40},{56,48},{64,88... | collective-permute-start | bytes 589832 | tf_op jit(solution)/shard_map/ppermute | solution.py:493
  250.9 7.3 %collective-permute-start.17 = (bf16[256,768]{1,0:T(8,128)(2,1)S(1)}, bf16[256,768]{1,0:T(8,128)(2,1)S(1)}, u32[]{:S(2)}, u32[]{:S(2)}) collective-permute-start(bf16[256,768]{1,0:T(8,128)(2,1)S(1)} %get-tuple-element.97), channel_id=1, source_target_pairs={{0,1},{1,0},{2,3},{3,2},{4,5},{5,4},{6,7},{7,6},{8,9},{9,8},{10,11... | collective-permute-start | bytes 1179656 | tf_op jit(solution)/shard_map/ppermute | solution.py:547
  255.4 6.4 %collective-permute-start.23 = (bf16[512,768]{1,0:T(8,128)(2,1)S(1)}, bf16[512,768]{1,0:T(8,128)(2,1)}, u32[]{:S(2)}, u32[]{:S(2)}) collective-permute-start(bf16[512,768]{1,0:T(8,128)(2,1)S(1)} %shard_map.249), channel_id=1, source_target_pairs={{0,1},{1,0},{2,3},{3,2},{4,5},{5,4},{6,7},{7,6},{8,9},{9,8},{10,11... | collective-permute-start | bytes 2359304 | tf_op jit(solution)/shard_map/ppermute | solution.py:547
  (33 other events, 242.0 us)
Sparse Core Ops, SparseCore 0:
  10.7 88.0 all-gather.2
  101.0 49.9 all-gather.4
  154.4 105.2 reduce-scatter.1

commit v6 on v5

--- a/solution.py
+++ b/solution.py
@@ -424,9 +424,15 @@
     return piece.reshape(shape)
 
 
-def unpack_kernel(where_ref, sum_ref, *refs):
-    pieces, (q_ref, k_ref, v_ref, wo_ref, gain_ref, router_ref, table_ref) = refs[:14], refs[14:21]
-    up_ref, down_ref, all_ref, sems = refs[21:]
+def widen_kernel(in_ref, up_ref, down_ref):
+    units = up_ref.shape[2]
+    up_ref[:, 0, :] = in_ref[:, 0:units].astype(f32)
+    down_ref[:, 0, :] = in_ref[:, units:].astype(f32)
+
+
+def unpack_kernel(where_ref, *refs):
+    pieces, (q_ref, k_ref, v_ref, wo_ref, gain_one_ref, gain_two_ref) = refs[:14], refs[14:20]
+    router_ref, table_ref, all_ref, sems = refs[20:]
     step = pl.program_id(0)
     x, y, z, core = where_ref[0], where_ref[1], where_ref[2], where_ref[3]
     copies = []
@@ -442,12 +448,6 @@
         for copy in copies:
             copy.start()
 
-    @pl.when(step < 3)
-    def _():
-        units = up_ref.shape[2]
-        up_ref[:, 0, :] = sum_ref[:, 0:units].astype(f32)
-        down_ref[:, 0, :] = sum_ref[:, units:].astype(f32)
-
     @pl.when(step == 0)
     def _():
         for copy in copies:
@@ -477,12 +477,12 @@
         total = tails[0]
         for part in tails[1:]:
             total = total + part
-        gain_ref[...] = total[0:8]
-        router_ref[...] = jnp.concatenate([total, total], axis=0).T[:, 8:16]
-        table = jnp.concatenate(
-            [part[2:3, 0:128] for part in tails[:HEADS]] + [jnp.zeros((128 - HEADS, 128), f32)], axis=0
+        gain_one_ref[...] = total[0:1]
+        gain_two_ref[...] = total[1:2]
+        router_ref[...] = total[8:16]
+        table_ref[...] = jnp.concatenate(
+            [part[2:3, 0 : table_ref.shape[1]] for part in tails[:HEADS]], axis=0
         )
-        table_ref[...] = table.T[0 : table_ref.shape[0], 0:HEADS]
 
 
 def ring(axis, stride, size, block, distance):
@@ -537,14 +537,13 @@
         refs[4][k * size : (k + 1) * size, :] = ref[...]
 
 
-def gather_far(first, second, n_ctx, n_exp, done):
+def gather_far(first, second, n_ctx, n_exp):
     a = gather_ring("ctx", 4, n_ctx, first)
     b = gather_ring("ctx", 1, n_ctx, second)
     far = call(far_kernel, 8, sds((2 * first.shape[0], first.shape[1]), bf16))(a[2], a[3], b[2], b[3])
     own = [a[0], a[1], a[4], b[0], b[1], b[4], far]
-    own[0], own[3], done = lax.optimization_barrier((own[0], own[3], done))
     pairs = [(i, i ^ 1) for i in range(n_exp)]
-    return own + [lax.ppermute(piece, "exp", pairs) for piece in own], done
+    return own + [lax.ppermute(piece, "exp", pairs) for piece in own]
 
 
 def on_device(
@@ -722,28 +721,18 @@
     parts = lax.all_to_all(
         packed.reshape(n_exp, ROWS // n_exp, width), "exp", split_axis=0, concat_axis=0, tiled=True
     )
-    parts, dqkv = lax.optimization_barrier((parts, dqkv))
-    back = lax.all_to_all(dqkv, "ctx", split_axis=0, concat_axis=0, tiled=True)
     share = jnp.sum(parts.astype(f32), axis=0).astype(bf16)
     first, second = gather_near_all(share, n_ctx, n_exp)
-    first, second, back = lax.optimization_barrier((first, second, back))
-    tokens_grad = call(
-        tokens_kernel,
-        60,
-        sds((rows, width), f32),
-        flops=6 * rows * width * width,
-        moved=6 * MB,
-    )(back, x, gain_one, residual_grad, query_weight, key_weight, value_weight)
-    everything, tokens_grad = gather_far(first, second, n_ctx, n_exp, tokens_grad)
+    first, second, dqkv = lax.optimization_barrier((first, second, dqkv))
+    back = lax.all_to_all(dqkv, "ctx", split_axis=0, concat_axis=0, tiled=True)
+    everything = gather_far(first, second, n_ctx, n_exp)
 
     full = sds((width, width), f32)
     column = pl.BlockSpec((width, 128), lambda i, w: (0, i))
     exp = lax.axis_index("exp")
     where = jnp.stack([head % 4, head // 4, exp // 2, exp % 2]).astype(jnp.int32)
-    own_rows = sds((summed.shape[0], 1, hidden_units), f32)
-    own_block = pl.BlockSpec((16, 1, hidden_units), lambda i, w: (jnp.minimum(i, 2), 0, 0))
     once = lambda shape: pl.BlockSpec(shape, lambda i, w: (0, 0))
-    query_grad, key_grad, value_grad, output_grad, gains, router_grad, table_grad, ups, downs = call(
+    query_grad, key_grad, value_grad, output_grad, gain_a, gain_b, router_grad, table_grad = call(
         unpack_kernel,
         60,
         (
@@ -751,27 +740,24 @@
             full,
             full,
             full,
-            sds((8, width), f32),
-            sds(router_weight.shape, f32),
-            sds(bias_table.shape, f32),
-            own_rows,
-            own_rows,
+            sds((1, width), f32),
+            sds((1, width), f32),
+            sds((experts, width), f32),
+            sds((HEADS, bias_table.shape[0]), f32),
         ),
         grid_spec=pltpu.PrefetchScalarGridSpec(
             num_scalar_prefetch=1,
             grid=(HEADS // 2,),
-            in_specs=[pl.BlockSpec((16, 2 * hidden_units), lambda i, w: (jnp.minimum(i, 2), 0))]
-            + [pl.BlockSpec(memory_space=pl.ANY) for _ in everything],
+            in_specs=[pl.BlockSpec(memory_space=pl.ANY) for _ in everything],
             out_specs=[
                 column,
                 column,
                 column,
                 pl.BlockSpec((192, width), lambda i, w: (jnp.minimum(i, 3), 0)),
-                once((8, width)),
-                once(router_weight.shape),
-                once(bias_table.shape),
-                own_block,
-                own_block,
+                once((1, width)),
+                once((1, width)),
+                once((experts, width)),
+                once((HEADS, bias_table.shape[0])),
             ],
             scratch_shapes=[
                 pltpu.VMEM((2, 2, 4, 4, 4, 16, width), bf16),
@@ -779,18 +765,37 @@
             ],
         ),
         moved=16 * MB,
-    )(where, summed, *[ring_rows(piece) for piece in everything])
+    )(where, *[ring_rows(piece) for piece in everything])
+    back, output_grad = lax.optimization_barrier((back, output_grad))
+    tokens_grad = call(
+        tokens_kernel,
+        60,
+        sds((rows, width), f32),
+        flops=6 * rows * width * width,
+        moved=6 * MB,
+    )(back, x, gain_one, residual_grad, query_weight, key_weight, value_weight)
+    summed, tokens_grad = lax.optimization_barrier((summed, tokens_grad))
+    own_rows = sds((summed.shape[0], 1, hidden_units), f32)
+    ups, downs = call(
+        widen_kernel,
+        60,
+        (own_rows, own_rows),
+        grid=(summed.shape[0] // 16,),
+        in_specs=[pl.BlockSpec((16, 2 * hidden_units), lambda i: (i, 0))],
+        out_specs=[pl.BlockSpec((16, 1, hidden_units), lambda i: (i, 0, 0))] * 2,
+        moved=2 * MB,
+    )(summed)
     return (
         layer_out[None],
         tokens_grad[None],
-        gains[0],
+        gain_a[0],
         query_grad,
         key_grad,
         value_grad,
         output_grad,
-        table_grad,
-        gains[1],
-        router_grad,
+        table_grad.T,
+        gain_b[0],
+        router_grad.T,
         ups,
         downs,
     )

time: 286 us -> 284 us (level)
  local copies, waits for them, and re-layouts: 20.1 us -> 11.3 us
  waiting for transfers between devices: 58.3 us -> 62.7 us
    unnamed x56 -> x48, local copies, waits for them, and re-layouts: 10.9 us -> 6.46 us
    ppermute x17, starting transfers between devices: 25 us -> 21.2 us  [ring(): return lax.ppermute(block, axis, [(i, to(i)) for i in range(size)])]
    ppermute x17, waiting for transfers between devices: 15 us -> 18.9 us  [ring(): return lax.ppermute(block, axis, [(i, to(i)) for i in range(size)])]
    pallas_call x1 -> x2, Pallas kernels: 10.2 us -> 11.4 us  [the longest x1 8.47 us: on_device(): call(unpack_kernel, 60, (full, full, full, full, sds((1, width), f32), sd...]
  transfers between devices with their start and end apart: 33 -> 33, of which waited for: 17 -> 20; matrix products, arithmetic and copies ran while one was open for 4% -> 4% of each run, Pallas kernels for 25% -> 28%
where the time goes in v6:
time: 284 us; the launch traced here: 282 us
  Pallas kernels  81.2 us (29%)
  waiting for transfers between devices  62.7 us (22%)
  starting transfers between devices  60.7 us (21%)
  blocking collectives  45.7 us (16%)
  between operations  14.1 us (5%)
  local copies, waits for them, and re-layouts  11.3 us (4%)
  other arithmetic  6.5 us (2%)
    all_to_all x1, blocking collectives, on_device(): lax.all_to_all(send, 'exp', split_axis=0, concat_axis=0, tiled=True)  29.7 us
    ppermute x17, starting transfers between devices, ring(): return lax.ppermute(block, axis, [(i, to(i)) for i in range(size)])  21.2 us
    ppermute x17, waiting for transfers between devices, ring(): return lax.ppermute(block, axis, [(i, to(i)) for i in range(size)])  18.9 us
    all_to_all x1, blocking collectives, on_device(): lax.all_to_all(packed.reshape(n_exp, ROWS // n_exp, width), 'exp', split_...  16 us
    all_to_all x1, waiting for transfers between devices, on_device(): qkv = lax.all_to_all(qkv, 'ctx', split_axis=0, concat_axis=0, tiled=True)  15.1 us
    pallas_call x1, Pallas kernels, on_device(): call(expert_grad_kernel, 60, sds((width, 2 * hidden_units), bf16), grid=(...  13.2 us
    pallas_call x1, Pallas kernels, on_device(): call(attend_back_kernel, 60, (sds((n_ctx, 3 * HEAD_DIM, rows), bf16), sds...  12.7 us
    pallas_call x1, Pallas kernels, on_device(): call(expert_kernel, 60, (sds((slots, 2 * width), bf16), sds((slots, hidde...  12.4 us
  transfers between devices with their start and end apart: 33, of which 20 were waited for; matrix products, arithmetic and copies ran while one was open for 4% of the time, Pallas kernels for 28%

profile of v6, /device:TPU:1, one launch (start us, length us, event | category | flops | bytes accessed | tf_op | source)
XLA Modules:
  0.0 282.1 jit_solution(3289311126913006707)
XLA Ops:
  9.8 3.8 %shard_map.238 = (bf16[16,224,128]{2,1,0:T(8,128)(2,1)}, bf16[128,768]{1,0:T(8,128)(2,1)}) custom-call(bf16[128,768]{1,0:T(8,128)(2,1)} %bitcast.54, f32[1,768]{1,0:T(1,128)} %reshape.85.gain_ref, s32[1,128]{1,0:T(1,128)} %seg_ref.1, bf16[768,768]{1,0:T(8,128)(2,1)} %wq_ref.3, bf16[768,768]{1,0:T(8,128)(2,1)} %wk_ref.3, bf16[768,768]{1,0:T(8,128)(2,1)} %wv_ref.3), custom_call_target="tpu_custom_call" | custom-call | flops 452984832 | bytes 4194304 | tf_op jit(solution)/shard_map/pallas_call | solution.py:571
  13.6 7.6 %all-to-all-start = ((bf16[16,224,128]{2,1,0:T(8,128)(2,1)}), bf16[16,224,128]{2,1,0:T(8,128)(2,1)S(1)}, u32[]{:S(2)}, u32[]{:S(2)}) async-start(bf16[16,224,128]{2,1,0:T(8,128)(2,1)} %get-tuple-element.60), calls=%async_computation | async-start | bytes 1835008 | tf_op jit(solution)/shard_map/all_to_all | solution.py:578
  25.4 15.1 %all-to-all-done.recv_ref = bf16[16,224,128]{2,1,0:T(8,128)(2,1)S(1)} async-done(((bf16[16,224,128]{2,1,0:T(8,128)(2,1)}), bf16[16,224,128]{2,1,0:T(8,128)(2,1)S(1)}, u32[]{:S(2)}, u32[]{:S(2)}) %all-to-all-start) | async-done | bytes 917536 | tf_op jit(solution)/shard_map/all_to_all | solution.py:578
  41.5 10.1 %shard_map.239 = (bf16[16,64,128]{2,1,0:T(8,128)(2,1)}, f32[8,64,256]{2,1,0:T(8,128)}, f32[8,1,256]{2,1,0:T(1,128)}) custom-call(bf16[16,224,128]{2,1,0:T(8,128)(2,1)} %copy-done.6, s32[1,2048]{1,0:T(1,128)} %bitcast.71, f32[32,1]{1,0:T(8,128)} %pad_dynamic-slice_fusion.tab_ref), custom_call_target="tpu_custom_call" | custom-call | flops 8000000000 | bytes 10485760 | tf_op jit(solution)/shard_map/pallas_call | solution.py:591
  57.3 7.9 %all-to-all-done.1.ot_ref = bf16[16,64,128]{2,1,0:T(8,128)(2,1)S(1)} async-done(((bf16[16,64,128]{2,1,0:T(8,128)(2,1)}), bf16[16,64,128]{2,1,0:T(8,128)(2,1)S(1)}, u32[]{:S(2)}, u32[]{:S(2)}) %all-to-all-start.1) | async-done | bytes 262176 | tf_op jit(solution)/shard_map/all_to_all | solution.py:606
  65.9 3.8 %shard_map.240 = (bf16[320,1536]{1,0:T(8,128)(2,1)}, f32[128,768]{1,0:T(8,128)}, f32[128,256]{1,0:T(8,128)}, bf16[128,768]{1,0:T(8,128)(2,1)}) custom-call(bf16[16,64,128]{2,1,0:T(8,128)(2,1)} %copy-done.13, bf16[128,768]{1,0:T(8,128)(2,1)} %bitcast.55, bf16[768,768]{1,0:T(8,128)(2,1)} %wo_ref.3, f32[1,768]{1,0:T(1,128)} %reshape.87.gain_ref, ...), custom_call_target="tpu_custom_call" | custom-call | flops 1000000000 | bytes 4194304 | tf_op jit(solution)/shard_map/pallas_call | solution.py:610
  69.7 29.7 %all_to_all.53 = bf16[8,40,1536]{2,1,0:T(8,128)(2,1)} all-to-all(bf16[8,40,1536]{2,1,0:T(8,128)(2,1)} %bitcast.49), channel_id=1, replica_groups=mesh['ctx'=16,'exp'=8] {'exp'}, dimensions={0} | all-to-all | bytes 1966080 | tf_op jit(solution)/shard_map/all_to_all | solution.py:622
  99.3 12.4 %shard_map.241 = (bf16[320,1536]{1,0:T(8,128)(2,1)}, bf16[320,3072]{1,0:T(8,128)(2,1)}, bf16[320,3072]{1,0:T(8,128)(2,1)}) custom-call(bf16[320,1536]{1,0:T(8,128)(2,1)} %bitcast.44, bf16[768,6144]{1,0:T(8,128)(2,1)} %all-gather.3.cloned.1.call-done.up_ref.down_ref, bf16[768,6144]{1,0:T(8,128)(2,1)} %all-gather.3.cloned.1.call-done.up_ref.down_ref), custom_call_target="tpu_custom_call" | custom-call | flops 6039797760 | bytes 16777216 | tf_op jit(solution)/shard_map/pallas_call | solution.py:627
  111.7 4.6 %all-to-all-start.3 = ((bf16[8,40,1536]{2,1,0:T(8,128)(2,1)}), bf16[8,40,1536]{2,1,0:T(8,128)(2,1)S(1)}, u32[]{:S(2)}, u32[]{:S(2)}) async-start(bf16[8,40,1536]{2,1,0:T(8,128)(2,1)} %bitcast.48), calls=%async_computation.3 | async-start | bytes 1966080 | tf_op jit(solution)/shard_map/all_to_all | solution.py:650
  117.0 13.2 %shard_map.242 = bf16[768,6144]{1,0:T(8,128)(2,1)} custom-call(bf16[320,1536]{1,0:T(8,128)(2,1)} %bitcast.45, bf16[320,3072]{1,0:T(8,128)(2,1)} %get-tuple-element.65.pre_ref, bf16[320,3072]{1,0:T(8,128)(2,1)} %get-tuple-element.66.act_ref), custom_call_target="tpu_custom_call" | custom-call | flops 3019898880 | bytes 16777216 | tf_op jit(solution)/shard_map/pallas_call | solution.py:651
  131.7 4.9 %shard_map.243 = (bf16[128,768]{1,0:T(8,128)(2,1)}, f32[128,768]{1,0:T(8,128)}, bf16[16,64,128]{2,1,0:T(8,128)(2,1)}, bf16[768,768]{1,0:T(8,128)(2,1)}, f32[16,768]{1,0:T(8,128)}) custom-call(bf16[320,1536]{1,0:T(8,128)(2,1)} %bitcast.47, f32[128,768]{1,0:T(8,128)} %get-tuple-element.68.res_ref, bf16[128,768]{1,0:T(8,128)(2,1)} %bitcast.69, ...), custom_call_target="tpu_custom_call" | custom-call | flops 1000000000 | bytes 6291456 | tf_op jit(solution)/shard_map/pallas_call | solution.py:668
  136.6 5.0 %all-to-all-start.4 = ((bf16[16,64,128]{2,1,0:T(8,128)(2,1)}), bf16[16,64,128]{2,1,0:T(8,128)(2,1)S(1)}, u32[]{:S(2)}, u32[]{:S(2)}) async-start(bf16[16,64,128]{2,1,0:T(8,128)(2,1)} %get-tuple-element.74), calls=%async_computation.4 | async-start | bytes 524288 | tf_op jit(solution)/shard_map/all_to_all | solution.py:687
  141.6 9.3 %all-gather.5.cloned.1.call-done.hid_ref = bf16[2048,768]{1,0:T(8,128)(2,1)} async-done(((bf16[128,768]{1,0:T(8,128)(2,1)}), bf16[2048,768]{1,0:T(8,128)(2,1)}) %all-gather.5.cloned.1.call-update) | async-done | bytes 3145744 | tf_op jit(solution)/shard_map/all_gather | solution.py:588
  152.3 3.9 %all-to-all-start.5 = ((bf16[16,48,768]{2,1,0:T(8,128)(2,1)}), bf16[16,48,768]{2,1,0:T(8,128)(2,1)S(1)}, u32[]{:S(2)}, u32[]{:S(2)}) async-start(bf16[16,48,768]{2,1,0:T(8,128)(2,1)} %bitcast.16), calls=%async_computation.6 | async-start | bytes 2359296 | tf_op jit(solution)/shard_map/all_to_all | solution.py:690
  156.2 12.7 %shard_map.244 = (bf16[16,192,128]{2,1,0:T(8,128)(2,1)}, bf16[192,2048]{1,0:T(8,128)(2,1)}, f32[8,128]{1,0:T(8,128)}) custom-call(bf16[16,224,128]{2,1,0:T(8,128)(2,1)} %copy-done.6, bf16[16,64,128]{2,1,0:T(8,128)(2,1)} %copy-done.14, f32[8,64,256]{2,1,0:T(8,128)} %get-tuple-element.77.otf_ref, f32[8,1,256]{2,1,0:T(1,128)} %get-tuple-element.78.lse_ref, ...), custom_call_target="tpu_custom_call" | custom-call | flops 20000000000 | bytes 20971520 | tf_op jit(solution)/shard_map/pallas_call | solution.py:694
  168.9 7.3 %all-to-all-done.5.wo_ref = bf16[16,48,768]{2,1,0:T(8,128)(2,1)S(1)} async-done(((bf16[16,48,768]{2,1,0:T(8,128)(2,1)}), bf16[16,48,768]{2,1,0:T(8,128)(2,1)S(1)}, u32[]{:S(2)}, u32[]{:S(2)}) %all-to-all-start.5) | async-done | bytes 1179680 | tf_op jit(solution)/shard_map/all_to_all | solution.py:690
  177.2 4.3 %shard_map.245 = bf16[256,768]{1,0:T(8,128)(2,1)} custom-call(bf16[192,2048]{1,0:T(8,128)(2,1)} %get-tuple-element.79.flat_ref, bf16[2048,768]{1,0:T(8,128)(2,1)} %all-gather.5.cloned.1.call-done.hid_ref, bf16[192,768]{1,0:T(8,128)(2,1)} %pad_maximum_fusion.1.wt_ref, f32[1,768]{1,0:T(1,128)} %reshape.85.gain_ref, bf16[16,48,768]{2,1,0:T(8,128)(2,1)} %copy-done.3, ...), custom_call_target="tpu_custom_call" | custom-call | flops 603979776 | bytes 6291456 | tf_op jit(solution)/shard_map/pallas_call | solution.py:714
  181.6 16.0 %all_to_all.54 = bf16[8,32,768]{2,1,0:T(8,128)(2,1)S(1)} all-to-all(bf16[8,32,768]{2,1,0:T(8,128)(2,1)} %bitcast.46), channel_id=1, replica_groups=mesh['ctx'=16,'exp'=8] {'exp'}, dimensions={0} | all-to-all | bytes 786432 | tf_op jit(solution)/shard_map/all_to_all | solution.py:721
  223.3 6.1 %collective-permute-done.9 = bf16[256,768]{1,0:T(8,128)(2,1)S(1)} collective-permute-done((bf16[256,768]{1,0:T(8,128)(2,1)S(1)}, bf16[256,768]{1,0:T(8,128)(2,1)S(1)}, u32[]{:S(2)}, u32[]{:S(2)}) %collective-permute-start.9) | collective-permute-done | bytes 393248 | tf_op jit(solution)/shard_map/ppermute | solution.py:493
  235.1 4.0 %collective-permute-start.17 = (bf16[256,768]{1,0:T(8,128)(2,1)S(1)}, bf16[256,768]{1,0:T(8,128)(2,1)}, u32[]{:S(2)}, u32[]{:S(2)}) collective-permute-start(bf16[256,768]{1,0:T(8,128)(2,1)S(1)} %get-tuple-element.91), channel_id=1, source_target_pairs={{0,1},{1,0},{2,3},{3,2},{4,5},{5,4},{6,7},{7,6},{8,9},{9,8},{10,11... | collective-permute-start | bytes 1179656 | tf_op jit(solution)/shard_map/ppermute | solution.py:546
  242.2 4.7 %collective-permute-start.23 = (bf16[512,768]{1,0:T(8,128)(2,1)S(1)}, bf16[512,768]{1,0:T(8,128)(2,1)}, u32[]{:S(2)}, u32[]{:S(2)}) collective-permute-start(bf16[512,768]{1,0:T(8,128)(2,1)S(1)} %shard_map.248), channel_id=1, source_target_pairs={{0,1},{1,0},{2,3},{3,2},{4,5},{5,4},{6,7},{7,6},{8,9},{9,8},{10,11... | collective-permute-start | bytes 2359304 | tf_op jit(solution)/shard_map/ppermute | solution.py:546
  246.9 4.8 %all-to-all-start.7 = ((bf16[16,192,128]{2,1,0:T(8,128)(2,1)}), bf16[16,192,128]{2,1,0:T(8,128)(2,1)S(1)}, u32[]{:S(2)}, u32[]{:S(2)}) async-start(bf16[16,192,128]{2,1,0:T(8,128)(2,1)} %get-tuple-element.90), calls=%async_computation.8 | async-start | bytes 1572864 | tf_op jit(solution)/shard_map/all_to_all | solution.py:727
  256.1 8.5 %shard_map.249 = (f32[768,768]{1,0:T(8,128)}, f32[768,768]{1,0:T(8,128)}, f32[768,768]{1,0:T(8,128)}, f32[768,768]{1,0:T(8,128)}, f32[1,768]{1,0:T(1,128)}, /*in...) custom-call(s32[4]{0:T(128)} %pad_add_fusion.where_ref, bf16[4,4,16,768]{3,2,1,0:T(8,128)(2,1)} %bitcast.42, ...), custom_call_target="tpu_custom_call" | custom-call | bytes 16777216 | tf_op jit(solution)/shard_map/pallas_call | solution.py:735
  268.1 4.5 %shard_map.250 = f32[128,768]{1,0:T(8,128)} custom-call(bf16[16,192,128]{2,1,0:T(8,128)(2,1)} %copy-done.4, bf16[128,768]{1,0:T(8,128)(2,1)} %bitcast.56, f32[1,768]{1,0:T(1,128)} %reshape.85.gain_ref, f32[128,768]{1,0:T(8,128)} %get-tuple-element.95.rgrad_ref, bf16[768,768]{1,0:T(8,128)(2,1)} %wq_ref.3, bf16[768,768]{1,0:T(8,128)(2,1)} %wk_ref.3, ...), custom_call_target="tpu_custom_call" | custom-call | flops 452984832 | bytes 6291456 | tf_op jit(solution)/shard_map/pallas_call | solution.py:770
  (126 shorter events, 63.9 us)
Async XLA Ops:
  7.2 92.2 %all-gather.3.cloned.1.call-start = ((), (), s32[]{:S(2)}) async-start(), calls=%async_computation.9 | async-start | bytes 10027008 | tf_op jit(solution)/shard_map/all_gather | solution.py:568
  9.2 141.7 %all-gather.5.cloned.1.call-start = ((), (), s32[]{:S(2)}) async-start(), calls=%async_computation.10 | async-start | bytes 3342336 | tf_op jit(solution)/shard_map/all_gather | solution.py:588
  13.6 26.9 %all-to-all-start = ((bf16[16,224,128]{2,1,0:T(8,128)(2,1)}), bf16[16,224,128]{2,1,0:T(8,128)(2,1)S(1)}, u32[]{:S(2)}, u32[]{:S(2)}) async-start(bf16[16,224,128]{2,1,0:T(8,128)(2,1)} %get-tuple-element.60), calls=%async_computation | async-start | bytes 1835008 | tf_op jit(solution)/shard_map/all_to_all | solution.py:578
  51.6 13.6 %all-to-all-start.1 = ((bf16[16,64,128]{2,1,0:T(8,128)(2,1)}), bf16[16,64,128]{2,1,0:T(8,128)(2,1)S(1)}, u32[]{:S(2)}, u32[]{:S(2)}) async-start(bf16[16,64,128]{2,1,0:T(8,128)(2,1)} %get-tuple-element.62), calls=%async_computation.1 | async-start | bytes 524288 | tf_op jit(solution)/shard_map/all_to_all | solution.py:606
  111.7 19.0 %all-to-all-start.3 = ((bf16[8,40,1536]{2,1,0:T(8,128)(2,1)}), bf16[8,40,1536]{2,1,0:T(8,128)(2,1)S(1)}, u32[]{:S(2)}, u32[]{:S(2)}) async-start(bf16[8,40,1536]{2,1,0:T(8,128)(2,1)} %bitcast.48), calls=%async_computation.3 | async-start | bytes 1966080 | tf_op jit(solution)/shard_map/all_to_all | solution.py:650
  136.6 15.0 %all-to-all-start.4 = ((bf16[16,64,128]{2,1,0:T(8,128)(2,1)}), bf16[16,64,128]{2,1,0:T(8,128)(2,1)S(1)}, u32[]{:S(2)}, u32[]{:S(2)}) async-start(bf16[16,64,128]{2,1,0:T(8,128)(2,1)} %get-tuple-element.74), calls=%async_computation.4 | async-start | bytes 524288 | tf_op jit(solution)/shard_map/all_to_all | solution.py:687
  141.6 131.0 %reduce-scatter.2.cloned.1.call-start = ((), (), s32[]{:S(2)}) async-start(), calls=%async_computation.11 | async-start | bytes 10027008 | tf_op jit(solution)/shard_map/reduce_scatter | solution.py:689
  152.3 23.9 %all-to-all-start.5 = ((bf16[16,48,768]{2,1,0:T(8,128)(2,1)}), bf16[16,48,768]{2,1,0:T(8,128)(2,1)S(1)}, u32[]{:S(2)}, u32[]{:S(2)}) async-start(bf16[16,48,768]{2,1,0:T(8,128)(2,1)} %bitcast.16), calls=%async_computation.6 | async-start | bytes 2359296 | tf_op jit(solution)/shard_map/all_to_all | solution.py:690
  204.7 8.4 %collective-permute-start.4 = (bf16[64,768]{1,0:T(8,128)(2,1)S(1)}, bf16[64,768]{1,0:T(8,128)(2,1)S(1)}, u32[]{:S(2)}, u32[]{:S(2)}) collective-permute-start(bf16[64,768]{1,0:T(8,128)(2,1)S(1)} %get-tuple-element.85.refs_0_), channel_id=1, source_target_pairs={{0,16},{8,24},{16,0},{24,8},{32,48},{40,56},{48,32},{56,40},{64,80... | collective-permute-start | bytes 294920 | tf_op jit(solution)/shard_map/ppermute | solution.py:493
  204.7 10.7 %collective-permute-start.5 = (bf16[64,768]{1,0:T(8,128)(2,1)S(1)}, bf16[64,768]{1,0:T(8,128)(2,1)S(1)}, u32[]{:S(2)}, u32[]{:S(2)}) collective-permute-start(bf16[64,768]{1,0:T(8,128)(2,1)S(1)} %get-tuple-element.85.refs_0_), channel_id=1, source_target_pairs={{0,24},{8,0},{16,8},{24,16},{32,56},{40,32},{48,40},{56,48},{64,88... | collective-permute-start | bytes 294920 | tf_op jit(solution)/shard_map/ppermute | solution.py:493
  207.2 8.2 %collective-permute-start.6 = (bf16[64,768]{1,0:T(8,128)(2,1)S(1)}, bf16[64,768]{1,0:T(8,128)(2,1)S(1)}, u32[]{:S(2)}, u32[]{:S(2)}) collective-permute-start(bf16[64,768]{1,0:T(8,128)(2,1)S(1)} %get-tuple-element.86.refs_4_), channel_id=1, source_target_pairs={{0,32},{8,40},{16,48},{24,56},{32,64},{40,72},{48,80},{56,88},{64,... | collective-permute-start | bytes 294920 | tf_op jit(solution)/shard_map/ppermute | solution.py:493
  207.2 9.0 %collective-permute-start.7 = (bf16[64,768]{1,0:T(8,128)(2,1)S(1)}, bf16[64,768]{1,0:T(8,128)(2,1)S(1)}, u32[]{:S(2)}, u32[]{:S(2)}) collective-permute-start(bf16[64,768]{1,0:T(8,128)(2,1)S(1)} %get-tuple-element.86.refs_4_), channel_id=1, source_target_pairs={{0,64},{8,72},{16,80},{24,88},{32,96},{40,104},{48,112},{56,120},{... | collective-permute-start | bytes 294920 | tf_op jit(solution)/shard_map/ppermute | solution.py:493
  210.5 7.3 %collective-permute-start.8 = (bf16[64,768]{1,0:T(8,128)(2,1)S(1)}, bf16[64,768]{1,0:T(8,128)(2,1)S(1)}, u32[]{:S(2)}, u32[]{:S(2)}) collective-permute-start(bf16[64,768]{1,0:T(8,128)(2,1)S(1)} %get-tuple-element.86.refs_4_), channel_id=1, source_target_pairs={{0,96},{8,104},{16,112},{24,120},{32,0},{40,8},{48,16},{56,24},{64... | collective-permute-start | bytes 294920 | tf_op jit(solution)/shard_map/ppermute | solution.py:493
  217.9 11.5 %collective-permute-start.9 = (bf16[256,768]{1,0:T(8,128)(2,1)S(1)}, bf16[256,768]{1,0:T(8,128)(2,1)S(1)}, u32[]{:S(2)}, u32[]{:S(2)}) collective-permute-start(bf16[256,768]{1,0:T(8,128)(2,1)S(1)} %get-tuple-element.91), channel_id=1, source_target_pairs={{0,32},{8,40},{16,48},{24,56},{32,64},{40,72},{48,80},{56,88},{64,... | collective-permute-start | bytes 1179656 | tf_op jit(solution)/shard_map/ppermute | solution.py:493
  218.3 11.1 %collective-permute-start.10 = (bf16[256,768]{1,0:T(8,128)(2,1)S(1)}, bf16[256,768]{1,0:T(8,128)(2,1)S(1)}, u32[]{:S(2)}, u32[]{:S(2)}) collective-permute-start(bf16[256,768]{1,0:T(8,128)(2,1)S(1)} %get-tuple-element.91), channel_id=1, source_target_pairs={{0,96},{8,104},{16,112},{24,120},{32,0},{40,8},{48,16},{56,24},{64... | collective-permute-start | bytes 1179656 | tf_op jit(solution)/shard_map/ppermute | solution.py:493
  220.6 11.6 %collective-permute-start.11 = (bf16[256,768]{1,0:T(8,128)(2,1)S(1)}, bf16[256,768]{1,0:T(8,128)(2,1)S(1)}, u32[]{:S(2)}, u32[]{:S(2)}) collective-permute-start(bf16[256,768]{1,0:T(8,128)(2,1)S(1)} %get-tuple-element.92), channel_id=1, source_target_pairs={{0,8},{8,16},{16,24},{24,0},{32,40},{40,48},{48,56},{56,32},{64,72... | collective-permute-start | bytes 1179656 | tf_op jit(solution)/shard_map/ppermute | solution.py:493
  220.6 11.7 %collective-permute-start.12 = (bf16[256,768]{1,0:T(8,128)(2,1)S(1)}, bf16[256,768]{1,0:T(8,128)(2,1)S(1)}, u32[]{:S(2)}, u32[]{:S(2)}) collective-permute-start(bf16[256,768]{1,0:T(8,128)(2,1)S(1)} %get-tuple-element.92), channel_id=1, source_target_pairs={{0,24},{8,0},{16,8},{24,16},{32,56},{40,32},{48,40},{56,48},{64,88... | collective-permute-start | bytes 1179656 | tf_op jit(solution)/shard_map/ppermute | solution.py:493
  229.4 9.7 %collective-permute-start.13 = (bf16[128,768]{1,0:T(8,128)(2,1)S(1)}, bf16[128,768]{1,0:T(8,128)(2,1)S(1)}, u32[]{:S(2)}, u32[]{:S(2)}) collective-permute-start(bf16[128,768]{1,0:T(8,128)(2,1)S(1)} %slice.16), channel_id=1, source_target_pairs={{0,32},{8,40},{16,48},{24,56},{32,64},{40,72},{48,80},{56,88},{64,... | collective-permute-start | bytes 589832 | tf_op jit(solution)/shard_map/ppermute | solution.py:493
  229.5 9.7 %collective-permute-start.14 = (bf16[128,768]{1,0:T(8,128)(2,1)S(1)}, bf16[128,768]{1,0:T(8,128)(2,1)S(1)}, u32[]{:S(2)}, u32[]{:S(2)}) collective-permute-start(bf16[128,768]{1,0:T(8,128)(2,1)S(1)} %slice.17), channel_id=1, source_target_pairs={{0,96},{8,104},{16,112},{24,120},{32,0},{40,8},{48,16},{56,24},{64... | collective-permute-start | bytes 589832 | tf_op jit(solution)/shard_map/ppermute | solution.py:493
  232.4 9.7 %collective-permute-start.16 = (bf16[128,768]{1,0:T(8,128)(2,1)S(1)}, bf16[128,768]{1,0:T(8,128)(2,1)S(1)}, u32[]{:S(2)}, u32[]{:S(2)}) collective-permute-start(bf16[128,768]{1,0:T(8,128)(2,1)S(1)} %slice.19), channel_id=1, source_target_pairs={{0,24},{8,0},{16,8},{24,16},{32,56},{40,32},{48,40},{56,48},{64,88... | collective-permute-start | bytes 589832 | tf_op jit(solution)/shard_map/ppermute | solution.py:493
  235.1 17.2 %collective-permute-start.17 = (bf16[256,768]{1,0:T(8,128)(2,1)S(1)}, bf16[256,768]{1,0:T(8,128)(2,1)}, u32[]{:S(2)}, u32[]{:S(2)}) collective-permute-start(bf16[256,768]{1,0:T(8,128)(2,1)S(1)} %get-tuple-element.91), channel_id=1, source_target_pairs={{0,1},{1,0},{2,3},{3,2},{4,5},{5,4},{6,7},{7,6},{8,9},{9,8},{10,11... | collective-permute-start | bytes 1179656 | tf_op jit(solution)/shard_map/ppermute | solution.py:546
  239.1 13.5 %collective-permute-start.20 = (bf16[256,768]{1,0:T(8,128)(2,1)S(1)}, bf16[256,768]{1,0:T(8,128)(2,1)}, u32[]{:S(2)}, u32[]{:S(2)}) collective-permute-start(bf16[256,768]{1,0:T(8,128)(2,1)S(1)} %get-tuple-element.92), channel_id=1, source_target_pairs={{0,1},{1,0},{2,3},{3,2},{4,5},{5,4},{6,7},{7,6},{8,9},{9,8},{10,11... | collective-permute-start | bytes 1179656 | tf_op jit(solution)/shard_map/ppermute | solution.py:546
  242.2 13.2 %collective-permute-start.23 = (bf16[512,768]{1,0:T(8,128)(2,1)S(1)}, bf16[512,768]{1,0:T(8,128)(2,1)}, u32[]{:S(2)}, u32[]{:S(2)}) collective-permute-start(bf16[512,768]{1,0:T(8,128)(2,1)S(1)} %shard_map.248), channel_id=1, source_target_pairs={{0,1},{1,0},{2,3},{3,2},{4,5},{5,4},{6,7},{7,6},{8,9},{9,8},{10,11... | collective-permute-start | bytes 2359304 | tf_op jit(solution)/shard_map/ppermute | solution.py:546
  246.9 18.7 %all-to-all-start.7 = ((bf16[16,192,128]{2,1,0:T(8,128)(2,1)}), bf16[16,192,128]{2,1,0:T(8,128)(2,1)S(1)}, u32[]{:S(2)}, u32[]{:S(2)}) async-start(bf16[16,192,128]{2,1,0:T(8,128)(2,1)} %get-tuple-element.90), calls=%async_computation.8 | async-start | bytes 1572864 | tf_op jit(solution)/shard_map/all_to_all | solution.py:727
  (30 other events, 235.3 us)
Sparse Core Ops, SparseCore 0:
  10.7 88.0 all-gather.2
  101.0 49.8 all-gather.4
  154.4 97.3 reduce-scatter.1

commit v7 on v6

--- a/solution.py
+++ b/solution.py
@@ -402,7 +402,12 @@
     out_ref[240:256, :] = jnp.concatenate([first, small_ref[8:16, :]], axis=0).astype(bf16)
 
 
-def tokens_kernel(recv_ref, tok_ref, gain_ref, rgrad_ref, wq_ref, wk_ref, wv_ref, out_ref):
+def tokens_kernel(
+    recv_ref, tok_ref, gain_ref, rgrad_ref, wq_ref, wk_ref, wv_ref, sum_ref, out_ref, up_ref, down_ref
+):
+    units = up_ref.shape[2]
+    up_ref[:, 0, :] = sum_ref[:, 0:units].astype(f32)
+    down_ref[:, 0, :] = sum_ref[:, units:].astype(f32)
     tokens, width = tok_ref.shape
     acc = None
     for weight_ref, at in ((wq_ref, 0), (wk_ref, HEAD_DIM), (wv_ref, 2 * HEAD_DIM)):
@@ -424,15 +429,9 @@
     return piece.reshape(shape)
 
 
-def widen_kernel(in_ref, up_ref, down_ref):
-    units = up_ref.shape[2]
-    up_ref[:, 0, :] = in_ref[:, 0:units].astype(f32)
-    down_ref[:, 0, :] = in_ref[:, units:].astype(f32)
-
-
 def unpack_kernel(where_ref, *refs):
-    pieces, (q_ref, k_ref, v_ref, wo_ref, gain_one_ref, gain_two_ref) = refs[:14], refs[14:20]
-    router_ref, table_ref, all_ref, sems = refs[20:]
+    pieces, (q_ref, k_ref, v_ref, wo_ref, gain_ref) = refs[:14], refs[14:19]
+    router_ref, table_ref, all_ref, sems = refs[19:]
     step = pl.program_id(0)
     x, y, z, core = where_ref[0], where_ref[1], where_ref[2], where_ref[3]
     copies = []
@@ -477,8 +476,7 @@
         total = tails[0]
         for part in tails[1:]:
             total = total + part
-        gain_one_ref[...] = total[0:1]
-        gain_two_ref[...] = total[1:2]
+        gain_ref[...] = total[0:8]
         router_ref[...] = total[8:16]
         table_ref[...] = jnp.concatenate(
             [part[2:3, 0 : table_ref.shape[1]] for part in tails[:HEADS]], axis=0
@@ -732,7 +730,7 @@
     exp = lax.axis_index("exp")
     where = jnp.stack([head % 4, head // 4, exp // 2, exp % 2]).astype(jnp.int32)
     once = lambda shape: pl.BlockSpec(shape, lambda i, w: (0, 0))
-    query_grad, key_grad, value_grad, output_grad, gain_a, gain_b, router_grad, table_grad = call(
+    query_grad, key_grad, value_grad, output_grad, gains, router_grad, table_grad = call(
         unpack_kernel,
         60,
         (
@@ -740,8 +738,7 @@
             full,
             full,
             full,
-            sds((1, width), f32),
-            sds((1, width), f32),
+            sds((8, width), f32),
             sds((experts, width), f32),
             sds((HEADS, bias_table.shape[0]), f32),
         ),
@@ -754,8 +751,7 @@
                 column,
                 column,
                 pl.BlockSpec((192, width), lambda i, w: (jnp.minimum(i, 3), 0)),
-                once((1, width)),
-                once((1, width)),
+                once((8, width)),
                 once((experts, width)),
                 once((HEADS, bias_table.shape[0])),
             ],
@@ -767,34 +763,24 @@
         moved=16 * MB,
     )(where, *[ring_rows(piece) for piece in everything])
     back, output_grad = lax.optimization_barrier((back, output_grad))
-    tokens_grad = call(
+    own_rows = sds((summed.shape[0], 1, hidden_units), f32)
+    tokens_grad, ups, downs = call(
         tokens_kernel,
         60,
-        sds((rows, width), f32),
+        (sds((rows, width), f32), own_rows, own_rows),
         flops=6 * rows * width * width,
-        moved=6 * MB,
-    )(back, x, gain_one, residual_grad, query_weight, key_weight, value_weight)
-    summed, tokens_grad = lax.optimization_barrier((summed, tokens_grad))
-    own_rows = sds((summed.shape[0], 1, hidden_units), f32)
-    ups, downs = call(
-        widen_kernel,
-        60,
-        (own_rows, own_rows),
-        grid=(summed.shape[0] // 16,),
-        in_specs=[pl.BlockSpec((16, 2 * hidden_units), lambda i: (i, 0))],
-        out_specs=[pl.BlockSpec((16, 1, hidden_units), lambda i: (i, 0, 0))] * 2,
-        moved=2 * MB,
-    )(summed)
+        moved=8 * MB,
+    )(back, x, gain_one, residual_grad, query_weight, key_weight, value_weight, summed)
     return (
         layer_out[None],
         tokens_grad[None],
-        gain_a[0],
+        gains[0],
         query_grad,
         key_grad,
         value_grad,
         output_grad,
         table_grad.T,
-        gain_b[0],
+        gains[1],
         router_grad.T,
         ups,
         downs,

time: 284 us -> 281 us (0.989)
  waiting for transfers between devices: 62.7 us -> 66.2 us
    ppermute x17, starting transfers between devices: 21.2 us -> 16.4 us  [ring(): return lax.ppermute(block, axis, [(i, to(i)) for i in range(size)])]
    ppermute x7, starting transfers between devices: 9.94 us -> 13 us  [gather_far(): return own + [lax.ppermute(piece, 'exp', pairs) for piece in own]]
    pallas_call x3 -> x2, Pallas kernels: 15.9 us -> 13.5 us  [the longest x1 8.47 us: on_device(): call(unpack_kernel, 60, (full, full, full, full, sds((8, width), f32), sd...]
  transfers between devices with their start and end apart: 33 -> 33, of which waited for: 20 -> 19; matrix products, arithmetic and copies ran while one was open for 4% -> 3% of each run, Pallas kernels for 28% -> 27%
where the time goes in v7:
time: 281 us; the launch traced here: 280 us
  Pallas kernels  79.7 us (28%)
  waiting for transfers between devices  66.2 us (24%)
  starting transfers between devices  59.9 us (21%)
  blocking collectives  43.2 us (15%)
  between operations  14 us (5%)
  local copies, waits for them, and re-layouts  12.7 us (5%)
  other arithmetic  3.91 us (1%)
    all_to_all x1, blocking collectives, on_device(): lax.all_to_all(send, 'exp', split_axis=0, concat_axis=0, tiled=True)  27.1 us
    ppermute x17, waiting for transfers between devices, ring(): return lax.ppermute(block, axis, [(i, to(i)) for i in range(size)])  21.3 us
    ppermute x17, starting transfers between devices, ring(): return lax.ppermute(block, axis, [(i, to(i)) for i in range(size)])  16.4 us
    all_to_all x1, blocking collectives, on_device(): lax.all_to_all(packed.reshape(n_exp, ROWS // n_exp, width), 'exp', split_...  16 us
    all_to_all x1, waiting for transfers between devices, on_device(): qkv = lax.all_to_all(qkv, 'ctx', split_axis=0, concat_axis=0, tiled=True)  15.1 us
    pallas_call x1, Pallas kernels, on_device(): call(attend_back_kernel, 60, (sds((n_ctx, 3 * HEAD_DIM, rows), bf16), sds...  13.3 us
    pallas_call x1, Pallas kernels, on_device(): call(expert_grad_kernel, 60, sds((width, 2 * hidden_units), bf16), grid=(...  13.1 us
    ppermute x7, starting transfers between devices, gather_far(): return own + [lax.ppermute(piece, 'exp', pairs) for piece in own]  13 us
  transfers between devices with their start and end apart: 33, of which 19 were waited for; matrix products, arithmetic and copies ran while one was open for 3% of the time, Pallas kernels for 27%

profile of v7, /device:TPU:1, one launch (start us, length us, event | category | flops | bytes accessed | tf_op | source)
XLA Modules:
  0.0 279.6 jit_solution(7664796386508620723)
XLA Ops:
  9.8 3.8 %shard_map.238 = (bf16[16,224,128]{2,1,0:T(8,128)(2,1)}, bf16[128,768]{1,0:T(8,128)(2,1)}) custom-call(bf16[128,768]{1,0:T(8,128)(2,1)} %bitcast.54, f32[1,768]{1,0:T(1,128)} %reshape.85.gain_ref, s32[1,128]{1,0:T(1,128)} %seg_ref.1, bf16[768,768]{1,0:T(8,128)(2,1)} %wq_ref.3, bf16[768,768]{1,0:T(8,128)(2,1)} %wk_ref.3, bf16[768,768]{1,0:T(8,128)(2,1)} %wv_ref.3), custom_call_target="tpu_custom_call" | custom-call | flops 452984832 | bytes 4194304 | tf_op jit(solution)/shard_map/pallas_call | solution.py:569
  13.6 7.6 %all-to-all-start = ((bf16[16,224,128]{2,1,0:T(8,128)(2,1)}), bf16[16,224,128]{2,1,0:T(8,128)(2,1)S(1)}, u32[]{:S(2)}, u32[]{:S(2)}) async-start(bf16[16,224,128]{2,1,0:T(8,128)(2,1)} %get-tuple-element.58), calls=%async_computation | async-start | bytes 1835008 | tf_op jit(solution)/shard_map/all_to_all | solution.py:576
  25.4 15.1 %all-to-all-done.recv_ref = bf16[16,224,128]{2,1,0:T(8,128)(2,1)S(1)} async-done(((bf16[16,224,128]{2,1,0:T(8,128)(2,1)}), bf16[16,224,128]{2,1,0:T(8,128)(2,1)S(1)}, u32[]{:S(2)}, u32[]{:S(2)}) %all-to-all-start) | async-done | bytes 917536 | tf_op jit(solution)/shard_map/all_to_all | solution.py:576
  41.5 10.6 %shard_map.239 = (bf16[16,64,128]{2,1,0:T(8,128)(2,1)}, f32[8,64,256]{2,1,0:T(8,128)}, f32[8,1,256]{2,1,0:T(1,128)}) custom-call(bf16[16,224,128]{2,1,0:T(8,128)(2,1)} %copy-done.6, s32[1,2048]{1,0:T(1,128)} %bitcast.71, f32[32,1]{1,0:T(8,128)} %pad_dynamic-slice_fusion.tab_ref), custom_call_target="tpu_custom_call" | custom-call | flops 8000000000 | bytes 10485760 | tf_op jit(solution)/shard_map/pallas_call | solution.py:589
  57.8 8.0 %all-to-all-done.1.ot_ref = bf16[16,64,128]{2,1,0:T(8,128)(2,1)S(1)} async-done(((bf16[16,64,128]{2,1,0:T(8,128)(2,1)}), bf16[16,64,128]{2,1,0:T(8,128)(2,1)S(1)}, u32[]{:S(2)}, u32[]{:S(2)}) %all-to-all-start.1) | async-done | bytes 262176 | tf_op jit(solution)/shard_map/all_to_all | solution.py:604
  66.5 3.8 %shard_map.240 = (bf16[320,1536]{1,0:T(8,128)(2,1)}, f32[128,768]{1,0:T(8,128)}, f32[128,256]{1,0:T(8,128)}, bf16[128,768]{1,0:T(8,128)(2,1)}) custom-call(bf16[16,64,128]{2,1,0:T(8,128)(2,1)} %copy-done.13, bf16[128,768]{1,0:T(8,128)(2,1)} %bitcast.55, bf16[768,768]{1,0:T(8,128)(2,1)} %wo_ref.3, f32[1,768]{1,0:T(1,128)} %reshape.87.gain_ref, ...), custom_call_target="tpu_custom_call" | custom-call | flops 1000000000 | bytes 4194304 | tf_op jit(solution)/shard_map/pallas_call | solution.py:608
  70.3 27.1 %all_to_all.53 = bf16[8,40,1536]{2,1,0:T(8,128)(2,1)} all-to-all(bf16[8,40,1536]{2,1,0:T(8,128)(2,1)} %bitcast.49), channel_id=1, replica_groups=mesh['ctx'=16,'exp'=8] {'exp'}, dimensions={0} | all-to-all | bytes 1966080 | tf_op jit(solution)/shard_map/all_to_all | solution.py:620
  98.8 12.3 %shard_map.241 = (bf16[320,1536]{1,0:T(8,128)(2,1)}, bf16[320,3072]{1,0:T(8,128)(2,1)}, bf16[320,3072]{1,0:T(8,128)(2,1)}) custom-call(bf16[320,1536]{1,0:T(8,128)(2,1)} %bitcast.44, bf16[768,6144]{1,0:T(8,128)(2,1)} %all-gather.3.cloned.1.call-done.up_ref.down_ref, bf16[768,6144]{1,0:T(8,128)(2,1)} %all-gather.3.cloned.1.call-done.up_ref.down_ref), custom_call_target="tpu_custom_call" | custom-call | flops 6039797760 | bytes 16777216 | tf_op jit(solution)/shard_map/pallas_call | solution.py:625
  111.2 5.2 %all-to-all-start.3 = ((bf16[8,40,1536]{2,1,0:T(8,128)(2,1)}), bf16[8,40,1536]{2,1,0:T(8,128)(2,1)S(1)}, u32[]{:S(2)}, u32[]{:S(2)}) async-start(bf16[8,40,1536]{2,1,0:T(8,128)(2,1)} %bitcast.48), calls=%async_computation.3 | async-start | bytes 1966080 | tf_op jit(solution)/shard_map/all_to_all | solution.py:648
  117.0 13.1 %shard_map.242 = bf16[768,6144]{1,0:T(8,128)(2,1)} custom-call(bf16[320,1536]{1,0:T(8,128)(2,1)} %bitcast.45, bf16[320,3072]{1,0:T(8,128)(2,1)} %get-tuple-element.63.pre_ref, bf16[320,3072]{1,0:T(8,128)(2,1)} %get-tuple-element.64.act_ref), custom_call_target="tpu_custom_call" | custom-call | flops 3019898880 | bytes 16777216 | tf_op jit(solution)/shard_map/pallas_call | solution.py:649
  131.7 4.9 %shard_map.243 = (bf16[128,768]{1,0:T(8,128)(2,1)}, f32[128,768]{1,0:T(8,128)}, bf16[16,64,128]{2,1,0:T(8,128)(2,1)}, bf16[768,768]{1,0:T(8,128)(2,1)}, f32[16,768]{1,0:T(8,128)}) custom-call(bf16[320,1536]{1,0:T(8,128)(2,1)} %bitcast.47, f32[128,768]{1,0:T(8,128)} %get-tuple-element.66.res_ref, bf16[128,768]{1,0:T(8,128)(2,1)} %bitcast.69, ...), custom_call_target="tpu_custom_call" | custom-call | flops 1000000000 | bytes 6291456 | tf_op jit(solution)/shard_map/pallas_call | solution.py:666
  136.6 5.0 %all-to-all-start.4 = ((bf16[16,64,128]{2,1,0:T(8,128)(2,1)}), bf16[16,64,128]{2,1,0:T(8,128)(2,1)S(1)}, u32[]{:S(2)}, u32[]{:S(2)}) async-start(bf16[16,64,128]{2,1,0:T(8,128)(2,1)} %get-tuple-element.72), calls=%async_computation.4 | async-start | bytes 524288 | tf_op jit(solution)/shard_map/all_to_all | solution.py:685
  141.7 9.3 %all-gather.5.cloned.1.call-done.hid_ref = bf16[2048,768]{1,0:T(8,128)(2,1)} async-done(((bf16[128,768]{1,0:T(8,128)(2,1)}), bf16[2048,768]{1,0:T(8,128)(2,1)}) %all-gather.5.cloned.1.call-update) | async-done | bytes 3145744 | tf_op jit(solution)/shard_map/all_gather | solution.py:586
  152.3 3.9 %all-to-all-start.5 = ((bf16[16,48,768]{2,1,0:T(8,128)(2,1)}), bf16[16,48,768]{2,1,0:T(8,128)(2,1)S(1)}, u32[]{:S(2)}, u32[]{:S(2)}) async-start(bf16[16,48,768]{2,1,0:T(8,128)(2,1)} %bitcast.16), calls=%async_computation.5 | async-start | bytes 2359296 | tf_op jit(solution)/shard_map/all_to_all | solution.py:688
  156.2 13.3 %shard_map.244 = (bf16[16,192,128]{2,1,0:T(8,128)(2,1)}, bf16[192,2048]{1,0:T(8,128)(2,1)}, f32[8,128]{1,0:T(8,128)}) custom-call(bf16[16,224,128]{2,1,0:T(8,128)(2,1)} %copy-done.6, bf16[16,64,128]{2,1,0:T(8,128)(2,1)} %copy-done.14, f32[8,64,256]{2,1,0:T(8,128)} %get-tuple-element.74.otf_ref, f32[8,1,256]{2,1,0:T(1,128)} %get-tuple-element.75.lse_ref, ...), custom_call_target="tpu_custom_call" | custom-call | flops 20000000000 | bytes 20971520 | tf_op jit(solution)/shard_map/pallas_call | solution.py:692
  169.5 6.7 %all-to-all-done.5.wo_ref = bf16[16,48,768]{2,1,0:T(8,128)(2,1)S(1)} async-done(((bf16[16,48,768]{2,1,0:T(8,128)(2,1)}), bf16[16,48,768]{2,1,0:T(8,128)(2,1)S(1)}, u32[]{:S(2)}, u32[]{:S(2)}) %all-to-all-start.5) | async-done | bytes 1179680 | tf_op jit(solution)/shard_map/all_to_all | solution.py:688
  177.3 4.3 %shard_map.245 = bf16[256,768]{1,0:T(8,128)(2,1)} custom-call(bf16[192,2048]{1,0:T(8,128)(2,1)} %get-tuple-element.76.flat_ref, bf16[2048,768]{1,0:T(8,128)(2,1)} %all-gather.5.cloned.1.call-done.hid_ref, bf16[192,768]{1,0:T(8,128)(2,1)} %pad_maximum_fusion.1.wt_ref, f32[1,768]{1,0:T(1,128)} %reshape.85.gain_ref, bf16[16,48,768]{2,1,0:T(8,128)(2,1)} %copy-done.3, ...), custom_call_target="tpu_custom_call" | custom-call | flops 603979776 | bytes 6291456 | tf_op jit(solution)/shard_map/pallas_call | solution.py:712
  181.6 16.0 %all_to_all.54 = bf16[8,32,768]{2,1,0:T(8,128)(2,1)S(1)} all-to-all(bf16[8,32,768]{2,1,0:T(8,128)(2,1)} %bitcast.46), channel_id=1, replica_groups=mesh['ctx'=16,'exp'=8] {'exp'}, dimensions={0} | all-to-all | bytes 786432 | tf_op jit(solution)/shard_map/all_to_all | solution.py:719
  212.0 4.2 %collective-permute-done.3.refs_1_ = bf16[64,768]{1,0:T(8,128)(2,1)S(1)} collective-permute-done((bf16[64,768]{1,0:T(8,128)(2,1)S(1)}, bf16[64,768]{1,0:T(8,128)(2,1)S(1)}, u32[]{:S(2)}, u32[]{:S(2)}) %collective-permute-start.3) | collective-permute-done | bytes 98336 | tf_op jit(solution)/shard_map/ppermute | solution.py:491
  222.7 7.1 %collective-permute-done.10 = bf16[256,768]{1,0:T(8,128)(2,1)S(1)} collective-permute-done((bf16[256,768]{1,0:T(8,128)(2,1)S(1)}, bf16[256,768]{1,0:T(8,128)(2,1)S(1)}, u32[]{:S(2)}, u32[]{:S(2)}) %collective-permute-start.10) | collective-permute-done | bytes 393248 | tf_op jit(solution)/shard_map/ppermute | solution.py:491
  242.6 5.1 %collective-permute-start.23 = (bf16[512,768]{1,0:T(8,128)(2,1)S(1)}, bf16[512,768]{1,0:T(8,128)(2,1)}, u32[]{:S(2)}, u32[]{:S(2)}) collective-permute-start(bf16[512,768]{1,0:T(8,128)(2,1)S(1)} %shard_map.248), channel_id=1, source_target_pairs={{0,1},{1,0},{2,3},{3,2},{4,5},{5,4},{6,7},{7,6},{8,9},{9,8},{10,11... | collective-permute-start | bytes 2359304 | tf_op jit(solution)/shard_map/ppermute | solution.py:544
  247.6 5.2 %all-to-all-start.7 = ((bf16[16,192,128]{2,1,0:T(8,128)(2,1)}), bf16[16,192,128]{2,1,0:T(8,128)(2,1)S(1)}, u32[]{:S(2)}, u32[]{:S(2)}) async-start(bf16[16,192,128]{2,1,0:T(8,128)(2,1)} %get-tuple-element.87), calls=%async_computation.7 | async-start | bytes 1572864 | tf_op jit(solution)/shard_map/all_to_all | solution.py:725
  257.3 8.5 %shard_map.249 = (f32[768,768]{1,0:T(8,128)}, f32[768,768]{1,0:T(8,128)}, f32[768,768]{1,0:T(8,128)}, f32[768,768]{1,0:T(8,128)}, f32[8,768]{1,0:T(8,128)}, /*index=5*/f32[8,768]{1,0:T(8,128)}, f32[12,32]{1,0:T(8,128)}) custom-call(s32[4]{0:T(128)} %pad_add_fusion.where_ref, bf16[4,4,16,768]{3,2,1,0:T(8,128)(2,1)} %bitcast.42, ...), custom_call_target="tpu_custom_call" | custom-call | bytes 16777216 | tf_op jit(solution)/shard_map/pallas_call | solution.py:733
  268.1 5.0 %shard_map.250 = (f32[128,768]{1,0:T(8,128)}, f32[48,1,3072]{2,1,0:T(1,128)}, f32[48,1,3072]{2,1,0:T(1,128)}) custom-call(bf16[16,192,128]{2,1,0:T(8,128)(2,1)} %copy-done.4, bf16[128,768]{1,0:T(8,128)(2,1)} %bitcast.56, f32[1,768]{1,0:T(1,128)} %reshape.85.gain_ref, f32[128,768]{1,0:T(8,128)} %get-tuple-element.92.rgrad_ref, bf16[768,768]{1,0:T(8,128)(2,1)} %wq_ref.3, ...), custom_call_target="tpu_custom_call" | custom-call | flops 452984832 | bytes 8388608 | tf_op jit(solution)/shard_map/pallas_call | solution.py:767
  (124 shorter events, 60.6 us)
Async XLA Ops:
  7.2 91.6 %all-gather.3.cloned.1.call-start = ((), (), s32[]{:S(2)}) async-start(), calls=%async_computation.9 | async-start | bytes 10027008 | tf_op jit(solution)/shard_map/all_gather | solution.py:566
  9.2 141.8 %all-gather.5.cloned.1.call-start = ((), (), s32[]{:S(2)}) async-start(), calls=%async_computation.10 | async-start | bytes 3342336 | tf_op jit(solution)/shard_map/all_gather | solution.py:586
  13.6 26.9 %all-to-all-start = ((bf16[16,224,128]{2,1,0:T(8,128)(2,1)}), bf16[16,224,128]{2,1,0:T(8,128)(2,1)S(1)}, u32[]{:S(2)}, u32[]{:S(2)}) async-start(bf16[16,224,128]{2,1,0:T(8,128)(2,1)} %get-tuple-element.58), calls=%async_computation | async-start | bytes 1835008 | tf_op jit(solution)/shard_map/all_to_all | solution.py:576
  52.0 13.7 %all-to-all-start.1 = ((bf16[16,64,128]{2,1,0:T(8,128)(2,1)}), bf16[16,64,128]{2,1,0:T(8,128)(2,1)S(1)}, u32[]{:S(2)}, u32[]{:S(2)}) async-start(bf16[16,64,128]{2,1,0:T(8,128)(2,1)} %get-tuple-element.60), calls=%async_computation.1 | async-start | bytes 524288 | tf_op jit(solution)/shard_map/all_to_all | solution.py:604
  111.2 19.6 %all-to-all-start.3 = ((bf16[8,40,1536]{2,1,0:T(8,128)(2,1)}), bf16[8,40,1536]{2,1,0:T(8,128)(2,1)S(1)}, u32[]{:S(2)}, u32[]{:S(2)}) async-start(bf16[8,40,1536]{2,1,0:T(8,128)(2,1)} %bitcast.48), calls=%async_computation.3 | async-start | bytes 1966080 | tf_op jit(solution)/shard_map/all_to_all | solution.py:648
  136.6 15.0 %all-to-all-start.4 = ((bf16[16,64,128]{2,1,0:T(8,128)(2,1)}), bf16[16,64,128]{2,1,0:T(8,128)(2,1)S(1)}, u32[]{:S(2)}, u32[]{:S(2)}) async-start(bf16[16,64,128]{2,1,0:T(8,128)(2,1)} %get-tuple-element.72), calls=%async_computation.4 | async-start | bytes 524288 | tf_op jit(solution)/shard_map/all_to_all | solution.py:685
  141.6 126.5 %reduce-scatter.2.cloned.1.call-start = ((), (), s32[]{:S(2)}) async-start(), calls=%async_computation.11 | async-start | bytes 10027008 | tf_op jit(solution)/shard_map/reduce_scatter | solution.py:687
  152.3 23.9 %all-to-all-start.5 = ((bf16[16,48,768]{2,1,0:T(8,128)(2,1)}), bf16[16,48,768]{2,1,0:T(8,128)(2,1)S(1)}, u32[]{:S(2)}, u32[]{:S(2)}) async-start(bf16[16,48,768]{2,1,0:T(8,128)(2,1)} %bitcast.16), calls=%async_computation.5 | async-start | bytes 2359296 | tf_op jit(solution)/shard_map/all_to_all | solution.py:688
  204.9 7.1 %collective-permute-start.4 = (bf16[64,768]{1,0:T(8,128)(2,1)S(1)}, bf16[64,768]{1,0:T(8,128)(2,1)S(1)}, u32[]{:S(2)}, u32[]{:S(2)}) collective-permute-start(bf16[64,768]{1,0:T(8,128)(2,1)S(1)} %get-tuple-element.82.refs_0_), channel_id=1, source_target_pairs={{0,16},{8,24},{16,0},{24,8},{32,48},{40,56},{48,32},{56,40},{64,80... | collective-permute-start | bytes 294920 | tf_op jit(solution)/shard_map/ppermute | solution.py:491
  207.7 8.5 %collective-permute-start.3 = (bf16[64,768]{1,0:T(8,128)(2,1)S(1)}, bf16[64,768]{1,0:T(8,128)(2,1)S(1)}, u32[]{:S(2)}, u32[]{:S(2)}) collective-permute-start(bf16[64,768]{1,0:T(8,128)(2,1)S(1)} %get-tuple-element.82.refs_0_), channel_id=1, source_target_pairs={{0,8},{8,16},{16,24},{24,0},{32,40},{40,48},{48,56},{56,32},{64,72... | collective-permute-start | bytes 294920 | tf_op jit(solution)/shard_map/ppermute | solution.py:491
  207.7 8.5 %collective-permute-start.8 = (bf16[64,768]{1,0:T(8,128)(2,1)S(1)}, bf16[64,768]{1,0:T(8,128)(2,1)S(1)}, u32[]{:S(2)}, u32[]{:S(2)}) collective-permute-start(bf16[64,768]{1,0:T(8,128)(2,1)S(1)} %get-tuple-element.83.refs_4_), channel_id=1, source_target_pairs={{0,96},{8,104},{16,112},{24,120},{32,0},{40,8},{48,16},{56,24},{64... | collective-permute-start | bytes 294920 | tf_op jit(solution)/shard_map/ppermute | solution.py:491
  210.4 8.7 %collective-permute-start.6 = (bf16[64,768]{1,0:T(8,128)(2,1)S(1)}, bf16[64,768]{1,0:T(8,128)(2,1)S(1)}, u32[]{:S(2)}, u32[]{:S(2)}) collective-permute-start(bf16[64,768]{1,0:T(8,128)(2,1)S(1)} %get-tuple-element.83.refs_4_), channel_id=1, source_target_pairs={{0,32},{8,40},{16,48},{24,56},{32,64},{40,72},{48,80},{56,88},{64,... | collective-permute-start | bytes 294920 | tf_op jit(solution)/shard_map/ppermute | solution.py:491
  219.2 10.7 %collective-permute-start.10 = (bf16[256,768]{1,0:T(8,128)(2,1)S(1)}, bf16[256,768]{1,0:T(8,128)(2,1)S(1)}, u32[]{:S(2)}, u32[]{:S(2)}) collective-permute-start(bf16[256,768]{1,0:T(8,128)(2,1)S(1)} %get-tuple-element.88), channel_id=1, source_target_pairs={{0,96},{8,104},{16,112},{24,120},{32,0},{40,8},{48,16},{56,24},{64... | collective-permute-start | bytes 1179656 | tf_op jit(solution)/shard_map/ppermute | solution.py:491
  219.9 12.0 %collective-permute-start.9 = (bf16[256,768]{1,0:T(8,128)(2,1)S(1)}, bf16[256,768]{1,0:T(8,128)(2,1)S(1)}, u32[]{:S(2)}, u32[]{:S(2)}) collective-permute-start(bf16[256,768]{1,0:T(8,128)(2,1)S(1)} %get-tuple-element.88), channel_id=1, source_target_pairs={{0,32},{8,40},{16,48},{24,56},{32,64},{40,72},{48,80},{56,88},{64,... | collective-permute-start | bytes 1179656 | tf_op jit(solution)/shard_map/ppermute | solution.py:491
  220.7 11.2 %collective-permute-start.12 = (bf16[256,768]{1,0:T(8,128)(2,1)S(1)}, bf16[256,768]{1,0:T(8,128)(2,1)S(1)}, u32[]{:S(2)}, u32[]{:S(2)}) collective-permute-start(bf16[256,768]{1,0:T(8,128)(2,1)S(1)} %get-tuple-element.89), channel_id=1, source_target_pairs={{0,24},{8,0},{16,8},{24,16},{32,56},{40,32},{48,40},{56,48},{64,88... | collective-permute-start | bytes 1179656 | tf_op jit(solution)/shard_map/ppermute | solution.py:491
  222.7 10.9 %collective-permute-start.11 = (bf16[256,768]{1,0:T(8,128)(2,1)S(1)}, bf16[256,768]{1,0:T(8,128)(2,1)S(1)}, u32[]{:S(2)}, u32[]{:S(2)}) collective-permute-start(bf16[256,768]{1,0:T(8,128)(2,1)S(1)} %get-tuple-element.89), channel_id=1, source_target_pairs={{0,8},{8,16},{16,24},{24,0},{32,40},{40,48},{48,56},{56,32},{64,72... | collective-permute-start | bytes 1179656 | tf_op jit(solution)/shard_map/ppermute | solution.py:491
  229.9 7.2 %collective-permute-start.14 = (bf16[128,768]{1,0:T(8,128)(2,1)S(1)}, bf16[128,768]{1,0:T(8,128)(2,1)S(1)}, u32[]{:S(2)}, u32[]{:S(2)}) collective-permute-start(bf16[128,768]{1,0:T(8,128)(2,1)S(1)} %slice.25), channel_id=1, source_target_pairs={{0,96},{8,104},{16,112},{24,120},{32,0},{40,8},{48,16},{56,24},{64... | collective-permute-start | bytes 589832 | tf_op jit(solution)/shard_map/ppermute | solution.py:491
  231.9 8.7 %collective-permute-start.13 = (bf16[128,768]{1,0:T(8,128)(2,1)S(1)}, bf16[128,768]{1,0:T(8,128)(2,1)S(1)}, u32[]{:S(2)}, u32[]{:S(2)}) collective-permute-start(bf16[128,768]{1,0:T(8,128)(2,1)S(1)} %slice.24), channel_id=1, source_target_pairs={{0,32},{8,40},{16,48},{24,56},{32,64},{40,72},{48,80},{56,88},{64,... | collective-permute-start | bytes 589832 | tf_op jit(solution)/shard_map/ppermute | solution.py:491
  232.0 8.6 %collective-permute-start.16 = (bf16[128,768]{1,0:T(8,128)(2,1)S(1)}, bf16[128,768]{1,0:T(8,128)(2,1)S(1)}, u32[]{:S(2)}, u32[]{:S(2)}) collective-permute-start(bf16[128,768]{1,0:T(8,128)(2,1)S(1)} %slice.27), channel_id=1, source_target_pairs={{0,24},{8,0},{16,8},{24,16},{32,56},{40,32},{48,40},{56,48},{64,88... | collective-permute-start | bytes 589832 | tf_op jit(solution)/shard_map/ppermute | solution.py:491
  233.7 8.8 %collective-permute-start.15 = (bf16[128,768]{1,0:T(8,128)(2,1)S(1)}, bf16[128,768]{1,0:T(8,128)(2,1)S(1)}, u32[]{:S(2)}, u32[]{:S(2)}) collective-permute-start(bf16[128,768]{1,0:T(8,128)(2,1)S(1)} %slice.26), channel_id=1, source_target_pairs={{0,8},{8,16},{16,24},{24,0},{32,40},{40,48},{48,56},{56,32},{64,72... | collective-permute-start | bytes 589832 | tf_op jit(solution)/shard_map/ppermute | solution.py:491
  233.7 19.7 %collective-permute-start.17 = (bf16[256,768]{1,0:T(8,128)(2,1)S(1)}, bf16[256,768]{1,0:T(8,128)(2,1)}, u32[]{:S(2)}, u32[]{:S(2)}) collective-permute-start(bf16[256,768]{1,0:T(8,128)(2,1)S(1)} %get-tuple-element.88), channel_id=1, source_target_pairs={{0,1},{1,0},{2,3},{3,2},{4,5},{5,4},{6,7},{7,6},{8,9},{9,8},{10,11... | collective-permute-start | bytes 1179656 | tf_op jit(solution)/shard_map/ppermute | solution.py:544
  237.1 16.7 %collective-permute-start.20 = (bf16[256,768]{1,0:T(8,128)(2,1)S(1)}, bf16[256,768]{1,0:T(8,128)(2,1)}, u32[]{:S(2)}, u32[]{:S(2)}) collective-permute-start(bf16[256,768]{1,0:T(8,128)(2,1)S(1)} %get-tuple-element.89), channel_id=1, source_target_pairs={{0,1},{1,0},{2,3},{3,2},{4,5},{5,4},{6,7},{7,6},{8,9},{9,8},{10,11... | collective-permute-start | bytes 1179656 | tf_op jit(solution)/shard_map/ppermute | solution.py:544
  242.6 14.0 %collective-permute-start.23 = (bf16[512,768]{1,0:T(8,128)(2,1)S(1)}, bf16[512,768]{1,0:T(8,128)(2,1)}, u32[]{:S(2)}, u32[]{:S(2)}) collective-permute-start(bf16[512,768]{1,0:T(8,128)(2,1)S(1)} %shard_map.248), channel_id=1, source_target_pairs={{0,1},{1,0},{2,3},{3,2},{4,5},{5,4},{6,7},{7,6},{8,9},{9,8},{10,11... | collective-permute-start | bytes 2359304 | tf_op jit(solution)/shard_map/ppermute | solution.py:544
  247.6 19.1 %all-to-all-start.7 = ((bf16[16,192,128]{2,1,0:T(8,128)(2,1)}), bf16[16,192,128]{2,1,0:T(8,128)(2,1)S(1)}, u32[]{:S(2)}, u32[]{:S(2)}) async-start(bf16[16,192,128]{2,1,0:T(8,128)(2,1)} %get-tuple-element.87), calls=%async_computation.7 | async-start | bytes 1572864 | tf_op jit(solution)/shard_map/all_to_all | solution.py:725
  (30 other events, 238.8 us)
Sparse Core Ops, SparseCore 0:
  10.7 88.0 all-gather.2
  101.0 49.9 all-gather.4
  154.4 99.0 reduce-scatter.1
